TPU v7x, 32 devices: a whole 2x2x4 slice. The times are simulated.
32 devices in a mesh: groups: 2 (over y), row: 16 (over z, x, core).
Axes of the slice: x: 2, y: 2, z: 4, core: 2. Of those that a mesh axis runs over, the one named last changes fastest.
Arguments:
- aligned_activations: bfloat16 [160, 128, 256], P('groups', 'row'), parts along dimension 0, may hold values from -6 to 6
- standardizer_scale: float32 [256], replicated, may hold values from 0.5 to 1.5
- standardizer_shift: float32 [256], replicated, may hold values from -3 to 3
- factor_matrices: bfloat16 [256, 64], replicated, may hold values from -0.375 to 0.375
- factor_shift: float32 [64], replicated, may hold values from -3 to 3
- final_matrix: bfloat16 [1024, 128], replicated, may hold values from -0.1875 to 0.1875
- final_shift: float32 [128], replicated, may hold values from -3 to 3
- interaction_adjoint: bfloat16 [256, 128, 128], P(('groups', 'row')), parts along dimension 0, may hold values from -6 to 6
- polymer_lengths: int32 [24], P('groups'), parts along dimension 0, may hold values from 1 to 32, 128 in all
- lone_homolog_numbers: int32 [24], P('groups'), parts along dimension 0, may hold values from 1 to 8, 48 in all
Outputs:
- pair_delta: bfloat16 [256, 128, 128], P(('groups', 'row')), parts along dimension 0
- alignment_gradient: bfloat16 [160, 128, 256], P('groups', 'row'), parts along dimension 0
- output_weight_gradient: float32 [2048, 128], P('groups'), parts along dimension 0
- factor_matrices_adjoint: float32 [512, 64], P('groups'), parts along dimension 0
There are 2 independent parts, one for each index of `groups`. A program takes and returns all parts, laid end to end along the dimension named above; an argument that names none is the same for every part. Nothing has to cross between parts.
Inputs may be any that keep to these rules, and one draw needn't show every extreme that they name: `polymer_lengths`: each chain has at least one residue; the chains' lengths sum to 128; the longest has exactly 32. `lone_homolog_numbers`: each chain has at least one unpaired row; the counts sum to 48; the largest is exactly 8.
All inputs are finite; a program needn't handle non-finite values.
Results may differ from a plain program's by a relative error of at most 0.0069.
Values may be sent and summed in bfloat16 or wider, within the bound.
No kernel may reach another device: no remote copies, remote signals or barrier semaphores. Data moves between devices by JAX's collectives and lax.ppermute only.
A program may use at most 192 MiB of HBM per device.

v0:
```python
import math

import jax
import jax.numpy as jnp
from jax import lax
from jax.sharding import PartitionSpec as P

P_SIZE = 32
U = 48
CHAINS = 12


def chain_tables(polymer_lengths, lone_homolog_numbers, residue_ids, unpaired_ids):
    bounds = jnp.cumsum(polymer_lengths, dtype=jnp.int32)
    res_chain = jnp.sum(
        (residue_ids[:, None] >= bounds[None, :]).astype(jnp.int32), axis=1, dtype=jnp.int32
    )
    row_bounds = jnp.cumsum(lone_homolog_numbers, dtype=jnp.int32)
    row_chain = jnp.sum(
        (unpaired_ids[:, None] >= row_bounds[None, :]).astype(jnp.int32), axis=1, dtype=jnp.int32
    )
    return (res_chain, row_chain)


def build_mask(res_chain, row_chain):
    paired = jnp.ones((P_SIZE, res_chain.shape[0]), jnp.float32)
    blocked = (row_chain[:, None] == res_chain[None, :]).astype(jnp.float32)
    return jnp.concatenate([paired, blocked], axis=0)


def unpaired_of(res_chain, lone_homolog_numbers):
    chain_ids = jnp.arange(CHAINS, dtype=jnp.int32)
    picked = jnp.where(res_chain[:, None] == chain_ids[None, :], lone_homolog_numbers[None, :], 0)
    return jnp.sum(picked, axis=1).astype(jnp.float32)


def pair_count(chain_rows, unpaired_rows, chain_cols):
    same_chain = chain_rows[:, None] == chain_cols[None, :]
    return (
        jnp.float32(P_SIZE)
        + jnp.where(same_chain, unpaired_rows[:, None], jnp.float32(0.0))
        + jnp.float32(0.001)
    )


def standardize_features(entry_tensor, standardizer_scale, standardizer_shift):
    average = jnp.mean(entry_tensor, axis=-1, keepdims=True)
    centred = entry_tensor - average
    spread = jnp.mean(centred * centred, axis=-1, keepdims=True)
    return centred * lax.rsqrt(spread + 1e-05) * standardizer_scale + standardizer_shift


def on_device(
    aligned_activations,
    standardizer_scale,
    standardizer_shift,
    factor_matrices,
    factor_shift,
    final_matrix,
    final_shift,
    interaction_adjoint,
    polymer_lengths,
    lone_homolog_numbers,
):
    aligned_depth, entries_each_device, feature_width = aligned_activations.shape
    width_rank = factor_matrices.shape[1] // 2
    residues = interaction_adjoint.shape[1]
    pair_width = final_matrix.shape[1]
    own_start = lax.axis_index("row") * entries_each_device
    res_chain, row_chain = chain_tables(
        polymer_lengths,
        lone_homolog_numbers,
        jnp.arange(residues, dtype=jnp.int32),
        jnp.arange(U, dtype=jnp.int32),
    )
    unpaired_res = unpaired_of(res_chain, lone_homolog_numbers)
    own_chain = lax.dynamic_slice_in_dim(res_chain, own_start, entries_each_device, 0)
    own_unpaired = lax.dynamic_slice_in_dim(unpaired_res, own_start, entries_each_device, 0)
    own_mask = build_mask(own_chain, row_chain)
    standardized_entry, standardize_reverse = jax.vjp(
        lambda entry_tensor: standardize_features(
            entry_tensor, standardizer_scale, standardizer_shift
        ),
        aligned_activations.astype(jnp.float32),
    )
    standardized_matrix = standardized_entry.astype(jnp.bfloat16)
    factor_vectors = (
        jnp.einsum(
            "src,ck->srk", standardized_matrix, factor_matrices, preferred_element_type=jnp.float32
        )
        + factor_shift
    )
    factor_vectors = (factor_vectors * own_mask[:, :, None]).astype(jnp.bfloat16)
    left_proj = factor_vectors[:, :, :width_rank]
    right_proj = factor_vectors[:, :, width_rank:]
    right_all = lax.all_gather(right_proj, "row", axis=1, tiled=True)
    block_cols = math.gcd(residues, 128)
    block_count = residues // block_cols

    def column_block(carried, block_index):
        out_acc, left_acc = carried
        block_start = block_index * block_cols
        right_block = lax.dynamic_slice_in_dim(right_all, block_start, block_cols, 1)
        cot_block = lax.dynamic_slice_in_dim(interaction_adjoint, block_start, block_cols, 1)
        chain_cols = lax.dynamic_slice_in_dim(res_chain, block_start, block_cols, 0)
        counts = pair_count(own_chain, own_unpaired, chain_cols)
        outer_block = jnp.einsum(
            "sic,sjd->ijcd", left_proj, right_block, preferred_element_type=jnp.float32
        )
        outer_block = outer_block.astype(jnp.bfloat16).reshape(
            entries_each_device * block_cols, width_rank * width_rank
        )
        pair_block = (
            jnp.dot(outer_block, final_matrix, preferred_element_type=jnp.float32).reshape(
                entries_each_device, block_cols, pair_width
            )
            + final_shift
        )
        pair_block = (pair_block / counts[:, :, None]).astype(jnp.bfloat16)
        scaled = (cot_block.astype(jnp.float32) / counts[:, :, None]).astype(jnp.bfloat16)
        scaled_flat = scaled.reshape(entries_each_device * block_cols, pair_width)
        out_acc = out_acc + jnp.einsum(
            "pk,pz->kz", outer_block, scaled_flat, preferred_element_type=jnp.float32
        )
        outer_grad = jnp.einsum(
            "pz,kz->pk", scaled_flat, final_matrix, preferred_element_type=jnp.float32
        ).astype(jnp.bfloat16)
        outer_grad = outer_grad.reshape(entries_each_device, block_cols, width_rank, width_rank)
        left_acc = left_acc + jnp.einsum(
            "ijcd,sjd->sic", outer_grad, right_block, preferred_element_type=jnp.float32
        )
        right_term = jnp.einsum(
            "ijcd,sic->sjd", outer_grad, left_proj, preferred_element_type=jnp.float32
        )
        return ((out_acc, left_acc), (pair_block, scaled, right_term))

    start_carry = (
        jnp.zeros((width_rank * width_rank, pair_width), jnp.float32),
        jnp.zeros((aligned_depth, entries_each_device, width_rank), jnp.float32),
    )
    (out_partial, left_grad), (pair_blocks, scaled_blocks, right_terms) = lax.scan(
        column_block, start_carry, jnp.arange(block_count, dtype=jnp.int32)
    )
    pair_delta = jnp.transpose(pair_blocks, (1, 0, 2, 3)).reshape(
        entries_each_device, residues, pair_width
    )
    right_full = jnp.transpose(right_terms, (1, 0, 2, 3)).reshape(
        aligned_depth, residues, width_rank
    )
    right_grad = lax.psum_scatter(right_full, "row", scatter_dimension=1, tiled=True)
    factor_sensitivity = (
        jnp.concatenate([left_grad, right_grad], axis=2) * own_mask[:, :, None]
    ).astype(jnp.bfloat16)
    weight_partial = jnp.einsum(
        "src,srk->ck", standardized_matrix, factor_sensitivity, preferred_element_type=jnp.float32
    )
    output_weight_gradient, factor_matrices_adjoint = lax.psum((out_partial, weight_partial), "row")
    standardized_sensitivity = jnp.einsum(
        "srk,ck->src", factor_sensitivity, factor_matrices, preferred_element_type=jnp.float32
    )
    alignment_gradient = standardize_reverse(standardized_sensitivity)[0].astype(jnp.bfloat16)
    return (pair_delta, alignment_gradient, output_weight_gradient, factor_matrices_adjoint)


def solution(mesh):
    return jax.shard_map(
        on_device,
        mesh=mesh,
        in_specs=(
            P("groups", "row", None),
            P(),
            P(),
            P(),
            P(),
            P(),
            P(),
            P(("groups", "row"), None, None),
            P("groups"),
            P("groups"),
        ),
        out_specs=(
            P(("groups", "row"), None, None),
            P("groups", "row", None),
            P("groups", None),
            P("groups", None),
        ),
        check_vma=False,
    )
```

profile of v0, /device:TPU:0, one launch (start us, length us, event | category | flops | bytes accessed | tf_op | source)
XLA Modules:
  0.0 213.3 jit_solution(5471815462682481710)
XLA Ops:
  7.2 0.9 reduce-window.17
  8.3 0.7 select_reduce_fusion
  9.0 0.8 reduce-window.16
  10.1 1.1 convert_reduce_fusion
  11.4 1.2 fusion.12
  12.8 1.4 fusion.6
  14.6 0.2 divide_convert_fusion
  14.8 0.7 convolution_convert_fusion
  15.5 2.6 %copy.72 = bf16[1024,1024]{0,1:T(8,128)(2,1)} copy(bf16[1024,1024]{1,0:T(8,128)(2,1)S(1)} %convolution_convert_fusion) | data formatting | bytes 4194304 | tf_op jit(solution)/shard_map/while/body/eval_jaxpr/convert_element_type | solution.py:127
  18.1 2.2 %copy.91 = bf16[128,8,8,128]{3,2,1,0:T(8,128)(2,1)S(1)} copy(bf16[128,8,8,128]{3,1,2,0:T(8,128)(2,1)} %bitcast.63) | data formatting | bytes 4194304
  20.3 1.4 copy-done.1
  21.7 0.5 convolution_bitcast_fusion
  22.2 3.7 %copy.76 = f32[80,128,32]{2,1,0:T(8,128)} copy(f32[80,128,32]{1,0,2:T(8,128)S(1)} %convolution_bitcast_fusion) | data formatting | bytes 2621440 | tf_op jit(solution)/shard_map/while/body/eval_jaxpr/ijcd,sic->sjd/dot_general | solution.py:132
  26.1 35.7 %all_gather.3 = bf16[80,128,32]{2,1,0:T(8,128)(2,1)S(1)} all-gather(bf16[80,8,32]{2,1,0:T(8,128)(2,1)S(1)} %get-tuple-element.33), channel_id=1, replica_groups=mesh['groups'=2,'row'=16] {'row'}, dimensions={1}, use_global_device_ids=true | all-gather | bytes 696320 | tf_op jit(solution)/shard_map/all_gather | solution.py:96
  61.9 4.2 %copy.73 = bf16[80,128,32]{0,1,2:T(8,128)(2,1)} copy(bf16[80,128,32]{2,1,0:T(8,128)(2,1)S(1)} %all_gather.3) | data formatting | bytes 1310720 | tf_op jit(solution)/shard_map/all_gather | solution.py:96
  66.1 4.2 %copy.83 = bf16[80,128,32,1]{0,1,3,2:T(8,128)(2,1)} copy(bf16[80,128,32,1]{2,1,0,3:T(8,128)(2,1)S(1)} %bitcast.60) | data formatting | bytes 1310720 | tf_op jit(solution)/shard_map/all_gather | solution.py:96
  70.3 1.9 convert_bitcast_fusion
  72.2 0.8 copy.82
  73.1 2.7 %copy.70 = bf16[8,128,32,32]{1,3,2,0:T(8,128)(2,1)} copy(bf16[8,128,32,32]{1,2,0,3:T(8,128)(2,1)S(1)} %convert_bitcast_fusion) | data formatting | bytes 4194304 | tf_op jit(solution)/shard_map/while/body/eval_jaxpr/convert_element_type | solution.py:110
  75.8 0.7 convolution_bitcast_fusion.1
  76.5 0.2 copy.77
  76.7 3.2 %fusion.4 = bf16[8,128,128]{2,1,0:T(8,128)(2,1)} fusion(bf16[8,128,1024]{1,2,0:T(8,128)(2,1)} %bitcast.65, bf16[1024,128]{1,0:T(8,128)(2,1)S(1)} %copy-done, f32[8,128]{1,0:T(8,128)S(1)} %select_add_fusion, f32[128]{0:T(128)S(1)} %copy-done.9), kind=kOutput, calls=%fused_computation.9 | convolution fusion | flops 268828672 | bytes 2626048 | tf_op jit(solution)/shard_map/while/body/eval_jaxpr/dot_general | solution.py:114
  79.9 1.5 fusion
  81.4 27.0 %reduce-scatter.2.cloned.1.call-done = f32[80,8,32]{2,1,0:T(8,128)} async-done(((f32[80,128,32]{2,1,0:T(8,128)}), f32[80,8,32]{2,1,0:T(8,128)}) %reduce-scatter.2.cloned.1.call-update) | async-done | bytes 81936 | tf_op jit(solution)/shard_map/reduce_scatter | solution.py:150
  108.5 1.2 fusion.17
  109.7 1.1 convolution_bitcast_fusion.2
  110.8 0.3 fusion.16
  111.3 0.4 fusion.19
  111.9 1.1 add_convert_fusion
  113.0 90.1 %all-reduce.4.cloned.1.call-done = (f32[1024,128]{1,0:T(8,128)}, f32[256,64]{0,1:T(8,128)}) async-done(((f32[1024,128]{1,0:T(8,128)}, f32[256,64]{0,1:T(8,128)}), (f32[1024,128]{1,0:T(8,128)}, f32[256,64]{0,1:T(8,128)})) %all-reduce.4.cloned.1.call-update) | async-done | bytes 589840 | tf_op jit(solution)/shard_map/psum | solution.py:157
  203.1 1.9 copy.99
  205.0 1.5 copy.100
  (46 shorter events, 1.7 us)
Async XLA Ops:
  7.2 7.7 %copy-start = (bf16[1024,128]{1,0:T(8,128)(2,1)S(1)}, bf16[1024,128]{1,0:T(8,128)(2,1)}, u32[]{:S(2)}) copy-start(bf16[1024,128]{1,0:T(8,128)(2,1)} %param.15) | copy-start | bytes 786436
  7.2 7.4 %copy-start.5 = (bf16[8,128,128]{2,1,0:T(8,128)(2,1)S(1)}, bf16[8,128,128]{2,1,0:T(8,128)(2,1)}, u32[]{:S(2)}) copy-start(bf16[8,128,128]{2,1,0:T(8,128)(2,1)} %param.17) | copy-start | bytes 786436
  7.2 101.3 %reduce-scatter.2.cloned.1.call-start = ((), (), s32[]{:S(2)}) async-start(), calls=%async_computation.1 | async-start | bytes 5570560 | tf_op jit(solution)/shard_map/reduce_scatter | solution.py:150
  20.3 1.4 copy-start.1
  25.9 177.2 %all-reduce.4.cloned.1.call-start = ((), (), s32[]{:S(2)}) async-start(), calls=%async_computation.2 | async-start | bytes 1179648 | tf_op jit(solution)/shard_map/psum | solution.py:157
  73.1 2.8 %copy-start.2 = (bf16[128,8,8,128]{3,2,1,0:T(8,128)(2,1)S(1)}, bf16[128,8,8,128]{3,2,1,0:T(8,128)(2,1)}, u32[]{:S(2)}) copy-start(bf16[128,8,8,128]{3,2,1,0:T(8,128)(2,1)} %copy-done.1) | copy-start | bytes 6291460
  73.1 2.8 %copy-start.4 = (bf16[80,128,32]{0,1,2:T(8,128)(2,1)S(1)}, bf16[80,128,32]{0,1,2:T(8,128)(2,1)}, u32[]{:S(2)}) copy-start(bf16[80,128,32]{0,1,2:T(8,128)(2,1)} %copy.73) | copy-start | bytes 1966084
  75.8 0.9 copy-start.9
  79.9 29.7 %copy-start.3 = (bf16[80,8,256]{2,1,0:T(8,128)(2,1)S(1)}, bf16[80,8,256]{2,1,0:T(8,128)(2,1)}, u32[]{:S(2)}) copy-start(bf16[80,8,256]{2,1,0:T(8,128)(2,1)} %param.10) | copy-start | bytes 983044
  79.9 29.7 %copy-start.7 = (f32[256]{0:T(256)S(1)}, f32[256]{0:T(256)}, u32[]{:S(2)}) copy-start(f32[256]{0:T(256)} %param.11) | copy-start | bytes 3076
  79.9 29.8 %copy-start.8 = (f32[256]{0:T(256)S(1)}, f32[256]{0:T(256)}, u32[]{:S(2)}) copy-start(f32[256]{0:T(256)} %param.12) | copy-start | bytes 3076
  79.9 30.8 %copy-start.6 = (bf16[256,64]{0,1:T(8,128)(2,1)S(1)}, bf16[256,64]{0,1:T(8,128)(2,1)}, u32[]{:S(2)}) copy-start(bf16[256,64]{0,1:T(8,128)(2,1)} %param.13) | copy-start | bytes 98308
Sparse Core Ops, SparseCore 0:
  26.1 82.3 reduce-scatter.1
  112.5 90.6 all-reduce.3
where the time goes:
time: 214 us; the launch traced here: 213 us
  waiting for transfers between devices  117 us (55%)
  blocking collectives  35.7 us (17%)
  local copies, waits for them, and re-layouts  26.6 us (12%)
  between operations  14.3 us (7%)
  matrix products  11.3 us (5%)
  other arithmetic  8.19 us (4%)
    psum x1, waiting for transfers between devices, on_device(): lax.psum((out_partial, weight_partial), 'row')  90.1 us
    all_gather x1, blocking collectives, on_device(): right_all = lax.all_gather(right_proj, 'row', axis=1, tiled=True)  35.7 us
    reduce_scatter x1, waiting for transfers between devices, on_device(): lax.psum_scatter(right_full, 'row', scatter_dimension=1, tiled=True)  27 us
    all_gather x2, local copies, waits for them, and re-layouts, on_device(): right_all = lax.all_gather(right_proj, 'row', axis=1, tiled=True)  8.45 us
    unnamed x23, local copies, waits for them, and re-layouts  6.95 us
  transfers between devices with their start and end apart: 2, of which 2 were waited for; matrix products, arithmetic and copies ran while one was open for 10% of the time, Pallas kernels for 0%

commit v1 on v0

v1 whole, which is shorter than its diff:
```python
import jax
import jax.numpy as jnp
from jax import lax
from jax.experimental import pallas as pl
from jax.experimental.pallas import tpu as pltpu
from jax.sharding import PartitionSpec as P

PAIRED = 32
EXTRA = 8
QUAD = 4
BLOCK = 8
RANK = 32
PACKED = 80
F32 = jnp.float32
BF16 = jnp.bfloat16
SMEM = pl.BlockSpec(memory_space=pltpu.SMEM)


def vmem():
    return pl.BlockSpec(memory_space=pltpu.VMEM)


def params(mib=48):
    return pltpu.CompilerParams(vmem_limit_bytes=mib * 1024 * 1024)


def sds(shape, dtype):
    return jax.ShapeDtypeStruct(shape, dtype)


def place():
    k = lax.axis_index("row")
    return k >> 2, k & 3


def bounds_of(ref):
    ends, total = [], jnp.int32(0)
    for c in range(ref.shape[0]):
        total = total + ref[c]
        ends.append(total)
    return ends


def chain_of(residue, ends):
    chain = jnp.zeros(residue.shape, jnp.int32)
    for end in ends:
        chain = chain + jnp.where(residue >= end, 1, 0)
    return chain


def count_of(chain, hom_ref):
    picked = jnp.zeros(chain.shape, F32)
    for c in range(hom_ref.shape[0]):
        picked = jnp.where(chain == c, hom_ref[c].astype(F32), picked)
    return picked


def swap4(xs, low):
    lane = lax.broadcasted_iota(jnp.int32, xs[0].shape, 1)
    for bit, step in ((2, 2 * low), (1, low)):
        keep = (lane & step) == 0
        ys = list(xs)
        for q in range(4):
            if q & bit == 0:
                lo, hi = xs[q], xs[q | bit]
                ys[q] = jnp.where(keep, lo, pltpu.roll(hi, step, 1))
                ys[q | bit] = jnp.where(keep, pltpu.roll(lo, 128 - step, 1), hi)
        xs = ys
    return xs


def unpack(message):
    m = message.astype(F32)
    return [
        jnp.concatenate([m[0:32], m[64:72]], axis=0),
        jnp.concatenate([m[32:64], m[72:80]], axis=0),
    ]


def pack(lo, hi):
    return jnp.concatenate([lo[0:32], hi[0:32], lo[32:40], hi[32:40]], axis=0).astype(BF16)


def spread_rows(compact, chain, chains):
    rows = [compact[0:PAIRED]]
    extra = compact[PAIRED:]
    for c in range(chains):
        rows.append(jnp.where(chain == c, extra, 0.0))
    return jnp.concatenate(rows, axis=0)


def gather_rows(full, chain, chains):
    extra = jnp.zeros((EXTRA, full.shape[1]), F32)
    for c in range(chains):
        top = PAIRED + EXTRA * c
        extra = jnp.where(chain == c, full[top : top + EXTRA], extra)
    return jnp.concatenate([full[0:PAIRED], extra], axis=0)


def left_chain(a, b, ends):
    lane = lax.broadcasted_iota(jnp.int32, (EXTRA, 128), 1)
    residue = 32 * a + 8 * (b ^ (lane >> 5)) + (lane & 7)
    return jnp.concatenate([chain_of(residue, ends)] * 8, axis=1)


def right_chain(a, b, chunk, ends):
    lane = lax.broadcasted_iota(jnp.int32, (EXTRA, 256), 1)
    parts = []
    for tt in range(4):
        residue = 32 * (a ^ (4 * chunk + tt)) + 8 * b + (lane >> 5)
        parts.append(chain_of(residue, ends))
    return jnp.concatenate(parts, axis=1)


def spread_matrix():
    row = lax.broadcasted_iota(jnp.int32, (512, 512), 0)
    o = lax.broadcasted_iota(jnp.int32, (512, 512), 1)
    r, k = row >> 6, row & 63
    target = jnp.where(k < RANK, k * 8 + r, 256 + r * 32 + (k - RANK))
    return jnp.where(o == target, 1.0, 0.0).astype(BF16)


def cut_kernel(adj_ref, *refs):
    outs, work = refs[:QUAD], refs[QUAD]
    residues = adj_ref.shape[1]
    groups = residues // 32
    a, b = place()
    work[...] = adj_ref[...].astype(F32).reshape(BLOCK * residues, 128)
    for t in range(QUAD):

        def step(u, _, t=t):
            tiles = []
            for jj in range(BLOCK):
                j = 32 * (a ^ u) + 8 * (b ^ t) + jj
                tiles.append(work[pl.ds(j, BLOCK, stride=residues), :])
            rows = pl.ds(pl.multiple_of(u * 64, 64), 64)
            outs[t][rows, :] = jnp.concatenate(tiles, axis=0).astype(BF16)
            return 0

        lax.fori_loop(0, groups, step, 0, unroll=groups <= 4)


def project_kernel(
    x_ref, scale_ref, shift_ref, mat_ref, off_ref, len_ref, hom_ref,
    left_ref, right_ref, norm_ref, hat_ref, rstd_ref, spread_ref, full, comp,
):
    depth = x_ref.shape[0]
    chains = len_ref.shape[0]
    a, b = place()
    x = x_ref[...].astype(F32)
    centred = x - jnp.mean(x, axis=-1, keepdims=True)
    rstd = lax.rsqrt(jnp.mean(centred * centred, axis=-1, keepdims=True) + 1e-05)
    hat = (centred * rstd).reshape(depth * BLOCK, 256)
    normed = (hat * scale_ref[...] + shift_ref[...]).astype(BF16)
    hat_ref[...] = hat
    norm_ref[...] = normed
    rstd_ref[...] = jnp.broadcast_to(rstd, (depth, BLOCK, 128)).reshape(depth * BLOCK, 128)
    proj = jnp.dot(normed, mat_ref[...], preferred_element_type=F32) + off_ref[...]
    full[0 : depth * BLOCK, :] = proj
    full[depth * BLOCK :, :] = jnp.zeros((EXTRA * BLOCK, 64), F32)
    comp[0 : PAIRED * BLOCK, :] = proj[0 : PAIRED * BLOCK]
    residue = lax.broadcasted_iota(jnp.int32, (EXTRA * BLOCK, 64), 0)
    entry = residue >> 3
    chain = chain_of(32 * a + 8 * b + (residue & 7), bounds_of(len_ref))
    extra = jnp.zeros((EXTRA * BLOCK, 64), F32)
    start = jnp.int32(PAIRED)
    for c in range(chains):
        rows = full[pl.ds(pl.multiple_of(start * BLOCK, BLOCK), EXTRA * BLOCK), :]
        extra = jnp.where((chain == c) & (entry < hom_ref[c]), rows, extra)
        start = start + hom_ref[c]
    comp[PAIRED * BLOCK :, :] = extra
    rows = PAIRED + EXTRA
    wide = jnp.concatenate([comp[pl.ds(r, rows, stride=BLOCK), :] for r in range(BLOCK)], axis=1)
    spread = spread_matrix()
    spread_ref[...] = spread
    out = jnp.dot(wide.astype(BF16), spread, preferred_element_type=F32)
    left_ref[...] = pack(out[:, 0:128], out[:, 128:256])
    right_ref[...] = pack(out[:, 256:384], out[:, 384:512])


def adjoint_kernel(len_ref, hom_ref, final_ref, *refs):
    pieces, (s_ref, og_ref, ft_ref) = refs[:QUAD], refs[QUAD:]
    chunk = pl.program_id(0)
    a, b = place()
    ends = bounds_of(len_ref)
    low = lax.broadcasted_iota(jnp.int32, (32, 128), 0)
    chain_i, inv_same = [], []
    for t in range(QUAD):
        chain = chain_of(32 * a + 8 * (b ^ t) + (low & 7), ends)
        chain_i.append(chain)
        inv_same.append(1.0 / (float(PAIRED) + count_of(chain, hom_ref) + 0.001))
    inv_other = 1.0 / jnp.full((32, 128), PAIRED + 0.001, F32)
    blocks = []
    for tt in range(4):
        for half in range(2):
            chain_j = chain_of(32 * (a ^ (4 * chunk + tt)) + 8 * b + 4 * half + (low >> 3), ends)
            top = tt * 64 + half * 32
            for t in range(QUAD):
                inv = jnp.where(chain_i[t] == chain_j, inv_same[t], inv_other)
                blocks.append(pieces[t][top : top + 32, :].astype(F32) * inv)
    s = jnp.concatenate(blocks, axis=0).astype(BF16)
    s_ref[...] = s
    ft_ref[...] = final_ref[...].astype(F32).T.astype(BF16)
    for cb in range(8):
        og = lax.dot_general(
            final_ref[cb * 128 : cb * 128 + 128, :], s, (((1,), (1,)), ((), ())),
            preferred_element_type=F32,
        ).astype(BF16)
        for jg in range(8):
            xs = [og[cl * 32 : cl * 32 + 32, jg * 128 : jg * 128 + 128] for cl in range(4)]
            ys = swap4(xs, 8)
            for jl in range(4):
                top = (jg * 4 + jl) * 32
                og_ref[top : top + 32, cb * 128 : cb * 128 + 128] = ys[jl]


def left_lanes(lefts):
    parts = [unpack(m[...]) for m in lefts]
    lanes = []
    for h in range(2):
        lanes += swap4([parts[t][h] for t in range(QUAD)], 32)
    return jnp.concatenate(lanes, axis=1)


def right_lanes(rights):
    return jnp.concatenate([blk for m in rights for blk in unpack(m[...])], axis=1)


def grad_kernel(len_ref, og_ref, *refs):
    lefts, rights = refs[0:4], refs[4:8]
    lg_refs, rg_refs = refs[8:12], refs[12:16]
    lx_ref, rt_ref, acc = refs[16:19]
    chains = len_ref.shape[0]
    chunk, chunks = pl.program_id(0), pl.num_programs(0)
    a, b = place()
    ends = bounds_of(len_ref)
    chain_l = left_chain(a, b, ends)
    chain_r = right_chain(a, b, chunk, ends)
    lx = spread_rows(left_lanes(lefts), chain_l, chains).astype(BF16)
    rx = spread_rows(right_lanes(rights), chain_r, chains)
    lx_ref[...] = lx
    rt_ref[...] = rx.T.astype(BF16)
    og = og_ref[...]
    lg = jnp.dot(rx.astype(BF16), og, preferred_element_type=F32)
    rg = lax.dot_general(lx, og, (((1,), (1,)), ((), ())), preferred_element_type=F32)
    rg = gather_rows(rg, chain_r, chains)
    for tt in range(4):
        rg_refs[tt][...] = pack(rg[:, tt * 256 : tt * 256 + 128], rg[:, tt * 256 + 128 : tt * 256 + 256])

    @pl.when(chunk == 0)
    def _():
        acc[...] = lg

    @pl.when(chunk > 0)
    def _():
        acc[...] += lg

    @pl.when(chunk == chunks - 1)
    def _():
        lgc = gather_rows(acc[...], chain_l, chains)
        halves = []
        for h in range(2):
            xs = [lgc[:, (4 * h + q) * 128 : (4 * h + q + 1) * 128] for q in range(4)]
            halves.append(swap4(xs, 32))
        for t in range(QUAD):
            lg_refs[t][...] = pack(halves[0][t], halves[1][t])


def outer_kernel(len_ref, hom_ref, lx_ref, rt_ref, s_ref, ft_ref, bias_ref, *refs):
    pair_refs, w_refs = refs[0:4], refs[4:8]
    n_buf, acc = refs[8:10]
    chunk, chunks = pl.program_id(0), pl.num_programs(0)
    a, b = place()
    ends = bounds_of(len_ref)
    lx = lx_ref[...]
    for jg in range(8):
        o = jnp.dot(rt_ref[jg * 128 : jg * 128 + 128, :], lx, preferred_element_type=F32).astype(BF16)
        for cb in range(8):
            xs = [o[jl * 32 : jl * 32 + 32, cb * 128 : cb * 128 + 128] for jl in range(4)]
            ys = swap4(xs, 8)
            for cl in range(4):
                top = (cb * 4 + cl) * 32
                n_buf[top : top + 32, jg * 128 : jg * 128 + 128] = ys[cl]
    n = n_buf[...]
    w = jnp.dot(n, s_ref[...], preferred_element_type=F32)

    @pl.when(chunk == 0)
    def _():
        acc[...] = w

    @pl.when(chunk > 0)
    def _():
        acc[...] += w

    @pl.when(chunk == chunks - 1)
    def _():
        for t in range(QUAD):
            rows = pl.ds(pl.multiple_of((b ^ t) * 256, 256), 256)
            w_refs[t][...] = acc[rows, :].astype(BF16)

    pt = jnp.dot(ft_ref[...], n, preferred_element_type=F32)
    lane = lax.broadcasted_iota(jnp.int32, (8, 128), 1)
    res_i = 32 * a + 8 * (b ^ (lane >> 5)) + (lane & 7)
    chain_i = chain_of(res_i, ends)
    same_inv = 1.0 / (float(PAIRED) + count_of(chain_i, hom_ref) + 0.001)
    other_inv = 1.0 / jnp.full((8, 128), PAIRED + 0.001, F32)
    bias = bias_ref[...]
    tiles = []
    for tt in range(4):
        for half in range(2):
            res_j = 32 * (a ^ (4 * chunk + tt)) + 8 * b + 4 * half + ((lane >> 3) & 3)
            inv = jnp.where(chain_i == chain_of(res_j, ends), same_inv, other_inv)
            inv_col = jnp.broadcast_to(inv[0:1], (128, 128)).T
            blk = tt * 2 + half
            tiles.append((pt[:, blk * 128 : blk * 128 + 128].T + bias) * inv_col)
    for t in range(QUAD):
        pair_refs[t][...] = jnp.concatenate([x[t * 32 : t * 32 + 32] for x in tiles], axis=0).astype(BF16)


def total(refs):
    out = refs[0][...].astype(F32)
    for ref in refs[1:]:
        out = out + ref[...].astype(F32)
    return out


def sum_kernel(*refs):
    refs[-1][...] = total(refs[:-1]).astype(BF16)


def back_kernel(quad, groups, len_ref, hom_ref, spread_ref, norm_ref, *refs):
    lgs, rgs = refs[:quad], refs[quad : quad + groups]
    pg_ref, fm_ref, comp, full = refs[quad + groups :]
    chains = len_ref.shape[0]
    depth8 = pg_ref.shape[0]
    a, b = place()
    lg, rg = total(lgs), total(rgs)
    wide = jnp.concatenate(
        [blk for g in (lg, rg) for blk in unpack(g)], axis=1
    ).astype(BF16)
    rows = PAIRED + EXTRA
    per = lax.dot_general(
        wide, spread_ref[...], (((1,), (1,)), ((), ())), preferred_element_type=F32
    )
    for r in range(BLOCK):
        comp[pl.ds(r, rows, stride=BLOCK), :] = per[:, r * 64 : r * 64 + 64]
    full[0 : PAIRED * BLOCK, :] = comp[0 : PAIRED * BLOCK, :]
    full[PAIRED * BLOCK :, :] = jnp.zeros((full.shape[0] - PAIRED * BLOCK, 64), F32)
    extra = comp[PAIRED * BLOCK :, :]
    residue = lax.broadcasted_iota(jnp.int32, (EXTRA * BLOCK, 64), 0)
    entry = residue >> 3
    chain = chain_of(32 * a + 8 * b + (residue & 7), bounds_of(len_ref))
    start = jnp.int32(PAIRED)
    for c in range(chains):
        at = pl.ds(pl.multiple_of(start * BLOCK, BLOCK), EXTRA * BLOCK)
        full[at, :] += jnp.where((chain == c) & (entry < hom_ref[c]), extra, 0.0)
        start = start + hom_ref[c]
    pg = full[0:depth8, :]
    pg_ref[...] = pg.astype(BF16)
    fm = jnp.dot(pg.T.astype(BF16), norm_ref[...], preferred_element_type=F32)
    fm_ref[...] = jnp.concatenate([fm[:, 0:128], fm[:, 128:256]], axis=0).astype(BF16)


def align_kernel(pg_ref, mat_ref, scale_ref, hat_ref, rstd_ref, out_ref):
    g = lax.dot_general(
        pg_ref[...], mat_ref[...], (((1,), (1,)), ((), ())), preferred_element_type=F32
    )
    g = g * scale_ref[...]
    hat = hat_ref[...]
    m1 = jnp.mean(g, axis=-1, keepdims=True)
    m2 = jnp.mean(g * hat, axis=-1, keepdims=True)
    rstd = rstd_ref[...]
    dx = (g - m1 - hat * m2) * jnp.concatenate([rstd, rstd], axis=1)
    out_ref[...] = dx.reshape(out_ref.shape).astype(BF16)


def pair_kernel(*refs):
    pieces, out_ref, work = refs[:QUAD], refs[QUAD], refs[QUAD + 1]
    residues = out_ref.shape[1]
    groups = residues // 32
    a, b = place()
    for t in range(QUAD):

        def step(u, _, t=t):
            tile = pieces[t][pl.ds(pl.multiple_of(u * 64, 64), 64), :].astype(F32)
            for jj in range(BLOCK):
                j = 32 * (a ^ u) + 8 * (b ^ t) + jj
                work[pl.ds(j, BLOCK, stride=residues), :] = tile[jj * 8 : jj * 8 + 8]
            return 0

        lax.fori_loop(0, groups, step, 0, unroll=groups <= 4)
    out_ref[...] = work[...].reshape(out_ref.shape).astype(BF16)


def merge_kernel(groups, *refs):
    out_ref = refs[-1]
    out_ref[0:256, :] = total(refs[:groups]).astype(BF16)
    out_ref[256:384, :] = total(refs[groups : 2 * groups]).astype(BF16)


def final_kernel(m0, m1, m2, m3, w_ref, fm_ref):
    _, b = place()
    fm = jnp.zeros((128, 128), F32)
    for t, m in enumerate((m0, m1, m2, m3)):
        rows = pl.ds(pl.multiple_of((b ^ t) * 256, 256), 256)
        w_ref[rows, :] = m[0:256, :].astype(F32)
        fm = fm + m[256:384, :].astype(F32)
    fm_ref[0:128, :] = fm[0:64].T
    fm_ref[128:256, :] = fm[64:128].T


def call(kernel, outs, ins, in_specs=None, scratch=(), **kw):
    many = isinstance(outs, (list, tuple))
    return pl.pallas_call(
        kernel,
        out_shape=outs,
        in_specs=in_specs if in_specs is not None else [vmem()] * len(ins),
        out_specs=[vmem()] * len(outs) if many else vmem(),
        scratch_shapes=list(scratch),
        compiler_params=params(),
        **kw,
    )(*ins)


def on_device(
    devices, x, scale, shift, mat, off, final, bias, adjoint, lengths, homologs
):
    groups = devices // QUAD
    chunks = groups // 4
    residues = adjoint.shape[1]
    depth = x.shape[0]
    scale, shift, off, bias = scale[None], shift[None], off[None], bias[None]

    def near(value, t):
        return lax.ppermute(value, "row", [(k, k ^ t) for k in range(devices)])

    def far(value, u):
        return lax.ppermute(value, "row", [(k, k ^ (4 * u)) for k in range(devices)])

    pieces = call(
        cut_kernel,
        [sds((groups * 64, 128), BF16)] * QUAD,
        [adjoint],
        scratch=[pltpu.VMEM((BLOCK * residues, 128), F32)],
    )
    pieces = [pieces[0]] + [near(pieces[t], t) for t in range(1, QUAD)]

    left, right, normed, hat, rstd, spread = call(
        project_kernel,
        [
            sds((PACKED, 128), BF16),
            sds((PACKED, 128), BF16),
            sds((depth * BLOCK, 256), BF16),
            sds((depth * BLOCK, 256), F32),
            sds((depth * BLOCK, 128), F32),
            sds((512, 512), BF16),
        ],
        [x, scale, shift, mat, off, lengths, homologs],
        in_specs=[vmem()] * 5 + [SMEM] * 2,
        scratch=[
            pltpu.VMEM(((depth + EXTRA) * BLOCK, 64), F32),
            pltpu.VMEM(((PAIRED + EXTRA) * BLOCK, 64), F32),
        ],
    )
    lefts = [left] + [near(left, t) for t in range(1, QUAD)]
    rights = [right] + [far(right, u) for u in range(1, groups)]

    def by_slot(parts):
        if chunks == 1:
            return parts
        return [jnp.concatenate(parts[s::4], axis=0) for s in range(4)]

    def from_slot(parts, rows):
        return [parts[u % 4][(u // 4) * rows : (u // 4 + 1) * rows] for u in range(groups)]

    rights = by_slot(rights)

    def rows_of(rows, lanes):
        return pl.BlockSpec((rows, lanes), lambda g: (g, 0))

    def whole(rows, lanes):
        return pl.BlockSpec((rows, lanes), lambda g: (0, 0))

    s, og, final_t = pl.pallas_call(
        adjoint_kernel,
        grid=(chunks,),
        out_shape=[
            sds((chunks * 1024, 128), BF16),
            sds((chunks * 1024, 1024), BF16),
            sds((128, 1024), BF16),
        ],
        in_specs=[SMEM, SMEM, whole(1024, 128)] + [rows_of(256, 128)] * QUAD,
        out_specs=[rows_of(1024, 128), rows_of(1024, 1024), whole(128, 1024)],
        compiler_params=params(),
    )(lengths, homologs, final, *pieces)

    grads = pl.pallas_call(
        grad_kernel,
        grid=(chunks,),
        out_shape=[sds((PACKED, 128), BF16)] * QUAD
        + [sds((chunks * PACKED, 128), BF16)] * 4
        + [sds((128, 1024), BF16), sds((chunks * 1024, 128), BF16)],
        in_specs=[SMEM, rows_of(1024, 1024)]
        + [whole(PACKED, 128)] * QUAD
        + [rows_of(PACKED, 128)] * 4,
        out_specs=[whole(PACKED, 128)] * QUAD
        + [rows_of(PACKED, 128)] * 4
        + [whole(128, 1024), rows_of(1024, 128)],
        scratch_shapes=[pltpu.VMEM((128, 1024), F32)],
        compiler_params=params(),
    )(lengths, og, *lefts, *rights)
    lgs, rgs, (lx, rt) = grads[0:4], grads[4:8], grads[8:10]
    rgs = list(rgs) if chunks == 1 else from_slot(rgs, PACKED)
    lgs = [lgs[0]] + [near(lgs[t], t) for t in range(1, QUAD)]
    rgs = [rgs[0]] + [far(rgs[u], u) for u in range(1, groups)]

    outs = pl.pallas_call(
        outer_kernel,
        grid=(chunks,),
        out_shape=[sds((groups * 64, 128), BF16)] * QUAD + [sds((256, 128), BF16)] * QUAD,
        in_specs=[SMEM, SMEM, whole(128, 1024), rows_of(1024, 128), rows_of(1024, 128)]
        + [whole(128, 1024), whole(1, 128)],
        out_specs=[rows_of(256, 128)] * QUAD + [whole(256, 128)] * QUAD,
        scratch_shapes=[pltpu.VMEM((1024, 1024), BF16), pltpu.VMEM((1024, 128), F32)],
        compiler_params=params(),
    )(lengths, homologs, lx, rt, s, final_t, bias)
    pairs, ws = outs[0:4], outs[4:8]
    ws = [ws[0]] + [near(ws[t], t) for t in range(1, QUAD)]
    pairs = [pairs[0]] + [near(pairs[t], t) for t in range(1, QUAD)]
    w_quad = call(sum_kernel, sds((256, 128), BF16), ws)
    w_quads = [w_quad] + [far(w_quad, u) for u in range(1, groups)]

    pg, fm = call(
        lambda *refs: back_kernel(QUAD, groups, *refs),
        [sds((depth * BLOCK, 64), BF16), sds((128, 128), BF16)],
        [lengths, homologs, spread, normed, *lgs, *rgs],
        in_specs=[SMEM] * 2 + [vmem()] * (2 + QUAD + groups),
        scratch=[
            pltpu.VMEM(((PAIRED + EXTRA) * BLOCK, 64), F32),
            pltpu.VMEM(((depth + EXTRA) * BLOCK, 64), F32),
        ],
    )
    fms = [fm] + [far(fm, u) for u in range(1, groups)]
    alignment_gradient = call(
        align_kernel, sds(x.shape, BF16), [pg, mat, scale, hat, rstd]
    )
    pair_delta = call(
        pair_kernel,
        sds(adjoint.shape, BF16),
        pairs,
        scratch=[pltpu.VMEM((BLOCK * residues, 128), F32)],
    )
    merged = call(
        lambda *refs: merge_kernel(groups, *refs), sds((384, 128), BF16), w_quads + fms
    )
    merged = [merged] + [near(merged, t) for t in range(1, QUAD)]
    w, fma = call(final_kernel, [sds((1024, 128), F32), sds((256, 64), F32)], merged)
    return pair_delta, alignment_gradient, w, fma


def solution(mesh):
    devices = mesh.shape["row"]

    def body(*args):
        return on_device(devices, *args)

    return jax.shard_map(
        body,
        mesh=mesh,
        in_specs=(
            P("groups", "row", None),
            P(),
            P(),
            P(),
            P(),
            P(),
            P(),
            P(("groups", "row"), None, None),
            P("groups"),
            P("groups"),
        ),
        out_specs=(
            P(("groups", "row"), None, None),
            P("groups", "row", None),
            P("groups", None),
            P("groups", None),
        ),
        check_vma=False,
    )
```

time: 214 us -> 74.6 us (0.35)
  waiting for transfers between devices: 117 us -> 14.2 us
  blocking collectives: 35.7 us -> 0 us
  starting transfers between devices: 0.08 us -> 34 us
  local copies, waits for them, and re-layouts: 26.6 us -> 7.78 us
  Pallas kernels: 0 us -> 17.5 us
  between operations: 14.3 us -> 0.82 us
  matrix products: 11.3 us -> 0 us
  other arithmetic: 8.19 us -> 0 us
    psum x1 -> x0, waiting for transfers between devices: 90.1 us -> none  [on_device(): lax.psum((out_partial, weight_partial), 'row')]
    all_gather x1 -> x0, blocking collectives: 35.7 us -> none  [on_device(): right_all = lax.all_gather(right_proj, 'row', axis=1, tiled=True)]
    ppermute x0 -> x30, starting transfers between devices: none -> 34 us  [the longest x12 20.2 us: far(): return lax.ppermute(value, 'row', [(k, k ^ 4 * u) for k in range(devices)])]
    reduce_scatter x1 -> x0, waiting for transfers between devices: 27 us -> none  [on_device(): lax.psum_scatter(right_full, 'row', scatter_dimension=1, tiled=True)]
    pallas_call x0 -> x11, Pallas kernels: none -> 17.5 us  [the longest x8 6.24 us: call(): pl.pallas_call(kernel, out_shape=outs, in_specs=in_specs if in_specs is n...]
    ppermute x0 -> x30, waiting for transfers between devices: none -> 14.2 us  [the longest x18 7.98 us: near(): return lax.ppermute(value, 'row', [(k, k ^ t) for k in range(devices)])]
    dot_general x9 -> x0, matrix products: 11.3 us -> none  [the longest x1 3.18 us: column_block(): jnp.dot(outer_block, final_matrix, preferred_element_type=jnp.float32)]
    all_gather x2 -> x0, local copies, waits for them, and re-layouts: 8.45 us -> none  [on_device(): right_all = lax.all_gather(right_proj, 'row', axis=1, tiled=True)]
  transfers between devices with their start and end apart: 2 -> 30, of which waited for: 2 -> 7; matrix products, arithmetic and copies ran while one was open for 10% -> 1% of each run, Pallas kernels for 0% -> 13%
where the time goes in v1:
time: 74.6 us; the launch traced here: 74.2 us
  starting transfers between devices  34 us (46%)
  Pallas kernels  17.5 us (23%)
  waiting for transfers between devices  14.2 us (19%)
  local copies, waits for them, and re-layouts  7.78 us (10%)
  between operations  0.82 us (1%)
    ppermute x12, starting transfers between devices, far(): return lax.ppermute(value, 'row', [(k, k ^ 4 * u) for k in range(devices)])  20.2 us
    ppermute x18, starting transfers between devices, near(): return lax.ppermute(value, 'row', [(k, k ^ t) for k in range(devices)])  13.8 us
    ppermute x18, waiting for transfers between devices, near(): return lax.ppermute(value, 'row', [(k, k ^ t) for k in range(devices)])  7.98 us
    unnamed x22, local copies, waits for them, and re-layouts  7.78 us
    pallas_call x8, Pallas kernels, call(): pl.pallas_call(kernel, out_shape=outs, in_specs=in_specs if in_specs is n...  6.24 us
    ppermute x12, waiting for transfers between devices, far(): return lax.ppermute(value, 'row', [(k, k ^ 4 * u) for k in range(devices)])  6.17 us
    pallas_call x1, Pallas kernels, on_device(): pl.pallas_call(adjoint_kernel, grid=(chunks,), out_shape=[sds((chunks * 1...  4.94 us
    pallas_call x1, Pallas kernels, on_device(): pl.pallas_call(outer_kernel, grid=(chunks,), out_shape=[sds((groups * 64,...  4.6 us
  transfers between devices with their start and end apart: 30, of which 7 were waited for; matrix products, arithmetic and copies ran while one was open for 1% of the time, Pallas kernels for 13%

profile of v1, /device:TPU:0, one launch (start us, length us, event | category | flops | bytes accessed | tf_op | source)
XLA Modules:
  0.0 74.2 jit_solution(63217804544482215)
XLA Ops:
  0.6 0.9 %copy-done.1 = bf16[8,128,128]{2,1,0:T(8,128)(2,1)S(1)} copy-done((bf16[8,128,128]{2,1,0:T(8,128)(2,1)S(1)}, bf16[8,128,128]{2,1,0:T(8,128)(2,1)}, u32[]{:S(2)}) %copy-start.1) | copy-done | bytes 262168
  2.4 2.6 %collective-permute-start.1 = (bf16[256,128]{1,0:T(8,128)(2,1)S(1)}, bf16[256,128]{1,0:T(8,128)(2,1)S(1)}, u32[]{:S(2)}, u32[]{:S(2)}) collective-permute-start(bf16[256,128]{1,0:T(8,128)(2,1)S(1)} %get-tuple-element.41), channel_id=1, source_target_pairs={{0,2},{1,3},{2,0},{3,1},{4,6},{5,7},{6,4},{7,5},{8,10},{9,11},{10,... | collective-permute-start | bytes 196616 | tf_op jit(solution)/shard_map/ppermute | solution.py:435
  5.1 0.9 %copy.14.mat_ref = bf16[256,64]{1,0:T(8,128)(2,1)S(1)} copy(bf16[256,64]{0,1:T(8,128)(2,1)} %param.13) | data formatting | bytes 65536 | tf_op args[3]
  6.0 1.0 %copy-done = bf16[80,8,256]{2,1,0:T(8,128)(2,1)S(1)} copy-done((bf16[80,8,256]{2,1,0:T(8,128)(2,1)S(1)}, bf16[80,8,256]{2,1,0:T(8,128)(2,1)}, u32[]{:S(2)}) %copy-start) | copy-done | bytes 327704
  10.2 1.5 %shard_map.131 = (bf16[80,128]{1,0:T(8,128)(2,1)S(1)}, bf16[80,128]{1,0:T(8,128)(2,1)S(1)}, bf16[640,256]{1,0:T(8,128)(2,1)S(1)}, f32[640,256]{1,0:T(8,128)S(1)}...) custom-call(bf16[80,8,256]{2,1,0:T(8,128)(2,1)S(1)} %copy-done, f32[1,256]{1,0:T(1,128)S(1)} %bitcast.4, ...), custom_call_target="tpu_custom_call" | custom-call | tf_op jit(solution)/shard_map/pallas_call | solution.py:414
  11.8 1.7 %collective-permute-start.5 = (bf16[80,128]{1,0:T(8,128)(2,1)S(1)}, bf16[80,128]{1,0:T(8,128)(2,1)S(1)}, u32[]{:S(2)}, u32[]{:S(2)}) collective-permute-start(bf16[80,128]{1,0:T(8,128)(2,1)S(1)} %get-tuple-element.44.refs_0_), channel_id=1, source_target_pairs={{0,3},{1,2},{2,1},{3,0},{4,7},{5,6},{6,5},{7,4},{8,11},{9,10},{10,... | collective-permute-start | bytes 61448 | tf_op jit(solution)/shard_map/ppermute | solution.py:435
  13.6 1.4 %collective-permute-done.5.refs_3_ = bf16[80,128]{1,0:T(8,128)(2,1)S(1)} collective-permute-done((bf16[80,128]{1,0:T(8,128)(2,1)S(1)}, bf16[80,128]{1,0:T(8,128)(2,1)S(1)}, u32[]{:S(2)}, u32[]{:S(2)}) %collective-permute-start.5) | collective-permute-done | bytes 20512 | tf_op jit(solution)/shard_map/ppermute | solution.py:435
  15.2 4.0 %collective-permute-start.8 = (bf16[80,128]{1,0:T(8,128)(2,1)S(1)}, bf16[80,128]{1,0:T(8,128)(2,1)S(1)}, u32[]{:S(2)}, u32[]{:S(2)}) collective-permute-start(bf16[80,128]{1,0:T(8,128)(2,1)S(1)} %get-tuple-element.45.refs_4_), channel_id=1, source_target_pairs={{0,12},{1,13},{2,14},{3,15},{4,8},{5,9},{6,10},{7,11},{8,4},{9,5},... | collective-permute-start | bytes 61448 | tf_op jit(solution)/shard_map/ppermute | solution.py:438
  19.9 0.9 %copy-done.2 = bf16[1024,128]{1,0:T(8,128)(2,1)S(1)} copy-done((bf16[1024,128]{1,0:T(8,128)(2,1)S(1)}, bf16[1024,128]{1,0:T(8,128)(2,1)}, u32[]{:S(2)}) %copy-start.2) | copy-done | bytes 262168
  20.8 4.9 %shard_map.130 = (bf16[1024,128]{1,0:T(8,128)(2,1)S(1)}, bf16[1024,1024]{1,0:T(8,128)(2,1)S(1)}, bf16[128,1024]{1,0:T(8,128)(2,1)S(1)}) custom-call(s32[12]{0:T(128)S(1)} %copy-done.3, s32[12]{0:T(128)S(1)} %copy-done.4, bf16[1024,128]{1,0:T(8,128)(2,1)S(1)} %copy-done.2, bf16[256,128]{1,0:T(8,128)(2,1)S(1)} %get-tuple-element.39.refs_0_, ...), custom_call_target="tpu_custom_call" | custom-call | tf_op jit(solution)/shard_map/pallas_call | solution.py:484
  25.8 1.7 %shard_map.132 = (bf16[80,128]{1,0:T(8,128)(2,1)S(1)}, bf16[80,128]{1,0:T(8,128)(2,1)S(1)}, bf16[80,128]{1,0:T(8,128)(2,1)S(1)}, bf16[80,128]{1,0:T(8,128)(2,1)S...) custom-call(s32[12]{0:T(128)S(1)} %copy-done.3, ...), custom_call_target="tpu_custom_call" | custom-call | tf_op jit(solution)/shard_map/pallas_call | solution.py:497
  27.6 4.6 %shard_map.133 = (bf16[256,128]{1,0:T(8,128)(2,1)S(1)}, bf16[256,128]{1,0:T(8,128)(2,1)S(1)}, bf16[256,128]{1,0:T(8,128)(2,1)S(1)}, bf16[256,128]{1,0:T(8,128)(2...) custom-call(s32[12]{0:T(128)S(1)} %copy-done.3, ...), custom_call_target="tpu_custom_call" | custom-call | tf_op jit(solution)/shard_map/pallas_call | solution.py:517
  32.2 1.7 %collective-permute-start.19 = (bf16[256,128]{1,0:T(8,128)(2,1)S(1)}, bf16[256,128]{1,0:T(8,128)(2,1)S(1)}, u32[]{:S(2)}, u32[]{:S(2)}) collective-permute-start(bf16[256,128]{1,0:T(8,128)(2,1)S(1)} %get-tuple-element.69), channel_id=1, source_target_pairs={{0,2},{1,3},{2,0},{3,1},{4,6},{5,7},{6,4},{7,5},{8,10},{9,11},{10,... | collective-permute-start | bytes 196616 | tf_op jit(solution)/shard_map/ppermute | solution.py:435
  34.4 1.6 %collective-permute-start.13 = (bf16[80,128]{1,0:T(8,128)(2,1)S(1)}, bf16[80,128]{1,0:T(8,128)(2,1)S(1)}, u32[]{:S(2)}, u32[]{:S(2)}) collective-permute-start(bf16[80,128]{1,0:T(8,128)(2,1)S(1)} %get-tuple-element.58), channel_id=1, source_target_pairs={{0,2},{1,3},{2,0},{3,1},{4,6},{5,7},{6,4},{7,5},{8,10},{9,11},{10,... | collective-permute-start | bytes 61448 | tf_op jit(solution)/shard_map/ppermute | solution.py:435
  36.1 0.8 %collective-permute-start.14 = (bf16[80,128]{1,0:T(8,128)(2,1)S(1)}, bf16[80,128]{1,0:T(8,128)(2,1)S(1)}, u32[]{:S(2)}, u32[]{:S(2)}) collective-permute-start(bf16[80,128]{1,0:T(8,128)(2,1)S(1)} %get-tuple-element.59), channel_id=1, source_target_pairs={{0,3},{1,2},{2,1},{3,0},{4,7},{5,6},{6,5},{7,4},{8,11},{9,10},{10,... | collective-permute-start | bytes 61448 | tf_op jit(solution)/shard_map/ppermute | solution.py:435
  36.9 1.9 %collective-permute-done.13.refs_6_ = bf16[80,128]{1,0:T(8,128)(2,1)S(1)} collective-permute-done((bf16[80,128]{1,0:T(8,128)(2,1)S(1)}, bf16[80,128]{1,0:T(8,128)(2,1)S(1)}, u32[]{:S(2)}, u32[]{:S(2)}) %collective-permute-start.13) | collective-permute-done | bytes 20512 | tf_op jit(solution)/shard_map/ppermute | solution.py:435
  38.8 1.3 %collective-permute-start.15 = (bf16[80,128]{1,0:T(8,128)(2,1)S(1)}, bf16[80,128]{1,0:T(8,128)(2,1)S(1)}, u32[]{:S(2)}, u32[]{:S(2)}) collective-permute-start(bf16[80,128]{1,0:T(8,128)(2,1)S(1)} %get-tuple-element.61), channel_id=1, source_target_pairs={{0,4},{1,5},{2,6},{3,7},{4,0},{5,1},{6,2},{7,3},{8,12},{9,13},{10,... | collective-permute-start | bytes 61448 | tf_op jit(solution)/shard_map/ppermute | solution.py:438
  40.1 2.9 %collective-permute-start.16 = (bf16[80,128]{1,0:T(8,128)(2,1)S(1)}, bf16[80,128]{1,0:T(8,128)(2,1)S(1)}, u32[]{:S(2)}, u32[]{:S(2)}) collective-permute-start(bf16[80,128]{1,0:T(8,128)(2,1)S(1)} %get-tuple-element.62), channel_id=1, source_target_pairs={{0,8},{1,9},{2,10},{3,11},{4,12},{5,13},{6,14},{7,15},{8,0},{9,1},... | collective-permute-start | bytes 61448 | tf_op jit(solution)/shard_map/ppermute | solution.py:438
  43.0 3.2 %collective-permute-start.17 = (bf16[80,128]{1,0:T(8,128)(2,1)S(1)}, bf16[80,128]{1,0:T(8,128)(2,1)S(1)}, u32[]{:S(2)}, u32[]{:S(2)}) collective-permute-start(bf16[80,128]{1,0:T(8,128)(2,1)S(1)} %get-tuple-element.63), channel_id=1, source_target_pairs={{0,12},{1,13},{2,14},{3,15},{4,8},{5,9},{6,10},{7,11},{8,4},{9,5},... | collective-permute-start | bytes 61448 | tf_op jit(solution)/shard_map/ppermute | solution.py:438
  46.2 2.4 %collective-permute-done.17.refs_11_ = bf16[80,128]{1,0:T(8,128)(2,1)S(1)} collective-permute-done((bf16[80,128]{1,0:T(8,128)(2,1)S(1)}, bf16[80,128]{1,0:T(8,128)(2,1)S(1)}, u32[]{:S(2)}, u32[]{:S(2)}) %collective-permute-start.17) | collective-permute-done | bytes 20512 | tf_op jit(solution)/shard_map/ppermute | solution.py:438
  48.5 1.3 %shard_map.135 = (bf16[640,64]{1,0:T(8,128)(2,1)S(1)}, bf16[128,128]{1,0:T(8,128)(2,1)S(1)}) custom-call(s32[12]{0:T(128)S(1)} %copy-done.3, s32[12]{0:T(128)S(1)} %copy-done.4, bf16[512,512]{1,0:T(8,128)(2,1)S(1)} %get-tuple-element.54.refs_2_, bf16[640,256]{1,0:T(8,128)(2,1)S(1)} %get-tuple-element.55.refs_3_, ...), custom_call_target="tpu_custom_call" | custom-call | tf_op jit(solution)/shard_map/pallas_call | solution.py:414
  49.8 3.3 %collective-permute-start.26 = (bf16[128,128]{1,0:T(8,128)(2,1)S(1)}, bf16[128,128]{1,0:T(8,128)(2,1)S(1)}, u32[]{:S(2)}, u32[]{:S(2)}) collective-permute-start(bf16[128,128]{1,0:T(8,128)(2,1)S(1)} %get-tuple-element.71.refs_4_), channel_id=1, source_target_pairs={{0,12},{1,13},{2,14},{3,15},{4,8},{5,9},{6,10},{7,11},{8,4},{9,5},... | collective-permute-start | bytes 98312 | tf_op jit(solution)/shard_map/ppermute | solution.py:438
  53.9 2.4 %collective-permute-start.22 = (bf16[256,128]{1,0:T(8,128)(2,1)S(1)}, bf16[256,128]{1,0:T(8,128)(2,1)S(1)}, u32[]{:S(2)}, u32[]{:S(2)}) collective-permute-start(bf16[256,128]{1,0:T(8,128)(2,1)S(1)} %shard_map.137.refs_0_), channel_id=1, source_target_pairs={{0,8},{1,9},{2,10},{3,11},{4,12},{5,13},{6,14},{7,15},{8,0},{9,1},... | collective-permute-start | bytes 196616 | tf_op jit(solution)/shard_map/ppermute | solution.py:438
  56.2 1.4 %collective-permute-start.21 = (bf16[256,128]{1,0:T(8,128)(2,1)S(1)}, bf16[256,128]{1,0:T(8,128)(2,1)S(1)}, u32[]{:S(2)}, u32[]{:S(2)}) collective-permute-start(bf16[256,128]{1,0:T(8,128)(2,1)S(1)} %shard_map.137.refs_0_), channel_id=1, source_target_pairs={{0,4},{1,5},{2,6},{3,7},{4,0},{5,1},{6,2},{7,3},{8,12},{9,13},{10,... | collective-permute-start | bytes 196616 | tf_op jit(solution)/shard_map/ppermute | solution.py:438
  58.3 3.5 %collective-permute-done.24.refs_5_ = bf16[128,128]{1,0:T(8,128)(2,1)S(1)} collective-permute-done((bf16[128,128]{1,0:T(8,128)(2,1)S(1)}, bf16[128,128]{1,0:T(8,128)(2,1)S(1)}, u32[]{:S(2)}, u32[]{:S(2)}) %collective-permute-start.24) | collective-permute-done | bytes 32800 | tf_op jit(solution)/shard_map/ppermute | solution.py:438
  62.6 1.4 %collective-permute-start.28 = (bf16[384,128]{1,0:T(8,128)(2,1)S(1)}, bf16[384,128]{1,0:T(8,128)(2,1)S(1)}, u32[]{:S(2)}, u32[]{:S(2)}) collective-permute-start(bf16[384,128]{1,0:T(8,128)(2,1)S(1)} %shard_map.138.m0), channel_id=1, source_target_pairs={{0,2},{1,3},{2,0},{3,1},{4,6},{5,7},{6,4},{7,5},{8,10},{9,11},{10,... | collective-permute-start | bytes 294920 | tf_op jit(solution)/shard_map/ppermute | solution.py:435
  64.0 1.7 %collective-permute-start.10 = (bf16[256,128]{1,0:T(8,128)(2,1)S(1)}, bf16[256,128]{1,0:T(8,128)(2,1)S(1)}, u32[]{:S(2)}, u32[]{:S(2)}) collective-permute-start(bf16[256,128]{1,0:T(8,128)(2,1)S(1)} %get-tuple-element.52), channel_id=1, source_target_pairs={{0,2},{1,3},{2,0},{3,1},{4,6},{5,7},{6,4},{7,5},{8,10},{9,11},{10,... | collective-permute-start | bytes 196616 | tf_op jit(solution)/shard_map/ppermute | solution.py:435
  65.8 1.2 %shard_map.136 = bf16[80,8,256]{2,1,0:T(8,128)(2,1)} custom-call(bf16[640,64]{1,0:T(8,128)(2,1)S(1)} %get-tuple-element.64.pg_ref, bf16[256,64]{1,0:T(8,128)(2,1)S(1)} %copy.14.mat_ref, f32[1,256]{1,0:T(1,128)S(1)} %bitcast.5, f32[640,256]{1,0:T(8,128)S(1)} %get-tuple-element.65.hat_ref, f32[640,128]{1,0:T(8,128)S(1)} %get-tuple-element.66.rstd_ref), custom_call_target="tpu_custom_call" | custom-call | tf_op jit(solution)/shard_map/pallas_call | solution.py:414
  67.0 4.0 %collective-permute-done.10.refs_2_ = bf16[256,128]{1,0:T(8,128)(2,1)S(1)} collective-permute-done((bf16[256,128]{1,0:T(8,128)(2,1)S(1)}, bf16[256,128]{1,0:T(8,128)(2,1)S(1)}, u32[]{:S(2)}, u32[]{:S(2)}) %collective-permute-start.10) | collective-permute-done | bytes 65568 | tf_op jit(solution)/shard_map/ppermute | solution.py:435
  71.6 1.0 %shard_map.134 = bf16[8,128,128]{2,1,0:T(8,128)(2,1)} custom-call(bf16[256,128]{1,0:T(8,128)(2,1)S(1)} %get-tuple-element.50.refs_0_, bf16[256,128]{1,0:T(8,128)(2,1)S(1)} %collective-permute-done.9.refs_1_, bf16[256,128]{1,0:T(8,128)(2,1)S(1)} %collective-permute-done.10.refs_2_, bf16[256,128]{1,0:T(8,128)(2,1)S(1)} %collective-permute-done.11.refs_3_), custom_call_target="tpu_custom_call" | custom-call | tf_op jit(solution)/shard_map/pallas_call | solution.py:414
  72.7 0.8 %shard_map.139 = (f32[1024,128]{1,0:T(8,128)}, f32[256,64]{1,0:T(8,128)S(1)}) custom-call(bf16[384,128]{1,0:T(8,128)(2,1)S(1)} %shard_map.138.m0, bf16[384,128]{1,0:T(8,128)(2,1)S(1)} %collective-permute-done.27.m1, bf16[384,128]{1,0:T(8,128)(2,1)S(1)} %collective-permute-done.28.m2, bf16[384,128]{1,0:T(8,128)(2,1)S(1)} %collective-permute-done.29.m3), custom_call_target="tpu_custom_call" | custom-call | tf_op jit(solution)/shard_map/pallas_call | solution.py:414
  73.5 0.7 copy.16
  (61 shorter events, 8.7 us)
Async XLA Ops:
  1.6 26.0 %copy-start.9 = (f32[128]{0:T(128)S(1)}, f32[128]{0:T(128)}, u32[]{:S(2)}) copy-start(f32[128]{0:T(128)} %param.16) | copy-start | bytes 1540
  1.9 13.3 %collective-permute-start = (bf16[256,128]{1,0:T(8,128)(2,1)S(1)}, bf16[256,128]{1,0:T(8,128)(2,1)S(1)}, u32[]{:S(2)}, u32[]{:S(2)}) collective-permute-start(bf16[256,128]{1,0:T(8,128)(2,1)S(1)} %get-tuple-element.40), channel_id=1, source_target_pairs={{0,1},{1,0},{2,3},{3,2},{4,5},{5,4},{6,7},{7,6},{8,9},{9,8},{10,11... | collective-permute-start | bytes 196616 | tf_op jit(solution)/shard_map/ppermute | solution.py:435
  2.4 16.8 %collective-permute-start.1 = (bf16[256,128]{1,0:T(8,128)(2,1)S(1)}, bf16[256,128]{1,0:T(8,128)(2,1)S(1)}, u32[]{:S(2)}, u32[]{:S(2)}) collective-permute-start(bf16[256,128]{1,0:T(8,128)(2,1)S(1)} %get-tuple-element.41), channel_id=1, source_target_pairs={{0,2},{1,3},{2,0},{3,1},{4,6},{5,7},{6,4},{7,5},{8,10},{9,11},{10,... | collective-permute-start | bytes 196616 | tf_op jit(solution)/shard_map/ppermute | solution.py:435
  5.0 14.2 %collective-permute-start.2 = (bf16[256,128]{1,0:T(8,128)(2,1)S(1)}, bf16[256,128]{1,0:T(8,128)(2,1)S(1)}, u32[]{:S(2)}, u32[]{:S(2)}) collective-permute-start(bf16[256,128]{1,0:T(8,128)(2,1)S(1)} %get-tuple-element.42), channel_id=1, source_target_pairs={{0,3},{1,2},{2,1},{3,0},{4,7},{5,6},{6,5},{7,4},{8,11},{9,10},{10,... | collective-permute-start | bytes 196616 | tf_op jit(solution)/shard_map/ppermute | solution.py:435
  11.8 3.3 %collective-permute-start.5 = (bf16[80,128]{1,0:T(8,128)(2,1)S(1)}, bf16[80,128]{1,0:T(8,128)(2,1)S(1)}, u32[]{:S(2)}, u32[]{:S(2)}) collective-permute-start(bf16[80,128]{1,0:T(8,128)(2,1)S(1)} %get-tuple-element.44.refs_0_), channel_id=1, source_target_pairs={{0,3},{1,2},{2,1},{3,0},{4,7},{5,6},{6,5},{7,4},{8,11},{9,10},{10,... | collective-permute-start | bytes 61448 | tf_op jit(solution)/shard_map/ppermute | solution.py:435
  13.5 12.3 %collective-permute-start.4 = (bf16[80,128]{1,0:T(8,128)(2,1)S(1)}, bf16[80,128]{1,0:T(8,128)(2,1)S(1)}, u32[]{:S(2)}, u32[]{:S(2)}) collective-permute-start(bf16[80,128]{1,0:T(8,128)(2,1)S(1)} %get-tuple-element.44.refs_0_), channel_id=1, source_target_pairs={{0,2},{1,3},{2,0},{3,1},{4,6},{5,7},{6,4},{7,5},{8,10},{9,11},{10,... | collective-permute-start | bytes 61448 | tf_op jit(solution)/shard_map/ppermute | solution.py:435
  15.0 10.7 %collective-permute-start.3 = (bf16[80,128]{1,0:T(8,128)(2,1)S(1)}, bf16[80,128]{1,0:T(8,128)(2,1)S(1)}, u32[]{:S(2)}, u32[]{:S(2)}) collective-permute-start(bf16[80,128]{1,0:T(8,128)(2,1)S(1)} %get-tuple-element.44.refs_0_), channel_id=1, source_target_pairs={{0,1},{1,0},{2,3},{3,2},{4,5},{5,4},{6,7},{7,6},{8,9},{9,8},{10,11... | collective-permute-start | bytes 61448 | tf_op jit(solution)/shard_map/ppermute | solution.py:435
  15.2 10.6 %collective-permute-start.8 = (bf16[80,128]{1,0:T(8,128)(2,1)S(1)}, bf16[80,128]{1,0:T(8,128)(2,1)S(1)}, u32[]{:S(2)}, u32[]{:S(2)}) collective-permute-start(bf16[80,128]{1,0:T(8,128)(2,1)S(1)} %get-tuple-element.45.refs_4_), channel_id=1, source_target_pairs={{0,12},{1,13},{2,14},{3,15},{4,8},{5,9},{6,10},{7,11},{8,4},{9,5},... | collective-permute-start | bytes 61448 | tf_op jit(solution)/shard_map/ppermute | solution.py:438
  19.2 6.6 %collective-permute-start.7 = (bf16[80,128]{1,0:T(8,128)(2,1)S(1)}, bf16[80,128]{1,0:T(8,128)(2,1)S(1)}, u32[]{:S(2)}, u32[]{:S(2)}) collective-permute-start(bf16[80,128]{1,0:T(8,128)(2,1)S(1)} %get-tuple-element.45.refs_4_), channel_id=1, source_target_pairs={{0,8},{1,9},{2,10},{3,11},{4,12},{5,13},{6,14},{7,15},{8,0},{9,1},... | collective-permute-start | bytes 61448 | tf_op jit(solution)/shard_map/ppermute | solution.py:438
  19.2 6.6 %collective-permute-start.6 = (bf16[80,128]{1,0:T(8,128)(2,1)S(1)}, bf16[80,128]{1,0:T(8,128)(2,1)S(1)}, u32[]{:S(2)}, u32[]{:S(2)}) collective-permute-start(bf16[80,128]{1,0:T(8,128)(2,1)S(1)} %get-tuple-element.45.refs_4_), channel_id=1, source_target_pairs={{0,4},{1,5},{2,6},{3,7},{4,0},{5,1},{6,2},{7,3},{8,12},{9,13},{10,... | collective-permute-start | bytes 61448 | tf_op jit(solution)/shard_map/ppermute | solution.py:438
  25.8 40.0 %copy-start.6 = (f32[256]{0:T(256)S(1)}, f32[256]{0:T(256)}, u32[]{:S(2)}) copy-start(f32[256]{0:T(256)} %param.11) | copy-start | bytes 3076
  32.2 21.0 %collective-permute-start.18 = (bf16[256,128]{1,0:T(8,128)(2,1)S(1)}, bf16[256,128]{1,0:T(8,128)(2,1)S(1)}, u32[]{:S(2)}, u32[]{:S(2)}) collective-permute-start(bf16[256,128]{1,0:T(8,128)(2,1)S(1)} %get-tuple-element.68), channel_id=1, source_target_pairs={{0,1},{1,0},{2,3},{3,2},{4,5},{5,4},{6,7},{7,6},{8,9},{9,8},{10,11... | collective-permute-start | bytes 196616 | tf_op jit(solution)/shard_map/ppermute | solution.py:435
  32.2 20.9 %collective-permute-start.19 = (bf16[256,128]{1,0:T(8,128)(2,1)S(1)}, bf16[256,128]{1,0:T(8,128)(2,1)S(1)}, u32[]{:S(2)}, u32[]{:S(2)}) collective-permute-start(bf16[256,128]{1,0:T(8,128)(2,1)S(1)} %get-tuple-element.69), channel_id=1, source_target_pairs={{0,2},{1,3},{2,0},{3,1},{4,6},{5,7},{6,4},{7,5},{8,10},{9,11},{10,... | collective-permute-start | bytes 196616 | tf_op jit(solution)/shard_map/ppermute | solution.py:435
  33.9 19.2 %collective-permute-start.20 = (bf16[256,128]{1,0:T(8,128)(2,1)S(1)}, bf16[256,128]{1,0:T(8,128)(2,1)S(1)}, u32[]{:S(2)}, u32[]{:S(2)}) collective-permute-start(bf16[256,128]{1,0:T(8,128)(2,1)S(1)} %get-tuple-element.70), channel_id=1, source_target_pairs={{0,3},{1,2},{2,1},{3,0},{4,7},{5,6},{6,5},{7,4},{8,11},{9,10},{10,... | collective-permute-start | bytes 196616 | tf_op jit(solution)/shard_map/ppermute | solution.py:435
  34.1 2.0 %collective-permute-start.12 = (bf16[80,128]{1,0:T(8,128)(2,1)S(1)}, bf16[80,128]{1,0:T(8,128)(2,1)S(1)}, u32[]{:S(2)}, u32[]{:S(2)}) collective-permute-start(bf16[80,128]{1,0:T(8,128)(2,1)S(1)} %get-tuple-element.57), channel_id=1, source_target_pairs={{0,1},{1,0},{2,3},{3,2},{4,5},{5,4},{6,7},{7,6},{8,9},{9,8},{10,11... | collective-permute-start | bytes 61448 | tf_op jit(solution)/shard_map/ppermute | solution.py:435
  34.4 4.3 %collective-permute-start.13 = (bf16[80,128]{1,0:T(8,128)(2,1)S(1)}, bf16[80,128]{1,0:T(8,128)(2,1)S(1)}, u32[]{:S(2)}, u32[]{:S(2)}) collective-permute-start(bf16[80,128]{1,0:T(8,128)(2,1)S(1)} %get-tuple-element.58), channel_id=1, source_target_pairs={{0,2},{1,3},{2,0},{3,1},{4,6},{5,7},{6,4},{7,5},{8,10},{9,11},{10,... | collective-permute-start | bytes 61448 | tf_op jit(solution)/shard_map/ppermute | solution.py:435
  36.1 4.0 %collective-permute-start.14 = (bf16[80,128]{1,0:T(8,128)(2,1)S(1)}, bf16[80,128]{1,0:T(8,128)(2,1)S(1)}, u32[]{:S(2)}, u32[]{:S(2)}) collective-permute-start(bf16[80,128]{1,0:T(8,128)(2,1)S(1)} %get-tuple-element.59), channel_id=1, source_target_pairs={{0,3},{1,2},{2,1},{3,0},{4,7},{5,6},{6,5},{7,4},{8,11},{9,10},{10,... | collective-permute-start | bytes 61448 | tf_op jit(solution)/shard_map/ppermute | solution.py:435
  38.8 4.2 %collective-permute-start.15 = (bf16[80,128]{1,0:T(8,128)(2,1)S(1)}, bf16[80,128]{1,0:T(8,128)(2,1)S(1)}, u32[]{:S(2)}, u32[]{:S(2)}) collective-permute-start(bf16[80,128]{1,0:T(8,128)(2,1)S(1)} %get-tuple-element.61), channel_id=1, source_target_pairs={{0,4},{1,5},{2,6},{3,7},{4,0},{5,1},{6,2},{7,3},{8,12},{9,13},{10,... | collective-permute-start | bytes 61448 | tf_op jit(solution)/shard_map/ppermute | solution.py:438
  40.1 6.1 %collective-permute-start.16 = (bf16[80,128]{1,0:T(8,128)(2,1)S(1)}, bf16[80,128]{1,0:T(8,128)(2,1)S(1)}, u32[]{:S(2)}, u32[]{:S(2)}) collective-permute-start(bf16[80,128]{1,0:T(8,128)(2,1)S(1)} %get-tuple-element.62), channel_id=1, source_target_pairs={{0,8},{1,9},{2,10},{3,11},{4,12},{5,13},{6,14},{7,15},{8,0},{9,1},... | collective-permute-start | bytes 61448 | tf_op jit(solution)/shard_map/ppermute | solution.py:438
  43.0 5.6 %collective-permute-start.17 = (bf16[80,128]{1,0:T(8,128)(2,1)S(1)}, bf16[80,128]{1,0:T(8,128)(2,1)S(1)}, u32[]{:S(2)}, u32[]{:S(2)}) collective-permute-start(bf16[80,128]{1,0:T(8,128)(2,1)S(1)} %get-tuple-element.63), channel_id=1, source_target_pairs={{0,12},{1,13},{2,14},{3,15},{4,8},{5,9},{6,10},{7,11},{8,4},{9,5},... | collective-permute-start | bytes 61448 | tf_op jit(solution)/shard_map/ppermute | solution.py:438
  49.8 7.8 %collective-permute-start.26 = (bf16[128,128]{1,0:T(8,128)(2,1)S(1)}, bf16[128,128]{1,0:T(8,128)(2,1)S(1)}, u32[]{:S(2)}, u32[]{:S(2)}) collective-permute-start(bf16[128,128]{1,0:T(8,128)(2,1)S(1)} %get-tuple-element.71.refs_4_), channel_id=1, source_target_pairs={{0,12},{1,13},{2,14},{3,15},{4,8},{5,9},{6,10},{7,11},{8,4},{9,5},... | collective-permute-start | bytes 98312 | tf_op jit(solution)/shard_map/ppermute | solution.py:438
  53.1 4.8 %collective-permute-start.25 = (bf16[128,128]{1,0:T(8,128)(2,1)S(1)}, bf16[128,128]{1,0:T(8,128)(2,1)S(1)}, u32[]{:S(2)}, u32[]{:S(2)}) collective-permute-start(bf16[128,128]{1,0:T(8,128)(2,1)S(1)} %get-tuple-element.71.refs_4_), channel_id=1, source_target_pairs={{0,8},{1,9},{2,10},{3,11},{4,12},{5,13},{6,14},{7,15},{8,0},{9,1},... | collective-permute-start | bytes 98312 | tf_op jit(solution)/shard_map/ppermute | solution.py:438
  53.2 8.7 %collective-permute-start.23 = (bf16[256,128]{1,0:T(8,128)(2,1)S(1)}, bf16[256,128]{1,0:T(8,128)(2,1)S(1)}, u32[]{:S(2)}, u32[]{:S(2)}) collective-permute-start(bf16[256,128]{1,0:T(8,128)(2,1)S(1)} %shard_map.137.refs_0_), channel_id=1, source_target_pairs={{0,12},{1,13},{2,14},{3,15},{4,8},{5,9},{6,10},{7,11},{8,4},{9,5},... | collective-permute-start | bytes 196616 | tf_op jit(solution)/shard_map/ppermute | solution.py:438
  53.9 8.0 %collective-permute-start.22 = (bf16[256,128]{1,0:T(8,128)(2,1)S(1)}, bf16[256,128]{1,0:T(8,128)(2,1)S(1)}, u32[]{:S(2)}, u32[]{:S(2)}) collective-permute-start(bf16[256,128]{1,0:T(8,128)(2,1)S(1)} %shard_map.137.refs_0_), channel_id=1, source_target_pairs={{0,8},{1,9},{2,10},{3,11},{4,12},{5,13},{6,14},{7,15},{8,0},{9,1},... | collective-permute-start | bytes 196616 | tf_op jit(solution)/shard_map/ppermute | solution.py:438
  56.2 5.6 %collective-permute-start.21 = (bf16[256,128]{1,0:T(8,128)(2,1)S(1)}, bf16[256,128]{1,0:T(8,128)(2,1)S(1)}, u32[]{:S(2)}, u32[]{:S(2)}) collective-permute-start(bf16[256,128]{1,0:T(8,128)(2,1)S(1)} %shard_map.137.refs_0_), channel_id=1, source_target_pairs={{0,4},{1,5},{2,6},{3,7},{4,0},{5,1},{6,2},{7,3},{8,12},{9,13},{10,... | collective-permute-start | bytes 196616 | tf_op jit(solution)/shard_map/ppermute | solution.py:438
  57.6 8.1 %collective-permute-start.9 = (bf16[256,128]{1,0:T(8,128)(2,1)S(1)}, bf16[256,128]{1,0:T(8,128)(2,1)S(1)}, u32[]{:S(2)}, u32[]{:S(2)}) collective-permute-start(bf16[256,128]{1,0:T(8,128)(2,1)S(1)} %get-tuple-element.51), channel_id=1, source_target_pairs={{0,1},{1,0},{2,3},{3,2},{4,5},{5,4},{6,7},{7,6},{8,9},{9,8},{10,11... | collective-permute-start | bytes 196616 | tf_op jit(solution)/shard_map/ppermute | solution.py:435
  57.9 3.9 %collective-permute-start.24 = (bf16[128,128]{1,0:T(8,128)(2,1)S(1)}, bf16[128,128]{1,0:T(8,128)(2,1)S(1)}, u32[]{:S(2)}, u32[]{:S(2)}) collective-permute-start(bf16[128,128]{1,0:T(8,128)(2,1)S(1)} %get-tuple-element.71.refs_4_), channel_id=1, source_target_pairs={{0,4},{1,5},{2,6},{3,7},{4,0},{5,1},{6,2},{7,3},{8,12},{9,13},{10,... | collective-permute-start | bytes 98312 | tf_op jit(solution)/shard_map/ppermute | solution.py:438
  61.9 10.7 %collective-permute-start.29 = (bf16[384,128]{1,0:T(8,128)(2,1)S(1)}, bf16[384,128]{1,0:T(8,128)(2,1)S(1)}, u32[]{:S(2)}, u32[]{:S(2)}) collective-permute-start(bf16[384,128]{1,0:T(8,128)(2,1)S(1)} %shard_map.138.m0), channel_id=1, source_target_pairs={{0,3},{1,2},{2,1},{3,0},{4,7},{5,6},{6,5},{7,4},{8,11},{9,10},{10,... | collective-permute-start | bytes 294920 | tf_op jit(solution)/shard_map/ppermute | solution.py:435
  62.6 10.1 %collective-permute-start.28 = (bf16[384,128]{1,0:T(8,128)(2,1)S(1)}, bf16[384,128]{1,0:T(8,128)(2,1)S(1)}, u32[]{:S(2)}, u32[]{:S(2)}) collective-permute-start(bf16[384,128]{1,0:T(8,128)(2,1)S(1)} %shard_map.138.m0), channel_id=1, source_target_pairs={{0,2},{1,3},{2,0},{3,1},{4,6},{5,7},{6,4},{7,5},{8,10},{9,11},{10,... | collective-permute-start | bytes 294920 | tf_op jit(solution)/shard_map/ppermute | solution.py:435
  64.0 8.7 %collective-permute-start.27 = (bf16[384,128]{1,0:T(8,128)(2,1)S(1)}, bf16[384,128]{1,0:T(8,128)(2,1)S(1)}, u32[]{:S(2)}, u32[]{:S(2)}) collective-permute-start(bf16[384,128]{1,0:T(8,128)(2,1)S(1)} %shard_map.138.m0), channel_id=1, source_target_pairs={{0,1},{1,0},{2,3},{3,2},{4,5},{5,4},{6,7},{7,6},{8,9},{9,8},{10,11... | collective-permute-start | bytes 294920 | tf_op jit(solution)/shard_map/ppermute | solution.py:435
  64.0 7.0 %collective-permute-start.10 = (bf16[256,128]{1,0:T(8,128)(2,1)S(1)}, bf16[256,128]{1,0:T(8,128)(2,1)S(1)}, u32[]{:S(2)}, u32[]{:S(2)}) collective-permute-start(bf16[256,128]{1,0:T(8,128)(2,1)S(1)} %get-tuple-element.52), channel_id=1, source_target_pairs={{0,2},{1,3},{2,0},{3,1},{4,6},{5,7},{6,4},{7,5},{8,10},{9,11},{10,... | collective-permute-start | bytes 196616 | tf_op jit(solution)/shard_map/ppermute | solution.py:435
  65.7 5.9 %collective-permute-start.11 = (bf16[256,128]{1,0:T(8,128)(2,1)S(1)}, bf16[256,128]{1,0:T(8,128)(2,1)S(1)}, u32[]{:S(2)}, u32[]{:S(2)}) collective-permute-start(bf16[256,128]{1,0:T(8,128)(2,1)S(1)} %get-tuple-element.53), channel_id=1, source_target_pairs={{0,3},{1,2},{2,1},{3,0},{4,7},{5,6},{6,5},{7,4},{8,11},{9,10},{10,... | collective-permute-start | bytes 196616 | tf_op jit(solution)/shard_map/ppermute | solution.py:435
  (8 other events, 6.2 us)

commit v2 on v1

v2 whole, which is shorter than its diff:
```python
import jax
import jax.numpy as jnp
from jax import lax
from jax.experimental import pallas as pl
from jax.experimental.pallas import tpu as pltpu
from jax.sharding import PartitionSpec as P

PAIRED = 32
EXTRA = 8
QUAD = 4
BLOCK = 8
RANK = 32
PACKED = 80
F32 = jnp.float32
BF16 = jnp.bfloat16
SMEM = pl.BlockSpec(memory_space=pltpu.SMEM)


def vmem():
    return pl.BlockSpec(memory_space=pltpu.VMEM)


def params(mib=48):
    return pltpu.CompilerParams(vmem_limit_bytes=mib * 1024 * 1024)


def sds(shape, dtype):
    return jax.ShapeDtypeStruct(shape, dtype)


def place():
    k = lax.axis_index("row")
    return k >> 2, k & 3


def bounds_of(ref):
    ends, total = [], jnp.int32(0)
    for c in range(ref.shape[0]):
        total = total + ref[c]
        ends.append(total)
    return ends


def chain_of(residue, ends):
    chain = jnp.zeros(residue.shape, jnp.int32)
    for end in ends:
        chain = chain + jnp.where(residue >= end, 1, 0)
    return chain


def count_of(chain, hom_ref):
    picked = jnp.zeros(chain.shape, F32)
    for c in range(hom_ref.shape[0]):
        picked = jnp.where(chain == c, hom_ref[c].astype(F32), picked)
    return picked


def swap4(xs, low):
    lane = lax.broadcasted_iota(jnp.int32, xs[0].shape, 1)
    for bit, step in ((2, 2 * low), (1, low)):
        keep = (lane & step) == 0
        ys = list(xs)
        for q in range(4):
            if q & bit == 0:
                lo, hi = xs[q], xs[q | bit]
                ys[q] = jnp.where(keep, lo, pltpu.roll(hi, step, 1))
                ys[q | bit] = jnp.where(keep, pltpu.roll(lo, 128 - step, 1), hi)
        xs = ys
    return xs


def unpack(message):
    m = message.astype(F32)
    return [
        jnp.concatenate([m[0:32], m[64:72]], axis=0),
        jnp.concatenate([m[32:64], m[72:80]], axis=0),
    ]


def pack(lo, hi):
    return jnp.concatenate([lo[0:32], hi[0:32], lo[32:40], hi[32:40]], axis=0).astype(BF16)


def spread_rows(compact, chain, chains):
    rows = [compact[0:PAIRED]]
    extra = compact[PAIRED:]
    for c in range(chains):
        rows.append(jnp.where(chain == c, extra, 0.0))
    return jnp.concatenate(rows, axis=0)


def gather_rows(full, chain, chains):
    extra = jnp.zeros((EXTRA, full.shape[1]), F32)
    for c in range(chains):
        top = PAIRED + EXTRA * c
        extra = jnp.where(chain == c, full[top : top + EXTRA], extra)
    return jnp.concatenate([full[0:PAIRED], extra], axis=0)


def left_chain(a, b, ends):
    lane = lax.broadcasted_iota(jnp.int32, (EXTRA, 128), 1)
    residue = 32 * a + 8 * (b ^ (lane >> 5)) + (lane & 7)
    return jnp.concatenate([chain_of(residue, ends)] * 8, axis=1)


def right_chain(a, b, chunk, ends):
    lane = lax.broadcasted_iota(jnp.int32, (EXTRA, 256), 1)
    parts = []
    for tt in range(4):
        residue = 32 * (a ^ (4 * chunk + tt)) + 8 * b + (lane >> 5)
        parts.append(chain_of(residue, ends))
    return jnp.concatenate(parts, axis=1)


def spread_matrix():
    row = lax.broadcasted_iota(jnp.int32, (512, 512), 0)
    o = lax.broadcasted_iota(jnp.int32, (512, 512), 1)
    r, k = row >> 6, row & 63
    target = jnp.where(k < RANK, k * 8 + r, 256 + r * 32 + (k - RANK))
    return jnp.where(o == target, 1.0, 0.0).astype(BF16)


def swap_matrix():
    row = lax.broadcasted_iota(jnp.int32, (512, 512), 0)
    col = lax.broadcasted_iota(jnp.int32, (512, 512), 1)
    q, m = row >> 7, (row >> 3) & 3
    target = (m << 7) | (row & 0x67) | (q << 3)
    return jnp.where(col == target, 1.0, 0.0).astype(BF16)


def fetch(pairs, sems):
    copies = [pltpu.make_async_copy(a, b, sems.at[n]) for n, (a, b) in enumerate(pairs)]
    for c in copies:
        c.start()
    return copies


def start_kernel(
    x_hbm, adj_hbm, scale_hbm, shift_hbm, mat_hbm, off_hbm, len_hbm, hom_hbm, final_hbm,
    m0, m1, m2, m3, right_ref, norm_ref, hat_ref, rstd_ref, spread_ref, swap_ref, final_ref,
    x_ref, adj_ref, scale_ref, shift_ref, mat_ref, off_ref, len_ref, hom_ref,
    work, full, comp, sems,
):
    messages = (m0, m1, m2, m3)
    copies = fetch(
        [
            (adj_hbm, adj_ref), (x_hbm, x_ref), (scale_hbm, scale_ref),
            (shift_hbm, shift_ref), (mat_hbm, mat_ref), (off_hbm, off_ref),
            (len_hbm, len_ref), (hom_hbm, hom_ref), (final_hbm, final_ref),
        ],
        sems,
    )
    depth = x_ref.shape[0]
    residues = adj_ref.shape[1]
    groups = residues // 32
    chains = len_ref.shape[0]
    a, b = place()
    spread = spread_matrix()
    spread_ref[...] = spread
    swap_ref[...] = swap_matrix()
    copies[0].wait()
    work[...] = adj_ref[...].astype(F32).reshape(BLOCK * residues, 128)
    for t in range(QUAD):

        def step(u, _, t=t):
            tiles = []
            for jj in range(BLOCK):
                j = 32 * (a ^ u) + 8 * (b ^ t) + jj
                tiles.append(work[pl.ds(j, BLOCK, stride=residues), :])
            rows = pl.ds(pl.multiple_of(u * 64, 64), 64)
            messages[t][rows, :] = jnp.concatenate(tiles, axis=0).astype(BF16)
            return 0

        lax.fori_loop(0, groups, step, 0, unroll=groups <= 4)
    for c in copies[1:8]:
        c.wait()
    x = x_ref[...].astype(F32)
    centred = x - jnp.mean(x, axis=-1, keepdims=True)
    rstd = lax.rsqrt(jnp.mean(centred * centred, axis=-1, keepdims=True) + 1e-05)
    hat = (centred * rstd).reshape(depth * BLOCK, 256)
    normed = (hat * scale_ref[...] + shift_ref[...]).astype(BF16)
    hat_ref[...] = hat
    norm_ref[...] = normed
    rstd_ref[...] = jnp.broadcast_to(rstd, (depth, BLOCK, 128)).reshape(depth * BLOCK, 128)
    proj = lax.dot_general(
        normed, mat_ref[...], (((1,), (1,)), ((), ())), preferred_element_type=F32
    ) + off_ref[...]
    full[0 : depth * BLOCK, :] = proj
    full[depth * BLOCK :, :] = jnp.zeros((EXTRA * BLOCK, 64), F32)
    comp[0 : PAIRED * BLOCK, :] = proj[0 : PAIRED * BLOCK]
    residue = lax.broadcasted_iota(jnp.int32, (EXTRA * BLOCK, 64), 0)
    entry = residue >> 3
    chain = chain_of(32 * a + 8 * b + (residue & 7), bounds_of(len_ref))
    extra = jnp.zeros((EXTRA * BLOCK, 64), F32)
    start = jnp.int32(PAIRED)
    for c in range(chains):
        rows = full[pl.ds(pl.multiple_of(start * BLOCK, BLOCK), EXTRA * BLOCK), :]
        extra = jnp.where((chain == c) & (entry < hom_ref[c]), rows, extra)
        start = start + hom_ref[c]
    comp[PAIRED * BLOCK :, :] = extra
    rows = PAIRED + EXTRA
    wide = jnp.concatenate([comp[pl.ds(r, rows, stride=BLOCK), :] for r in range(BLOCK)], axis=1)
    out = jnp.dot(wide.astype(BF16), spread, preferred_element_type=F32)
    left = pack(out[:, 0:128], out[:, 128:256])
    for m in messages:
        m[groups * 64 :, :] = left
    right_ref[...] = pack(out[:, 256:384], out[:, 384:512])
    copies[8].wait()


def adjoint_kernel(
    chunks, len_ref, hom_ref, final_ref, swap_ref, m0, m1, m2, m3, s_ref, og_ref, ft_ref
):
    messages = (m0, m1, m2, m3)
    a, b = place()
    ends = bounds_of(len_ref)
    swap = swap_ref[...]
    low = lax.broadcasted_iota(jnp.int32, (32, 128), 0)
    chain_i, inv_same = [], []
    for t in range(QUAD):
        chain = chain_of(32 * a + 8 * (b ^ t) + (low & 7), ends)
        chain_i.append(chain)
        inv_same.append(1.0 / (float(PAIRED) + count_of(chain, hom_ref) + 0.001))
    inv_other = 1.0 / jnp.full((32, 128), PAIRED + 0.001, F32)
    final = final_ref[...]
    ft_ref[...] = final.astype(F32).T.astype(BF16)

    def step(g, _):
        blocks = []
        for tt in range(4):
            u = 4 * g + tt
            for half in range(2):
                chain_j = chain_of(32 * (a ^ u) + 8 * b + 4 * half + (low >> 3), ends)
                top = pl.ds(pl.multiple_of(u * 64 + half * 32, 32), 32)
                for t in range(QUAD):
                    inv = jnp.where(chain_i[t] == chain_j, inv_same[t], inv_other)
                    blocks.append(messages[t][top, :].astype(F32) * inv)
        s = jnp.concatenate(blocks, axis=0)
        s_ref[pl.ds(pl.multiple_of(g * 1024, 1024), 1024), :] = s.astype(BF16)
        st = s.T.astype(BF16)
        for cb in range(8):
            og = jnp.dot(
                final[cb * 128 : cb * 128 + 128, :], st, preferred_element_type=F32
            ).astype(BF16)
            wide = jnp.concatenate(
                [
                    jnp.concatenate(
                        [og[q * 32 : q * 32 + 32, jg * 128 : jg * 128 + 128] for q in range(4)],
                        axis=1,
                    )
                    for jg in range(8)
                ],
                axis=0,
            )
            moved = jnp.dot(wide, swap, preferred_element_type=F32).astype(BF16)
            for jg in range(8):
                for jl in range(4):
                    top = pl.ds(pl.multiple_of(g * 1024 + (jg * 4 + jl) * 32, 32), 32)
                    og_ref[top, cb * 128 : cb * 128 + 128] = moved[
                        jg * 32 : jg * 32 + 32, jl * 128 : jl * 128 + 128
                    ]
        return 0

    lax.fori_loop(0, chunks, step, 0, unroll=chunks == 1)


def left_lanes(lefts):
    parts = [unpack(m) for m in lefts]
    lanes = []
    for h in range(2):
        lanes += swap4([parts[t][h] for t in range(QUAD)], 32)
    return jnp.concatenate(lanes, axis=1)


def right_lanes(rights):
    return jnp.concatenate([blk for m in rights for blk in unpack(m)], axis=1)


def grad_kernel(
    chunks, len_ref, og_ref, m0, m1, m2, m3, r0, r1, r2, r3,
    l0, l1, l2, l3, g0, g1, g2, g3, lx_ref, rt_ref, lg_acc,
):
    messages, rights = (m0, m1, m2, m3), (r0, r1, r2, r3)
    lefts, grads = (l0, l1, l2, l3), (g0, g1, g2, g3)
    chains = len_ref.shape[0]
    a, b = place()
    ends = bounds_of(len_ref)
    chain_l = left_chain(a, b, ends)
    top = chunks * 256
    lx = spread_rows(
        left_lanes([m[top : top + PACKED, :] for m in messages]), chain_l, chains
    ).astype(BF16)
    lx_ref[...] = lx
    lg_acc[...] = jnp.zeros(lg_acc.shape, F32)

    def step(g, _):
        chain_r = right_chain(a, b, g, ends)
        at80 = pl.ds(pl.multiple_of(g * PACKED, 16), PACKED)
        at1024 = pl.ds(pl.multiple_of(g * 1024, 1024), 1024)
        rx = spread_rows(right_lanes([r[at80, :] for r in rights]), chain_r, chains)
        rt_ref[at1024, :] = rx.T.astype(BF16)
        og = og_ref[at1024, :]
        rg = lax.dot_general(lx, og, (((1,), (1,)), ((), ())), preferred_element_type=F32)
        rg = gather_rows(rg, chain_r, chains)
        for tt in range(4):
            grads[tt][at80, :] = pack(
                rg[:, tt * 256 : tt * 256 + 128], rg[:, tt * 256 + 128 : tt * 256 + 256]
            )
        lg_acc[...] += jnp.dot(rx.astype(BF16), og, preferred_element_type=F32)
        return 0

    lax.fori_loop(0, chunks, step, 0, unroll=chunks == 1)
    lgc = gather_rows(lg_acc[...], chain_l, chains)
    halves = []
    for h in range(2):
        xs = [lgc[:, (4 * h + q) * 128 : (4 * h + q + 1) * 128] for q in range(4)]
        halves.append(swap4(xs, 32))
    for t in range(QUAD):
        lefts[t][...] = pack(halves[0][t], halves[1][t])


def pair_kernel(
    chunks, len_ref, hom_ref, s_ref, ft_ref, swap_ref, bias_ref, lx_ref, rt_ref,
    l0, l1, l2, l3, own_ref, cross_ref, core_ref, p0, p1, px, n_buf, w_acc,
):
    lefts = (l0, l1, l2, l3)
    quads = ((own_ref, 0), (core_ref, 0), (cross_ref, 0), (core_ref, 256 + PACKED))
    pairs = ((p0, 0), (p1, 0), (px, 0), (px, chunks * 256))
    a, b = place()
    ends = bounds_of(len_ref)
    w_acc[...] = jnp.zeros(w_acc.shape, F32)
    lx = lx_ref[...]
    swap = swap_ref[...]
    bias = bias_ref[...]
    lane = lax.broadcasted_iota(jnp.int32, (8, 128), 1)
    chain_i = chain_of(32 * a + 8 * (b ^ (lane >> 5)) + (lane & 7), ends)
    same_inv = 1.0 / (float(PAIRED) + count_of(chain_i, hom_ref) + 0.001)
    other_inv = 1.0 / jnp.full((8, 128), PAIRED + 0.001, F32)

    def step(g, _):
        for jg in range(8):
            at = pl.ds(pl.multiple_of(g * 1024 + jg * 128, 128), 128)
            o = jnp.dot(rt_ref[at, :], lx, preferred_element_type=F32).astype(BF16)
            wide = jnp.concatenate(
                [
                    jnp.concatenate(
                        [o[q * 32 : q * 32 + 32, cb * 128 : cb * 128 + 128] for q in range(4)],
                        axis=1,
                    )
                    for cb in range(8)
                ],
                axis=0,
            )
            moved = jnp.dot(wide, swap, preferred_element_type=F32).astype(BF16)
            for cb in range(8):
                for cl in range(4):
                    row = (cb * 4 + cl) * 32
                    n_buf[row : row + 32, jg * 128 : jg * 128 + 128] = moved[
                        cb * 32 : cb * 32 + 32, cl * 128 : cl * 128 + 128
                    ]
        n = n_buf[...]
        s = s_ref[pl.ds(pl.multiple_of(g * 1024, 1024), 1024), :]
        w_acc[...] += jnp.dot(n, s, preferred_element_type=F32)
        pt = jnp.dot(ft_ref[...], n, preferred_element_type=F32)
        tiles = []
        for tt in range(4):
            for half in range(2):
                res_j = 32 * (a ^ (4 * g + tt)) + 8 * b + 4 * half + ((lane >> 3) & 3)
                inv = jnp.where(chain_i == chain_of(res_j, ends), same_inv, other_inv)
                inv_col = jnp.broadcast_to(inv[0:1], (128, 128)).T
                blk = tt * 2 + half
                tiles.append((pt[:, blk * 128 : blk * 128 + 128].T + bias) * inv_col)
        for t in range(QUAD):
            ref, top = pairs[t]
            ref[pl.ds(pl.multiple_of(top + g * 256, 256), 256), :] = jnp.concatenate(
                [v[t * 32 : t * 32 + 32] for v in tiles], axis=0
            ).astype(BF16)
        return 0

    lax.fori_loop(0, chunks, step, 0, unroll=chunks == 1)
    for t in range(QUAD):
        ref, top = quads[t]
        ref[top + 256 : top + 256 + PACKED, :] = lefts[t][...]
        rows = pl.ds(pl.multiple_of((b ^ t) * 256, 256), 256)
        ref[top : top + 256, :] = w_acc[rows, :].astype(BF16)


def total(values):
    out = values[0].astype(F32)
    for value in values[1:]:
        out = out + value.astype(F32)
    return out


def middle_kernel(own_ref, cross_ref, core_ref, mine_ref, theirs_ref):
    rows = 256 + PACKED
    mine_ref[...] = own_ref[...].astype(F32) + core_ref[0:rows, :].astype(F32)
    theirs_ref[...] = total([cross_ref[...], core_ref[rows:, :]]).astype(BF16)


def back_kernel(groups, len_ref, hom_ref, spread_ref, norm_ref, *refs):
    quads, rgs = refs[:2], refs[2 : 2 + groups]
    pg_ref, out_ref, comp, full = refs[2 + groups :]
    chains = len_ref.shape[0]
    depth8 = pg_ref.shape[0]
    a, b = place()
    out_ref[0:256, :] = total([q[0:256, :] for q in quads]).astype(BF16)
    lg = total([q[256:, :] for q in quads])
    rg = total([r[...] for r in rgs])
    wide = jnp.concatenate([blk for g in (lg, rg) for blk in unpack(g)], axis=1)
    rows = PAIRED + EXTRA
    per = lax.dot_general(
        wide.astype(BF16), spread_ref[...], (((1,), (1,)), ((), ())), preferred_element_type=F32
    )
    for r in range(BLOCK):
        comp[pl.ds(r, rows, stride=BLOCK), :] = per[:, r * 64 : r * 64 + 64]
    full[0 : PAIRED * BLOCK, :] = comp[0 : PAIRED * BLOCK, :]
    full[PAIRED * BLOCK :, :] = jnp.zeros((full.shape[0] - PAIRED * BLOCK, 64), F32)
    extra = comp[PAIRED * BLOCK :, :]
    residue = lax.broadcasted_iota(jnp.int32, (EXTRA * BLOCK, 64), 0)
    entry = residue >> 3
    chain = chain_of(32 * a + 8 * b + (residue & 7), bounds_of(len_ref))
    start = jnp.int32(PAIRED)
    for c in range(chains):
        at = pl.ds(pl.multiple_of(start * BLOCK, BLOCK), EXTRA * BLOCK)
        full[at, :] += jnp.where((chain == c) & (entry < hom_ref[c]), extra, 0.0)
        start = start + hom_ref[c]
    pg = full[0:depth8, :]
    pg_ref[...] = pg.astype(BF16)
    fm = jnp.dot(pg.T.astype(BF16), norm_ref[...], preferred_element_type=F32)
    out_ref[256:384, :] = jnp.concatenate([fm[:, 0:128], fm[:, 128:256]], axis=0).astype(BF16)


def align_kernel(pg_ref, mat_ref, scale_ref, hat_ref, rstd_ref, out_ref):
    g = jnp.dot(pg_ref[...], mat_ref[...], preferred_element_type=F32)
    g = g * scale_ref[...]
    hat = hat_ref[...]
    m1 = jnp.mean(g, axis=-1, keepdims=True)
    m2 = jnp.mean(g * hat, axis=-1, keepdims=True)
    rstd = rstd_ref[...]
    dx = (g - m1 - hat * m2) * jnp.concatenate([rstd, rstd], axis=1)
    out_ref[...] = dx.reshape(out_ref.shape).astype(BF16)


def assemble_kernel(*refs):
    pieces, out_ref, work = refs[:QUAD], refs[QUAD], refs[QUAD + 1]
    residues = out_ref.shape[1]
    groups = residues // 32
    tops = (0, 0, 0, groups * 64)
    a, b = place()
    for t in range(QUAD):

        def step(u, _, t=t):
            tile = pieces[t][pl.ds(pl.multiple_of(tops[t] + u * 64, 64), 64), :].astype(F32)
            for jj in range(BLOCK):
                j = 32 * (a ^ u) + 8 * (b ^ t) + jj
                work[pl.ds(j, BLOCK, stride=residues), :] = tile[jj * 8 : jj * 8 + 8]
            return 0

        lax.fori_loop(0, groups, step, 0, unroll=groups <= 4)
    out_ref[...] = work[...].reshape(out_ref.shape).astype(BF16)


def merge_kernel(*refs):
    refs[-1][...] = total([r[...] for r in refs[:-1]]).astype(BF16)


def relay_kernel(own_ref, cross_ref, out_ref):
    out_ref[0:256, :] = own_ref[0:256, :]
    out_ref[256:512, :] = cross_ref[0:256, :]
    out_ref[512:640, :] = total([own_ref[256:384, :], cross_ref[256:384, :]]).astype(BF16)


def final_kernel(mine_ref, core_ref, w_ref, fm_ref):
    _, b = place()
    for t in range(QUAD):
        rows = pl.ds(pl.multiple_of((b ^ t) * 256, 256), 256)
        ref, top = (mine_ref, core_ref)[t & 1], (t >> 1) * 256
        w_ref[rows, :] = ref[top : top + 256, :].astype(F32)
    fm = total([mine_ref[512:640, :], core_ref[512:640, :]])
    fm_ref[...] = jnp.concatenate([fm[0:64], fm[64:128]], axis=1)


HBM = pl.BlockSpec(memory_space=pltpu.HBM)


def call(kernel, outs, ins, in_specs=None, out_specs=None, scratch=(), work=0, mib=48):
    many = isinstance(outs, (list, tuple))
    if in_specs is not None:
        ins = [
            pltpu.with_memory_space_constraint(v, pltpu.HBM) if spec is HBM else v
            for v, spec in zip(ins, in_specs)
        ]
    return pl.pallas_call(
        kernel,
        out_shape=outs,
        in_specs=in_specs if in_specs is not None else [vmem()] * len(ins),
        out_specs=out_specs or ([vmem()] * len(outs) if many else vmem()),
        scratch_shapes=list(scratch),
        compiler_params=params(mib),
        cost_estimate=pl.CostEstimate(flops=work, bytes_accessed=work // 500, transcendentals=0),
    )(*ins)


def on_device(
    devices, x, scale, shift, mat, off, final, bias, adjoint, lengths, homologs
):
    groups = devices // QUAD
    chunks = groups // 4
    residues = adjoint.shape[1]
    depth = x.shape[0]
    scale, shift, off, bias = scale[None], shift[None], off[None], bias[None]
    mat = mat.T

    def near(value, t):
        return lax.ppermute(value, "row", [(k, k ^ t) for k in range(devices)])

    def far(value, u):
        return lax.ppermute(value, "row", [(k, k ^ (4 * u)) for k in range(devices)])

    def quad(parts):
        return [parts[0]] + [near(parts[t], t) for t in range(1, QUAD)]

    def by_slot(parts):
        if chunks == 1:
            return parts
        return [jnp.concatenate(parts[s::4], axis=0) for s in range(4)]

    def from_slot(parts, rows):
        if chunks == 1:
            return parts
        return [parts[u % 4][(u // 4) * rows : (u // 4 + 1) * rows] for u in range(groups)]

    *messages, right, normed, hat, rstd, spread, swap, final = call(
        start_kernel,
        [sds((groups * 64 + PACKED, 128), BF16)] * QUAD
        + [
            sds((PACKED, 128), BF16),
            sds((depth * BLOCK, 256), BF16),
            sds((depth * BLOCK, 256), F32),
            sds((depth * BLOCK, 128), F32),
            sds((512, 512), BF16),
            sds((512, 512), BF16),
            sds(final.shape, BF16),
        ],
        [x, adjoint, scale, shift, mat, off, lengths, homologs, final],
        in_specs=[HBM] * 9,
        scratch=[
            pltpu.VMEM(x.shape, BF16),
            pltpu.VMEM(adjoint.shape, BF16),
            pltpu.VMEM((1, 256), F32),
            pltpu.VMEM((1, 256), F32),
            pltpu.VMEM((64, 256), BF16),
            pltpu.VMEM((1, 64), F32),
            pltpu.SMEM(lengths.shape, jnp.int32),
            pltpu.SMEM(homologs.shape, jnp.int32),
            pltpu.VMEM((BLOCK * residues, 128), F32),
            pltpu.VMEM(((depth + EXTRA) * BLOCK, 64), F32),
            pltpu.VMEM(((PAIRED + EXTRA) * BLOCK, 64), F32),
            pltpu.SemaphoreType.DMA((9,)),
        ],
        work=10**9,
    )
    messages = quad(messages)
    rights = by_slot([right] + [far(right, u) for u in range(1, groups)])

    s, og, final_t = call(
        lambda *refs: adjoint_kernel(chunks, *refs),
        [
            sds((chunks * 1024, 128), BF16),
            sds((chunks * 1024, 1024), BF16),
            sds((128, 1024), BF16),
        ],
        [lengths, homologs, final, swap, *messages],
        in_specs=[SMEM] * 2 + [vmem()] * (2 + QUAD),
        work=2 * 10**9,
    )

    outs = call(
        lambda *refs: grad_kernel(chunks, *refs),
        [sds((PACKED, 128), BF16)] * QUAD
        + [sds((chunks * PACKED, 128), BF16)] * 4
        + [sds((128, 1024), BF16), sds((chunks * 1024, 128), BF16)],
        [lengths, og, *messages, *rights],
        in_specs=[SMEM] + [vmem()] * (1 + 2 * QUAD),
        scratch=[pltpu.VMEM((128, 1024), F32)],
        work=2 * 10**9,
    )
    lgs, rgs, (lx, rt) = outs[0:4], list(outs[4:8]), outs[8:10]
    rgs = from_slot(rgs, PACKED)
    rgs = [rgs[0]] + [far(rgs[u], u) for u in range(1, groups)]
    own, cross, core, pair_own, pair_core, pair_cross = call(
        lambda *refs: pair_kernel(chunks, *refs),
        [sds((256 + PACKED, 128), BF16)] * 2
        + [sds((512 + 2 * PACKED, 128), BF16)]
        + [sds((groups * 64, 128), BF16)] * 2
        + [sds((groups * 128, 128), BF16)],
        [lengths, homologs, s, final_t, swap, bias, lx, rt, *lgs],
        in_specs=[SMEM] * 2 + [vmem()] * (6 + QUAD),
        scratch=[pltpu.VMEM((1024, 1024), BF16), pltpu.VMEM((1024, 128), F32)],
        work=4 * 10**9,
    )
    core = near(core, 1)
    mine, theirs = call(
        middle_kernel,
        [sds((256 + PACKED, 128), F32), sds((256 + PACKED, 128), BF16)],
        [own, cross, core],
        work=10**7,
    )
    quads = [mine, near(theirs, 2)]

    pg, part = call(
        lambda *refs: back_kernel(groups, *refs),
        [sds((depth * BLOCK, 64), BF16), sds((384, 128), BF16)],
        [lengths, homologs, spread, normed, *quads, *rgs],
        in_specs=[SMEM] * 2 + [vmem()] * (4 + groups),
        scratch=[
            pltpu.VMEM(((PAIRED + EXTRA) * BLOCK, 64), F32),
            pltpu.VMEM(((depth + EXTRA) * BLOCK, 64), F32),
        ],
        work=10**9,
    )
    parts = [part] + [far(part, u) for u in range(1, groups)]
    pair_cross = near(pair_cross, 2)
    pairs = [pair_own, near(pair_core, 1), pair_cross, near(pair_cross, 1)]
    alignment_gradient = call(
        align_kernel,
        sds(x.shape, BF16),
        [pg, mat, scale, hat, rstd],
        work=10**9,
    )
    pair_delta = call(
        assemble_kernel,
        sds(adjoint.shape, BF16),
        pairs,
        scratch=[pltpu.VMEM((BLOCK * residues, 128), F32)],
        work=10**9,
    )
    parts, alignment_gradient, pair_delta = lax.optimization_barrier(
        (parts, alignment_gradient, pair_delta)
    )
    merged = call(merge_kernel, sds((384, 128), BF16), parts, work=10**7)
    relay = call(relay_kernel, sds((640, 128), BF16), [merged, near(merged, 2)], work=10**7)
    w, fm = call(
        final_kernel,
        [sds((1024, 128), F32), sds((64, 256), F32)],
        [relay, near(relay, 1)],
        work=10**8,
    )
    return pair_delta, alignment_gradient, w, fm.T


def solution(mesh):
    devices = mesh.shape["row"]

    def body(*args):
        return on_device(devices, *args)

    return jax.shard_map(
        body,
        mesh=mesh,
        in_specs=(
            P("groups", "row", None),
            P(),
            P(),
            P(),
            P(),
            P(),
            P(),
            P(("groups", "row"), None, None),
            P("groups"),
            P("groups"),
        ),
        out_specs=(
            P(("groups", "row"), None, None),
            P("groups", "row", None),
            P("groups", None),
            P("groups", None),
        ),
        check_vma=False,
    )
```

time: 74.6 us -> 50.9 us (0.68)
  starting transfers between devices: 34 us -> 21 us
  local copies, waits for them, and re-layouts: 7.78 us -> 0.02 us
  waiting for transfers between devices: 14.2 us -> 12.7 us
  Pallas kernels: 17.5 us -> 16.2 us
    pallas_call x3 -> x0, Pallas kernels: 11.3 us -> none  [the longest x1 4.94 us: on_device(): pl.pallas_call(adjoint_kernel, grid=(chunks,), out_shape=[sds((chunks * 1...]
    pallas_call x8 -> x11, Pallas kernels: 6.24 us -> 16.2 us  [call(): pl.pallas_call(kernel, out_shape=outs, in_specs=in_specs if in_specs is n...]
    unnamed x22 -> x10, local copies, waits for them, and re-layouts: 7.78 us -> 0.02 us
    ppermute x12 -> x9, starting transfers between devices: 20.2 us -> 13.2 us  [far(): return lax.ppermute(value, 'row', [(k, k ^ 4 * u) for k in range(devices)])]
    ppermute x18 -> x10, starting transfers between devices: 13.8 us -> 7.75 us  [near(): return lax.ppermute(value, 'row', [(k, k ^ t) for k in range(devices)])]
    ppermute x18 -> x10, waiting for transfers between devices: 7.98 us -> 5.37 us  [near(): return lax.ppermute(value, 'row', [(k, k ^ t) for k in range(devices)])]
    ppermute x12 -> x9, waiting for transfers between devices: 6.17 us -> 7.36 us  [far(): return lax.ppermute(value, 'row', [(k, k ^ 4 * u) for k in range(devices)])]
  transfers between devices with their start and end apart: 30 -> 19, of which waited for: 7 -> 8; matrix products, arithmetic and copies ran while one was open for 1% -> 0% of each run, Pallas kernels for 13% -> 14%
where the time goes in v2:
time: 50.9 us; the launch traced here: 50.7 us
  starting transfers between devices  21 us (41%)
  Pallas kernels  16.2 us (32%)
  waiting for transfers between devices  12.7 us (25%)
  between operations  0.76 us (1%)
    pallas_call x11, Pallas kernels, call(): pl.pallas_call(kernel, out_shape=outs, in_specs=in_specs if in_specs is n...  16.2 us
    ppermute x9, starting transfers between devices, far(): return lax.ppermute(value, 'row', [(k, k ^ 4 * u) for k in range(devices)])  13.2 us
    ppermute x10, starting transfers between devices, near(): return lax.ppermute(value, 'row', [(k, k ^ t) for k in range(devices)])  7.75 us
    ppermute x9, waiting for transfers between devices, far(): return lax.ppermute(value, 'row', [(k, k ^ 4 * u) for k in range(devices)])  7.36 us
    ppermute x10, waiting for transfers between devices, near(): return lax.ppermute(value, 'row', [(k, k ^ t) for k in range(devices)])  5.37 us
  transfers between devices with their start and end apart: 19, of which 8 were waited for; matrix products, arithmetic and copies ran while one was open for 0% of the time, Pallas kernels for 14%

profile of v2, /device:TPU:0, one launch (start us, length us, event | category | flops | bytes accessed | tf_op | source)
XLA Modules:
  0.0 50.7 jit_solution(7927698552318272310)
XLA Ops:
  0.7 2.3 %shard_map.129 = (bf16[336,128]{1,0:T(8,128)(2,1)S(1)}, bf16[336,128]{1,0:T(8,128)(2,1)S(1)}, bf16[336,128]{1,0:T(8,128)(2,1)S(1)}, bf16[336,128]{1,0:T(8,128)(2...) custom-call(bf16[80,8,256]{2,1,0:T(8,128)(2,1)} %x_hbm.1, ...), custom_call_target="tpu_custom_call" | custom-call | flops 1000000000 | bytes 2000000 | tf_op jit(solution)/shard_map/pallas_call | solution.py:494
  3.0 0.5 %collective-permute-start = (bf16[336,128]{1,0:T(8,128)(2,1)S(1)}, bf16[336,128]{1,0:T(8,128)(2,1)S(1)}, u32[]{:S(2)}, u32[]{:S(2)}) collective-permute-start(bf16[336,128]{1,0:T(8,128)(2,1)S(1)} %get-tuple-element.51), channel_id=1, source_target_pairs={{0,1},{1,0},{2,3},{3,2},{4,5},{5,4},{6,7},{7,6},{8,9},{9,8},{10,11... | collective-permute-start | bytes 258056 | tf_op jit(solution)/shard_map/ppermute | solution.py:516
  3.5 2.6 %collective-permute-start.1 = (bf16[336,128]{1,0:T(8,128)(2,1)S(1)}, bf16[336,128]{1,0:T(8,128)(2,1)S(1)}, u32[]{:S(2)}, u32[]{:S(2)}) collective-permute-start(bf16[336,128]{1,0:T(8,128)(2,1)S(1)} %get-tuple-element.52), channel_id=1, source_target_pairs={{0,2},{1,3},{2,0},{3,1},{4,6},{5,7},{6,4},{7,5},{8,10},{9,11},{10,... | collective-permute-start | bytes 258056 | tf_op jit(solution)/shard_map/ppermute | solution.py:516
  6.0 0.1 collective-permute-start.2
  6.1 3.8 %collective-permute-start.5 = (bf16[80,128]{1,0:T(8,128)(2,1)S(1)}, bf16[80,128]{1,0:T(8,128)(2,1)S(1)}, u32[]{:S(2)}, u32[]{:S(2)}) collective-permute-start(bf16[80,128]{1,0:T(8,128)(2,1)S(1)} %get-tuple-element.57.refs_6_), channel_id=1, source_target_pairs={{0,12},{1,13},{2,14},{3,15},{4,8},{5,9},{6,10},{7,11},{8,4},{9,5},... | collective-permute-start | bytes 61448 | tf_op jit(solution)/shard_map/ppermute | solution.py:519
  10.0 0.6 %collective-permute-start.3 = (bf16[80,128]{1,0:T(8,128)(2,1)S(1)}, bf16[80,128]{1,0:T(8,128)(2,1)S(1)}, u32[]{:S(2)}, u32[]{:S(2)}) collective-permute-start(bf16[80,128]{1,0:T(8,128)(2,1)S(1)} %get-tuple-element.57.refs_6_), channel_id=1, source_target_pairs={{0,4},{1,5},{2,6},{3,7},{4,0},{5,1},{6,2},{7,3},{8,12},{9,13},{10,... | collective-permute-start | bytes 61448 | tf_op jit(solution)/shard_map/ppermute | solution.py:519
  10.5 0.3 collective-permute-done.2.refs_7_.refs_5_
  10.8 3.4 %shard_map.130 = (bf16[1024,128]{1,0:T(8,128)(2,1)S(1)}, bf16[1024,1024]{1,0:T(8,128)(2,1)S(1)}, bf16[128,1024]{1,0:T(8,128)(2,1)S(1)}) custom-call(s32[12]{0:T(128)S(1)} %copy-done.3, s32[12]{0:T(128)S(1)} %copy-done.4, bf16[1024,128]{1,0:T(8,128)(2,1)S(1)} %get-tuple-element.48.refs_2_, bf16[512,512]{1,0:T(8,128)(2,1)S(1)} %get-tuple-element.49.refs_3_.refs_4_, ...), custom_call_target="tpu_custom_call" | custom-call | flops 2000000000 | bytes 4000000 | tf_op jit(solution)/shard_map/pallas_call | solution.py:494
  14.3 0.4 collective-permute-done.4.refs_8_
  14.6 2.0 %shard_map.131 = (bf16[80,128]{1,0:T(8,128)(2,1)S(1)}, bf16[80,128]{1,0:T(8,128)(2,1)S(1)}, bf16[80,128]{1,0:T(8,128)(2,1)S(1)}, bf16[80,128]{1,0:T(8,128)(2,1)S...) custom-call(s32[12]{0:T(128)S(1)} %copy-done.3, ...), custom_call_target="tpu_custom_call" | custom-call | flops 2000000000 | bytes 4000000 | tf_op jit(solution)/shard_map/pallas_call | solution.py:494
  16.6 4.1 %shard_map.132 = (bf16[336,128]{1,0:T(8,128)(2,1)S(1)}, bf16[336,128]{1,0:T(8,128)(2,1)S(1)}, bf16[672,128]{1,0:T(8,128)(2,1)S(1)}, bf16[256,128]{1,0:T(8,128)(2...) custom-call(s32[12]{0:T(128)S(1)} %copy-done.3, s32[12]{0:T(128)S(1)} %copy-done.4, ...), custom_call_target="tpu_custom_call" | custom-call | flops 4000000000 | bytes 8000000 | tf_op jit(solution)/shard_map/pallas_call | solution.py:494
  20.7 0.1 collective-permute-start.6
  20.8 1.8 %collective-permute-start.15 = (bf16[512,128]{1,0:T(8,128)(2,1)S(1)}, bf16[512,128]{1,0:T(8,128)(2,1)S(1)}, u32[]{:S(2)}, u32[]{:S(2)}) collective-permute-start(bf16[512,128]{1,0:T(8,128)(2,1)S(1)} %get-tuple-element.79), channel_id=1, source_target_pairs={{0,2},{1,3},{2,0},{3,1},{4,6},{5,7},{6,4},{7,5},{8,10},{9,11},{10,... | collective-permute-start | bytes 393224 | tf_op jit(solution)/shard_map/ppermute | solution.py:516
  22.6 1.2 %collective-permute-start.7 = (bf16[336,128]{1,0:T(8,128)(2,1)S(1)}, bf16[336,128]{1,0:T(8,128)(2,1)S(1)}, u32[]{:S(2)}, u32[]{:S(2)}) collective-permute-start(bf16[336,128]{1,0:T(8,128)(2,1)S(1)} %get-tuple-element.68), channel_id=1, source_target_pairs={{0,2},{1,3},{2,0},{3,1},{4,6},{5,7},{6,4},{7,5},{8,10},{9,11},{10,... | collective-permute-start | bytes 258056 | tf_op jit(solution)/shard_map/ppermute | solution.py:516
  23.8 1.3 %collective-permute-start.8 = (bf16[80,128]{1,0:T(8,128)(2,1)S(1)}, bf16[80,128]{1,0:T(8,128)(2,1)S(1)}, u32[]{:S(2)}, u32[]{:S(2)}) collective-permute-start(bf16[80,128]{1,0:T(8,128)(2,1)S(1)} %get-tuple-element.70), channel_id=1, source_target_pairs={{0,4},{1,5},{2,6},{3,7},{4,0},{5,1},{6,2},{7,3},{8,12},{9,13},{10,... | collective-permute-start | bytes 61448 | tf_op jit(solution)/shard_map/ppermute | solution.py:519
  25.1 2.8 %collective-permute-start.9 = (bf16[80,128]{1,0:T(8,128)(2,1)S(1)}, bf16[80,128]{1,0:T(8,128)(2,1)S(1)}, u32[]{:S(2)}, u32[]{:S(2)}) collective-permute-start(bf16[80,128]{1,0:T(8,128)(2,1)S(1)} %get-tuple-element.71), channel_id=1, source_target_pairs={{0,8},{1,9},{2,10},{3,11},{4,12},{5,13},{6,14},{7,15},{8,0},{9,1},... | collective-permute-start | bytes 61448 | tf_op jit(solution)/shard_map/ppermute | solution.py:519
  27.9 0.3 collective-permute-start.10
  28.2 0.5 collective-permute-start.16
  28.7 1.1 %collective-permute-done.9.refs_8_ = bf16[80,128]{1,0:T(8,128)(2,1)S(1)} collective-permute-done((bf16[80,128]{1,0:T(8,128)(2,1)S(1)}, bf16[80,128]{1,0:T(8,128)(2,1)S(1)}, u32[]{:S(2)}, u32[]{:S(2)}) %collective-permute-start.9) | collective-permute-done | bytes 20512 | tf_op jit(solution)/shard_map/ppermute | solution.py:519
  29.8 3.6 %collective-permute-done.10.refs_9_ = bf16[80,128]{1,0:T(8,128)(2,1)S(1)} collective-permute-done((bf16[80,128]{1,0:T(8,128)(2,1)S(1)}, bf16[80,128]{1,0:T(8,128)(2,1)S(1)}, u32[]{:S(2)}, u32[]{:S(2)}) %collective-permute-start.10) | collective-permute-done | bytes 20512 | tf_op jit(solution)/shard_map/ppermute | solution.py:519
  33.5 1.3 %shard_map.134 = (bf16[640,64]{1,0:T(8,128)(2,1)S(1)}, bf16[384,128]{1,0:T(8,128)(2,1)S(1)}) custom-call(s32[12]{0:T(128)S(1)} %copy-done.3, s32[12]{0:T(128)S(1)} %copy-done.4, bf16[512,512]{1,0:T(8,128)(2,1)S(1)} %get-tuple-element.46.refs_2_, bf16[640,256]{1,0:T(8,128)(2,1)S(1)} %get-tuple-element.47.refs_3_, f32[336,128]{1,0:T(8,128)S(1)} %get-tuple-element.67.refs_4_, ...), custom_call_target="tpu_custom_call" | custom-call | flops 1000000000 | bytes 2000000 | tf_op jit(solution)/shard_map/pallas_call | solution.py:494
  34.8 0.4 collective-permute-start.13
  35.2 4.1 %collective-permute-start.11 = (bf16[384,128]{1,0:T(8,128)(2,1)S(1)}, bf16[384,128]{1,0:T(8,128)(2,1)S(1)}, u32[]{:S(2)}, u32[]{:S(2)}) collective-permute-start(bf16[384,128]{1,0:T(8,128)(2,1)S(1)} %get-tuple-element.82.refs_0_), channel_id=1, source_target_pairs={{0,4},{1,5},{2,6},{3,7},{4,0},{5,1},{6,2},{7,3},{8,12},{9,13},{10,... | collective-permute-start | bytes 294920 | tf_op jit(solution)/shard_map/ppermute | solution.py:519
  39.2 1.1 %shard_map.135 = bf16[80,8,256]{2,1,0:T(8,128)(2,1)} custom-call(bf16[640,64]{1,0:T(8,128)(2,1)S(1)} %get-tuple-element.74.pg_ref, bf16[64,256]{1,0:T(8,128)(2,1)S(1)} %bitcast.7, f32[1,256]{1,0:T(1,128)S(1)} %bitcast.9, f32[640,256]{1,0:T(8,128)S(1)} %get-tuple-element.75.hat_ref, f32[640,128]{1,0:T(8,128)S(1)} %get-tuple-element.76.rstd_ref), custom_call_target="tpu_custom_call" | custom-call | flops 1000000000 | bytes 2000000 | tf_op jit(solution)/shard_map/pallas_call | solution.py:494
  40.4 1.0 %shard_map.136 = bf16[8,128,128]{2,1,0:T(8,128)(2,1)} custom-call(bf16[256,128]{1,0:T(8,128)(2,1)S(1)} %get-tuple-element.77.refs_0_, bf16[256,128]{1,0:T(8,128)(2,1)S(1)} %collective-permute-done.14.refs_1_, bf16[512,128]{1,0:T(8,128)(2,1)S(1)} %collective-permute-done.15.refs_2_, bf16[512,128]{1,0:T(8,128)(2,1)S(1)} %collective-permute-done.16.refs_3_), custom_call_target="tpu_custom_call" | custom-call | flops 1000000000 | bytes 2000000 | tf_op jit(solution)/shard_map/pallas_call | solution.py:494
  41.4 0.7 %collective-permute-done.13.refs_3_ = bf16[384,128]{1,0:T(8,128)(2,1)S(1)} collective-permute-done((bf16[384,128]{1,0:T(8,128)(2,1)S(1)}, bf16[384,128]{1,0:T(8,128)(2,1)S(1)}, u32[]{:S(2)}, u32[]{:S(2)}) %collective-permute-start.13) | collective-permute-done | bytes 98336 | tf_op jit(solution)/shard_map/ppermute | solution.py:519
  42.1 1.6 %collective-permute-done.12.refs_2_ = bf16[384,128]{1,0:T(8,128)(2,1)S(1)} collective-permute-done((bf16[384,128]{1,0:T(8,128)(2,1)S(1)}, bf16[384,128]{1,0:T(8,128)(2,1)S(1)}, u32[]{:S(2)}, u32[]{:S(2)}) %collective-permute-start.12) | collective-permute-done | bytes 98336 | tf_op jit(solution)/shard_map/ppermute | solution.py:519
  43.7 1.0 %collective-permute-start.17 = (bf16[384,128]{1,0:T(8,128)(2,1)S(1)}, bf16[384,128]{1,0:T(8,128)(2,1)S(1)}, u32[]{:S(2)}, u32[]{:S(2)}) collective-permute-start(bf16[384,128]{1,0:T(8,128)(2,1)S(1)} %shard_map.137.own_ref), channel_id=1, source_target_pairs={{0,2},{1,3},{2,0},{3,1},{4,6},{5,7},{6,4},{7,5},{8,10},{9,11},{10,... | collective-permute-start | bytes 294920 | tf_op jit(solution)/shard_map/ppermute | solution.py:516
  44.7 3.7 %collective-permute-done.17.cross_ref = bf16[384,128]{1,0:T(8,128)(2,1)S(1)} collective-permute-done((bf16[384,128]{1,0:T(8,128)(2,1)S(1)}, bf16[384,128]{1,0:T(8,128)(2,1)S(1)}, u32[]{:S(2)}, u32[]{:S(2)}) %collective-permute-start.17) | collective-permute-done | bytes 98336 | tf_op jit(solution)/shard_map/ppermute | solution.py:516
  48.4 0.1 collective-permute-start.18
  48.5 1.4 %collective-permute-done.18.core_ref = bf16[640,128]{1,0:T(8,128)(2,1)S(1)} collective-permute-done((bf16[640,128]{1,0:T(8,128)(2,1)S(1)}, bf16[640,128]{1,0:T(8,128)(2,1)S(1)}, u32[]{:S(2)}, u32[]{:S(2)}) %collective-permute-start.18) | collective-permute-done | bytes 163872 | tf_op jit(solution)/shard_map/ppermute | solution.py:516
  49.9 0.8 %shard_map.139 = (f32[1024,128]{1,0:T(8,128)}, f32[64,256]{1,0:T(8,128)}) custom-call(bf16[640,128]{1,0:T(8,128)(2,1)S(1)} %shard_map.138.mine_ref, bf16[640,128]{1,0:T(8,128)(2,1)S(1)} %collective-permute-done.18.core_ref), custom_call_target="tpu_custom_call" | custom-call | flops 100000000 | bytes 200000 | tf_op jit(solution)/shard_map/pallas_call | solution.py:494
  (27 shorter events, 0.2 us)
Async XLA Ops:
  0.6 10.2 %copy-start.3 = (s32[12]{0:T(128)S(1)}, s32[12]{0:T(128)}, u32[]{:S(2)}) copy-start(s32[12]{0:T(128)} %refs_0_.7) | copy-start | bytes 148
  0.6 10.2 %copy-start.4 = (s32[12]{0:T(128)S(1)}, s32[12]{0:T(128)}, u32[]{:S(2)}) copy-start(s32[12]{0:T(128)} %refs_1_.5) | copy-start | bytes 148
  3.0 7.0 %collective-permute-start = (bf16[336,128]{1,0:T(8,128)(2,1)S(1)}, bf16[336,128]{1,0:T(8,128)(2,1)S(1)}, u32[]{:S(2)}, u32[]{:S(2)}) collective-permute-start(bf16[336,128]{1,0:T(8,128)(2,1)S(1)} %get-tuple-element.51), channel_id=1, source_target_pairs={{0,1},{1,0},{2,3},{3,2},{4,5},{5,4},{6,7},{7,6},{8,9},{9,8},{10,11... | collective-permute-start | bytes 258056 | tf_op jit(solution)/shard_map/ppermute | solution.py:516
  3.5 7.0 %collective-permute-start.1 = (bf16[336,128]{1,0:T(8,128)(2,1)S(1)}, bf16[336,128]{1,0:T(8,128)(2,1)S(1)}, u32[]{:S(2)}, u32[]{:S(2)}) collective-permute-start(bf16[336,128]{1,0:T(8,128)(2,1)S(1)} %get-tuple-element.52), channel_id=1, source_target_pairs={{0,2},{1,3},{2,0},{3,1},{4,6},{5,7},{6,4},{7,5},{8,10},{9,11},{10,... | collective-permute-start | bytes 258056 | tf_op jit(solution)/shard_map/ppermute | solution.py:516
  6.0 4.8 %collective-permute-start.2 = (bf16[336,128]{1,0:T(8,128)(2,1)S(1)}, bf16[336,128]{1,0:T(8,128)(2,1)S(1)}, u32[]{:S(2)}, u32[]{:S(2)}) collective-permute-start(bf16[336,128]{1,0:T(8,128)(2,1)S(1)} %get-tuple-element.53), channel_id=1, source_target_pairs={{0,3},{1,2},{2,1},{3,0},{4,7},{5,6},{6,5},{7,4},{8,11},{9,10},{10,... | collective-permute-start | bytes 258056 | tf_op jit(solution)/shard_map/ppermute | solution.py:516
  6.1 8.1 %collective-permute-start.5 = (bf16[80,128]{1,0:T(8,128)(2,1)S(1)}, bf16[80,128]{1,0:T(8,128)(2,1)S(1)}, u32[]{:S(2)}, u32[]{:S(2)}) collective-permute-start(bf16[80,128]{1,0:T(8,128)(2,1)S(1)} %get-tuple-element.57.refs_6_), channel_id=1, source_target_pairs={{0,12},{1,13},{2,14},{3,15},{4,8},{5,9},{6,10},{7,11},{8,4},{9,5},... | collective-permute-start | bytes 61448 | tf_op jit(solution)/shard_map/ppermute | solution.py:519
  9.9 4.7 %collective-permute-start.4 = (bf16[80,128]{1,0:T(8,128)(2,1)S(1)}, bf16[80,128]{1,0:T(8,128)(2,1)S(1)}, u32[]{:S(2)}, u32[]{:S(2)}) collective-permute-start(bf16[80,128]{1,0:T(8,128)(2,1)S(1)} %get-tuple-element.57.refs_6_), channel_id=1, source_target_pairs={{0,8},{1,9},{2,10},{3,11},{4,12},{5,13},{6,14},{7,15},{8,0},{9,1},... | collective-permute-start | bytes 61448 | tf_op jit(solution)/shard_map/ppermute | solution.py:519
  10.0 4.7 %collective-permute-start.3 = (bf16[80,128]{1,0:T(8,128)(2,1)S(1)}, bf16[80,128]{1,0:T(8,128)(2,1)S(1)}, u32[]{:S(2)}, u32[]{:S(2)}) collective-permute-start(bf16[80,128]{1,0:T(8,128)(2,1)S(1)} %get-tuple-element.57.refs_6_), channel_id=1, source_target_pairs={{0,4},{1,5},{2,6},{3,7},{4,0},{5,1},{6,2},{7,3},{8,12},{9,13},{10,... | collective-permute-start | bytes 61448 | tf_op jit(solution)/shard_map/ppermute | solution.py:519
  14.6 2.0 %copy-start.2 = (f32[128]{0:T(128)S(1)}, f32[128]{0:T(128)}, u32[]{:S(2)}) copy-start(f32[128]{0:T(128)} %param.16) | copy-start | bytes 1540
  20.7 18.5 %copy-start = (bf16[256,64]{0,1:T(8,128)(2,1)S(1)}, bf16[256,64]{0,1:T(8,128)(2,1)}, u32[]{:S(2)}) copy-start(bf16[256,64]{0,1:T(8,128)(2,1)} %param.13) | copy-start | bytes 98308
  20.7 18.5 %copy-start.1 = (f32[256]{0:T(256)S(1)}, f32[256]{0:T(256)}, u32[]{:S(2)}) copy-start(f32[256]{0:T(256)} %param.11) | copy-start | bytes 3076
  20.7 1.9 %collective-permute-start.6 = (bf16[672,128]{1,0:T(8,128)(2,1)S(1)}, bf16[672,128]{1,0:T(8,128)(2,1)S(1)}, u32[]{:S(2)}, u32[]{:S(2)}) collective-permute-start(bf16[672,128]{1,0:T(8,128)(2,1)S(1)} %get-tuple-element.66), channel_id=1, source_target_pairs={{0,1},{1,0},{2,3},{3,2},{4,5},{5,4},{6,7},{7,6},{8,9},{9,8},{10,11... | collective-permute-start | bytes 516104 | tf_op jit(solution)/shard_map/ppermute | solution.py:516
  20.8 7.4 %collective-permute-start.15 = (bf16[512,128]{1,0:T(8,128)(2,1)S(1)}, bf16[512,128]{1,0:T(8,128)(2,1)S(1)}, u32[]{:S(2)}, u32[]{:S(2)}) collective-permute-start(bf16[512,128]{1,0:T(8,128)(2,1)S(1)} %get-tuple-element.79), channel_id=1, source_target_pairs={{0,2},{1,3},{2,0},{3,1},{4,6},{5,7},{6,4},{7,5},{8,10},{9,11},{10,... | collective-permute-start | bytes 393224 | tf_op jit(solution)/shard_map/ppermute | solution.py:516
  22.6 10.8 %collective-permute-start.7 = (bf16[336,128]{1,0:T(8,128)(2,1)S(1)}, bf16[336,128]{1,0:T(8,128)(2,1)S(1)}, u32[]{:S(2)}, u32[]{:S(2)}) collective-permute-start(bf16[336,128]{1,0:T(8,128)(2,1)S(1)} %get-tuple-element.68), channel_id=1, source_target_pairs={{0,2},{1,3},{2,0},{3,1},{4,6},{5,7},{6,4},{7,5},{8,10},{9,11},{10,... | collective-permute-start | bytes 258056 | tf_op jit(solution)/shard_map/ppermute | solution.py:516
  23.8 4.4 %collective-permute-start.8 = (bf16[80,128]{1,0:T(8,128)(2,1)S(1)}, bf16[80,128]{1,0:T(8,128)(2,1)S(1)}, u32[]{:S(2)}, u32[]{:S(2)}) collective-permute-start(bf16[80,128]{1,0:T(8,128)(2,1)S(1)} %get-tuple-element.70), channel_id=1, source_target_pairs={{0,4},{1,5},{2,6},{3,7},{4,0},{5,1},{6,2},{7,3},{8,12},{9,13},{10,... | collective-permute-start | bytes 61448 | tf_op jit(solution)/shard_map/ppermute | solution.py:519
  25.1 4.7 %collective-permute-start.9 = (bf16[80,128]{1,0:T(8,128)(2,1)S(1)}, bf16[80,128]{1,0:T(8,128)(2,1)S(1)}, u32[]{:S(2)}, u32[]{:S(2)}) collective-permute-start(bf16[80,128]{1,0:T(8,128)(2,1)S(1)} %get-tuple-element.71), channel_id=1, source_target_pairs={{0,8},{1,9},{2,10},{3,11},{4,12},{5,13},{6,14},{7,15},{8,0},{9,1},... | collective-permute-start | bytes 61448 | tf_op jit(solution)/shard_map/ppermute | solution.py:519
  27.9 5.6 %collective-permute-start.10 = (bf16[80,128]{1,0:T(8,128)(2,1)S(1)}, bf16[80,128]{1,0:T(8,128)(2,1)S(1)}, u32[]{:S(2)}, u32[]{:S(2)}) collective-permute-start(bf16[80,128]{1,0:T(8,128)(2,1)S(1)} %get-tuple-element.72), channel_id=1, source_target_pairs={{0,12},{1,13},{2,14},{3,15},{4,8},{5,9},{6,10},{7,11},{8,4},{9,5},... | collective-permute-start | bytes 61448 | tf_op jit(solution)/shard_map/ppermute | solution.py:519
  28.2 12.2 %collective-permute-start.14 = (bf16[256,128]{1,0:T(8,128)(2,1)S(1)}, bf16[256,128]{1,0:T(8,128)(2,1)S(1)}, u32[]{:S(2)}, u32[]{:S(2)}) collective-permute-start(bf16[256,128]{1,0:T(8,128)(2,1)S(1)} %get-tuple-element.78), channel_id=1, source_target_pairs={{0,1},{1,0},{2,3},{3,2},{4,5},{5,4},{6,7},{7,6},{8,9},{9,8},{10,11... | collective-permute-start | bytes 196616 | tf_op jit(solution)/shard_map/ppermute | solution.py:516
  28.2 12.2 %collective-permute-start.16 = (bf16[512,128]{1,0:T(8,128)(2,1)S(1)}, bf16[512,128]{1,0:T(8,128)(2,1)S(1)}, u32[]{:S(2)}, u32[]{:S(2)}) collective-permute-start(bf16[512,128]{1,0:T(8,128)(2,1)S(1)} %collective-permute-done.15.refs_2_), channel_id=1, source_target_pairs={{0,1},{1,0},{2,3},{3,2},{4,5},{5,4},{6,7},{7,6},{8,9},{9,8},{10,11... | collective-permute-start | bytes 393224 | tf_op jit(solution)/shard_map/ppermute | solution.py:516
  34.8 7.3 %collective-permute-start.13 = (bf16[384,128]{1,0:T(8,128)(2,1)S(1)}, bf16[384,128]{1,0:T(8,128)(2,1)S(1)}, u32[]{:S(2)}, u32[]{:S(2)}) collective-permute-start(bf16[384,128]{1,0:T(8,128)(2,1)S(1)} %get-tuple-element.82.refs_0_), channel_id=1, source_target_pairs={{0,12},{1,13},{2,14},{3,15},{4,8},{5,9},{6,10},{7,11},{8,4},{9,5},... | collective-permute-start | bytes 294920 | tf_op jit(solution)/shard_map/ppermute | solution.py:519
  35.2 8.5 %collective-permute-start.12 = (bf16[384,128]{1,0:T(8,128)(2,1)S(1)}, bf16[384,128]{1,0:T(8,128)(2,1)S(1)}, u32[]{:S(2)}, u32[]{:S(2)}) collective-permute-start(bf16[384,128]{1,0:T(8,128)(2,1)S(1)} %get-tuple-element.82.refs_0_), channel_id=1, source_target_pairs={{0,8},{1,9},{2,10},{3,11},{4,12},{5,13},{6,14},{7,15},{8,0},{9,1},... | collective-permute-start | bytes 294920 | tf_op jit(solution)/shard_map/ppermute | solution.py:519
  35.2 8.5 %collective-permute-start.11 = (bf16[384,128]{1,0:T(8,128)(2,1)S(1)}, bf16[384,128]{1,0:T(8,128)(2,1)S(1)}, u32[]{:S(2)}, u32[]{:S(2)}) collective-permute-start(bf16[384,128]{1,0:T(8,128)(2,1)S(1)} %get-tuple-element.82.refs_0_), channel_id=1, source_target_pairs={{0,4},{1,5},{2,6},{3,7},{4,0},{5,1},{6,2},{7,3},{8,12},{9,13},{10,... | collective-permute-start | bytes 294920 | tf_op jit(solution)/shard_map/ppermute | solution.py:519
  43.7 4.7 %collective-permute-start.17 = (bf16[384,128]{1,0:T(8,128)(2,1)S(1)}, bf16[384,128]{1,0:T(8,128)(2,1)S(1)}, u32[]{:S(2)}, u32[]{:S(2)}) collective-permute-start(bf16[384,128]{1,0:T(8,128)(2,1)S(1)} %shard_map.137.own_ref), channel_id=1, source_target_pairs={{0,2},{1,3},{2,0},{3,1},{4,6},{5,7},{6,4},{7,5},{8,10},{9,11},{10,... | collective-permute-start | bytes 294920 | tf_op jit(solution)/shard_map/ppermute | solution.py:516
  48.4 1.5 %collective-permute-start.18 = (bf16[640,128]{1,0:T(8,128)(2,1)S(1)}, bf16[640,128]{1,0:T(8,128)(2,1)S(1)}, u32[]{:S(2)}, u32[]{:S(2)}) collective-permute-start(bf16[640,128]{1,0:T(8,128)(2,1)S(1)} %shard_map.138.mine_ref), channel_id=1, source_target_pairs={{0,1},{1,0},{2,3},{3,2},{4,5},{5,4},{6,7},{7,6},{8,9},{9,8},{10,11... | collective-permute-start | bytes 491528 | tf_op jit(solution)/shard_map/ppermute | solution.py:516

commit v3 on v2

--- a/solution.py
+++ b/solution.py
@@ -126,6 +126,24 @@
     q, m = row >> 7, (row >> 3) & 3
     target = (m << 7) | (row & 0x67) | (q << 3)
     return jnp.where(col == target, 1.0, 0.0).astype(BF16)
+
+
+def swap_blocks(o, swap):
+    blocks = o.shape[1] // 128
+    wide = [
+        jnp.concatenate(
+            [
+                o[(g * 4 + q) * 32 : (g * 4 + q + 1) * 32, blk * 128 : blk * 128 + 128]
+                for q in range(4)
+            ],
+            axis=1,
+        )
+        for blk in range(blocks)
+        for g in range(8)
+    ]
+    return jnp.dot(
+        jnp.concatenate(wide, axis=0), swap, preferred_element_type=F32
+    ).astype(BF16)
 
 
 def fetch(pairs, sems):
@@ -209,12 +227,19 @@
 
 
 def adjoint_kernel(
-    chunks, len_ref, hom_ref, final_ref, swap_ref, m0, m1, m2, m3, s_ref, og_ref, ft_ref
+    chunks, len_ref, hom_ref, final_ref, swap_ref, m0, m1, m2, m3,
+    s_ref, og_ref, ft_ref, lx_ref,
 ):
     messages = (m0, m1, m2, m3)
     a, b = place()
     ends = bounds_of(len_ref)
     swap = swap_ref[...]
+    bottom = chunks * 256
+    lx_ref[...] = spread_rows(
+        left_lanes([m[bottom : bottom + PACKED, :] for m in messages]),
+        left_chain(a, b, ends),
+        len_ref.shape[0],
+    ).astype(BF16)
     low = lax.broadcasted_iota(jnp.int32, (32, 128), 0)
     chain_i, inv_same = [], []
     for t in range(QUAD):
@@ -238,27 +263,20 @@
         s = jnp.concatenate(blocks, axis=0)
         s_ref[pl.ds(pl.multiple_of(g * 1024, 1024), 1024), :] = s.astype(BF16)
         st = s.T.astype(BF16)
-        for cb in range(8):
+        for half in range(2):
             og = jnp.dot(
-                final[cb * 128 : cb * 128 + 128, :], st, preferred_element_type=F32
+                final, st[:, half * 512 : half * 512 + 512], preferred_element_type=F32
             ).astype(BF16)
-            wide = jnp.concatenate(
-                [
-                    jnp.concatenate(
-                        [og[q * 32 : q * 32 + 32, jg * 128 : jg * 128 + 128] for q in range(4)],
-                        axis=1,
-                    )
-                    for jg in range(8)
-                ],
-                axis=0,
-            )
-            moved = jnp.dot(wide, swap, preferred_element_type=F32).astype(BF16)
-            for jg in range(8):
+            moved = swap_blocks(og, swap)
+            for jg in range(4):
                 for jl in range(4):
-                    top = pl.ds(pl.multiple_of(g * 1024 + (jg * 4 + jl) * 32, 32), 32)
-                    og_ref[top, cb * 128 : cb * 128 + 128] = moved[
-                        jg * 32 : jg * 32 + 32, jl * 128 : jl * 128 + 128
-                    ]
+                    row = ((half * 4 + jg) * 4 + jl) * 32
+                    at = pl.ds(pl.multiple_of(g * 1024 + row, 32), 32)
+                    for cb in range(8):
+                        top = (jg * 8 + cb) * 32
+                        og_ref[at, cb * 128 : cb * 128 + 128] = moved[
+                            top : top + 32, jl * 128 : jl * 128 + 128
+                        ]
         return 0
 
     lax.fori_loop(0, chunks, step, 0, unroll=chunks == 1)
@@ -277,20 +295,16 @@
 
 
 def grad_kernel(
-    chunks, len_ref, og_ref, m0, m1, m2, m3, r0, r1, r2, r3,
-    l0, l1, l2, l3, g0, g1, g2, g3, lx_ref, rt_ref, lg_acc,
+    chunks, len_ref, og_ref, lx_ref, r3, r2, r1, r0,
+    l0, l1, l2, l3, g0, g1, g2, g3, rt_ref, lg_acc,
 ):
-    messages, rights = (m0, m1, m2, m3), (r0, r1, r2, r3)
+    rights = (r0, r1, r2, r3)
     lefts, grads = (l0, l1, l2, l3), (g0, g1, g2, g3)
     chains = len_ref.shape[0]
     a, b = place()
     ends = bounds_of(len_ref)
     chain_l = left_chain(a, b, ends)
-    top = chunks * 256
-    lx = spread_rows(
-        left_lanes([m[top : top + PACKED, :] for m in messages]), chain_l, chains
-    ).astype(BF16)
-    lx_ref[...] = lx
+    lx = lx_ref[...]
     lg_acc[...] = jnp.zeros(lg_acc.shape, F32)
 
     def step(g, _):
@@ -338,26 +352,20 @@
     other_inv = 1.0 / jnp.full((8, 128), PAIRED + 0.001, F32)
 
     def step(g, _):
-        for jg in range(8):
-            at = pl.ds(pl.multiple_of(g * 1024 + jg * 128, 128), 128)
-            o = jnp.dot(rt_ref[at, :], lx, preferred_element_type=F32).astype(BF16)
-            wide = jnp.concatenate(
-                [
-                    jnp.concatenate(
-                        [o[q * 32 : q * 32 + 32, cb * 128 : cb * 128 + 128] for q in range(4)],
-                        axis=1,
-                    )
-                    for cb in range(8)
-                ],
-                axis=0,
-            )
-            moved = jnp.dot(wide, swap, preferred_element_type=F32).astype(BF16)
-            for cb in range(8):
+        rt = rt_ref[pl.ds(pl.multiple_of(g * 1024, 1024), 1024), :]
+        for half in range(2):
+            o = jnp.dot(
+                rt, lx[:, half * 512 : half * 512 + 512], preferred_element_type=F32
+            ).astype(BF16)
+            moved = swap_blocks(o, swap)
+            for cb in range(4):
                 for cl in range(4):
-                    row = (cb * 4 + cl) * 32
-                    n_buf[row : row + 32, jg * 128 : jg * 128 + 128] = moved[
-                        cb * 32 : cb * 32 + 32, cl * 128 : cl * 128 + 128
-                    ]
+                    row = ((half * 4 + cb) * 4 + cl) * 32
+                    for jg in range(8):
+                        top = (cb * 8 + jg) * 32
+                        n_buf[row : row + 32, jg * 128 : jg * 128 + 128] = moved[
+                            top : top + 32, cl * 128 : cl * 128 + 128
+                        ]
         n = n_buf[...]
         s = s_ref[pl.ds(pl.multiple_of(g * 1024, 1024), 1024), :]
         w_acc[...] += jnp.dot(n, s, preferred_element_type=F32)
@@ -404,7 +412,6 @@
     chains = len_ref.shape[0]
     depth8 = pg_ref.shape[0]
     a, b = place()
-    out_ref[0:256, :] = total([q[0:256, :] for q in quads]).astype(BF16)
     lg = total([q[256:, :] for q in quads])
     rg = total([r[...] for r in rgs])
     wide = jnp.concatenate([blk for g in (lg, rg) for blk in unpack(g)], axis=1)
@@ -428,7 +435,16 @@
     pg = full[0:depth8, :]
     pg_ref[...] = pg.astype(BF16)
     fm = jnp.dot(pg.T.astype(BF16), norm_ref[...], preferred_element_type=F32)
-    out_ref[256:384, :] = jnp.concatenate([fm[:, 0:128], fm[:, 128:256]], axis=0).astype(BF16)
+    out_ref[...] = jnp.concatenate([fm[:, 0:128], fm[:, 128:256]], axis=0).astype(BF16)
+
+
+def fold_kernel(mine_ref, theirs_ref, out_ref):
+    out_ref[...] = total([mine_ref[0:256, :], theirs_ref[0:256, :]]).astype(BF16)
+
+
+def join_kernel(w0, w1, fm_ref, out_ref):
+    out_ref[0:256, :] = total([w0[...], w1[...]]).astype(BF16)
+    out_ref[256:384, :] = fm_ref[...]
 
 
 def align_kernel(pg_ref, mat_ref, scale_ref, hat_ref, rstd_ref, out_ref):
@@ -461,8 +477,10 @@
     out_ref[...] = work[...].reshape(out_ref.shape).astype(BF16)
 
 
-def merge_kernel(*refs):
-    refs[-1][...] = total([r[...] for r in refs[:-1]]).astype(BF16)
+def merge_kernel(far_half, *refs):
+    out_ref, fms = refs[-1], refs[:-1]
+    out_ref[0:256, :] = total([fms[0][0:256, :], fms[far_half][0:256, :]]).astype(BF16)
+    out_ref[256:384, :] = total([f[f.shape[0] - 128 :, :] for f in fms]).astype(BF16)
 
 
 def relay_kernel(own_ref, cross_ref, out_ref):
@@ -564,12 +582,13 @@
     messages = quad(messages)
     rights = by_slot([right] + [far(right, u) for u in range(1, groups)])
 
-    s, og, final_t = call(
+    s, og, final_t, lx = call(
         lambda *refs: adjoint_kernel(chunks, *refs),
         [
             sds((chunks * 1024, 128), BF16),
             sds((chunks * 1024, 1024), BF16),
             sds((128, 1024), BF16),
+            sds((128, 1024), BF16),
         ],
         [lengths, homologs, final, swap, *messages],
         in_specs=[SMEM] * 2 + [vmem()] * (2 + QUAD),
@@ -580,13 +599,13 @@
         lambda *refs: grad_kernel(chunks, *refs),
         [sds((PACKED, 128), BF16)] * QUAD
         + [sds((chunks * PACKED, 128), BF16)] * 4
-        + [sds((128, 1024), BF16), sds((chunks * 1024, 128), BF16)],
-        [lengths, og, *messages, *rights],
-        in_specs=[SMEM] + [vmem()] * (1 + 2 * QUAD),
+        + [sds((chunks * 1024, 128), BF16)],
+        [lengths, og, lx, *rights[::-1]],
+        in_specs=[SMEM] + [vmem()] * (2 + QUAD),
         scratch=[pltpu.VMEM((128, 1024), F32)],
         work=2 * 10**9,
     )
-    lgs, rgs, (lx, rt) = outs[0:4], list(outs[4:8]), outs[8:10]
+    lgs, rgs, rt = outs[0:4], list(outs[4:8]), outs[8]
     rgs = from_slot(rgs, PACKED)
     rgs = [rgs[0]] + [far(rgs[u], u) for u in range(1, groups)]
     own, cross, core, pair_own, pair_core, pair_cross = call(
@@ -609,9 +628,9 @@
     )
     quads = [mine, near(theirs, 2)]
 
-    pg, part = call(
+    pg, fm = call(
         lambda *refs: back_kernel(groups, *refs),
-        [sds((depth * BLOCK, 64), BF16), sds((384, 128), BF16)],
+        [sds((depth * BLOCK, 64), BF16), sds((128, 128), BF16)],
         [lengths, homologs, spread, normed, *quads, *rgs],
         in_specs=[SMEM] * 2 + [vmem()] * (4 + groups),
         scratch=[
@@ -620,7 +639,13 @@
         ],
         work=10**9,
     )
-    parts = [part] + [far(part, u) for u in range(1, groups)]
+    half = groups // 2
+    w = call(fold_kernel, sds((256, 128), BF16), quads, work=10**7)
+    steps = [1 << k for k in range(half.bit_length() - 1)]
+    for u in steps[:-1]:
+        w = call(fold_kernel, sds((256, 128), BF16), [w, far(w, u)], work=10**7)
+    part = call(join_kernel, sds((384, 128), BF16), [w, far(w, steps[-1]), fm], work=10**7)
+    parts = [part] + [far(part if u == half else fm, u) for u in range(1, groups)]
     pair_cross = near(pair_cross, 2)
     pairs = [pair_own, near(pair_core, 1), pair_cross, near(pair_cross, 1)]
     alignment_gradient = call(
@@ -639,7 +664,9 @@
     parts, alignment_gradient, pair_delta = lax.optimization_barrier(
         (parts, alignment_gradient, pair_delta)
     )
-    merged = call(merge_kernel, sds((384, 128), BF16), parts, work=10**7)
+    merged = call(
+        lambda *refs: merge_kernel(half, *refs), sds((384, 128), BF16), parts, work=10**7
+    )
     relay = call(relay_kernel, sds((640, 128), BF16), [merged, near(merged, 2)], work=10**7)
     w, fm = call(
         final_kernel,

time: 50.9 us -> 48.7 us (0.957)
  Pallas kernels: 16.2 us -> 14.9 us
  starting transfers between devices: 21 us -> 19.8 us
    pallas_call x11 -> x13, Pallas kernels: 16.2 us -> 14.9 us  [call(): pl.pallas_call(kernel, out_shape=outs, in_specs=in_specs if in_specs is n...]
    ppermute x10, waiting for transfers between devices: 5.37 us -> 6.35 us  [near(): return lax.ppermute(value, 'row', [(k, k ^ t) for k in range(devices)])]
    ppermute x9 -> x10, starting transfers between devices: 13.2 us -> 12.3 us  [far(): return lax.ppermute(value, 'row', [(k, k ^ 4 * u) for k in range(devices)])]
    ppermute x9 -> x10, waiting for transfers between devices: 7.36 us -> 6.75 us  [far(): return lax.ppermute(value, 'row', [(k, k ^ 4 * u) for k in range(devices)])]
  transfers between devices with their start and end apart: 19 -> 20, of which waited for: 8 -> 9; matrix products, arithmetic and copies ran while one was open for 0% -> 0% of each run, Pallas kernels for 14% -> 13%
where the time goes in v3:
time: 48.7 us; the launch traced here: 48.5 us
  starting transfers between devices  19.8 us (41%)
  Pallas kernels  14.9 us (31%)
  waiting for transfers between devices  13.1 us (27%)
  between operations  0.76 us (2%)
    pallas_call x13, Pallas kernels, call(): pl.pallas_call(kernel, out_shape=outs, in_specs=in_specs if in_specs is n...  14.9 us
    ppermute x10, starting transfers between devices, far(): return lax.ppermute(value, 'row', [(k, k ^ 4 * u) for k in range(devices)])  12.3 us
    ppermute x10, starting transfers between devices, near(): return lax.ppermute(value, 'row', [(k, k ^ t) for k in range(devices)])  7.49 us
    ppermute x10, waiting for transfers between devices, far(): return lax.ppermute(value, 'row', [(k, k ^ 4 * u) for k in range(devices)])  6.75 us
    ppermute x10, waiting for transfers between devices, near(): return lax.ppermute(value, 'row', [(k, k ^ t) for k in range(devices)])  6.35 us
  transfers between devices with their start and end apart: 20, of which 9 were waited for; matrix products, arithmetic and copies ran while one was open for 0% of the time, Pallas kernels for 13%

profile of v3, /device:TPU:0, one launch (start us, length us, event | category | flops | bytes accessed | tf_op | source)
XLA Modules:
  0.0 48.5 jit_solution(11674817549768408828)
XLA Ops:
  0.7 2.3 %shard_map.129 = (bf16[336,128]{1,0:T(8,128)(2,1)S(1)}, bf16[336,128]{1,0:T(8,128)(2,1)S(1)}, bf16[336,128]{1,0:T(8,128)(2,1)S(1)}, bf16[336,128]{1,0:T(8,128)(2...) custom-call(bf16[80,8,256]{2,1,0:T(8,128)(2,1)} %x_hbm.1, ...), custom_call_target="tpu_custom_call" | custom-call | flops 1000000000 | bytes 2000000 | tf_op jit(solution)/shard_map/pallas_call | solution.py:512
  3.0 0.5 %collective-permute-start = (bf16[336,128]{1,0:T(8,128)(2,1)S(1)}, bf16[336,128]{1,0:T(8,128)(2,1)S(1)}, u32[]{:S(2)}, u32[]{:S(2)}) collective-permute-start(bf16[336,128]{1,0:T(8,128)(2,1)S(1)} %get-tuple-element.49), channel_id=1, source_target_pairs={{0,1},{1,0},{2,3},{3,2},{4,5},{5,4},{6,7},{7,6},{8,9},{9,8},{10,11... | collective-permute-start | bytes 258056 | tf_op jit(solution)/shard_map/ppermute | solution.py:534
  3.5 2.6 %collective-permute-start.1 = (bf16[336,128]{1,0:T(8,128)(2,1)S(1)}, bf16[336,128]{1,0:T(8,128)(2,1)S(1)}, u32[]{:S(2)}, u32[]{:S(2)}) collective-permute-start(bf16[336,128]{1,0:T(8,128)(2,1)S(1)} %get-tuple-element.50), channel_id=1, source_target_pairs={{0,2},{1,3},{2,0},{3,1},{4,6},{5,7},{6,4},{7,5},{8,10},{9,11},{10,... | collective-permute-start | bytes 258056 | tf_op jit(solution)/shard_map/ppermute | solution.py:534
  6.1 3.8 %collective-permute-start.3 = (bf16[80,128]{1,0:T(8,128)(2,1)S(1)}, bf16[80,128]{1,0:T(8,128)(2,1)S(1)}, u32[]{:S(2)}, u32[]{:S(2)}) collective-permute-start(bf16[80,128]{1,0:T(8,128)(2,1)S(1)} %get-tuple-element.56.refs_6_), channel_id=1, source_target_pairs={{0,12},{1,13},{2,14},{3,15},{4,8},{5,9},{6,10},{7,11},{8,4},{9,5},... | collective-permute-start | bytes 61448 | tf_op jit(solution)/shard_map/ppermute | solution.py:537
  10.0 0.6 %collective-permute-start.5 = (bf16[80,128]{1,0:T(8,128)(2,1)S(1)}, bf16[80,128]{1,0:T(8,128)(2,1)S(1)}, u32[]{:S(2)}, u32[]{:S(2)}) collective-permute-start(bf16[80,128]{1,0:T(8,128)(2,1)S(1)} %get-tuple-element.56.refs_6_), channel_id=1, source_target_pairs={{0,4},{1,5},{2,6},{3,7},{4,0},{5,1},{6,2},{7,3},{8,12},{9,13},{10,... | collective-permute-start | bytes 61448 | tf_op jit(solution)/shard_map/ppermute | solution.py:537
  10.5 0.3 collective-permute-done.2.refs_7_
  10.8 2.8 %shard_map.130 = (bf16[1024,128]{1,0:T(8,128)(2,1)S(1)}, bf16[1024,1024]{1,0:T(8,128)(2,1)S(1)}, bf16[128,1024]{1,0:T(8,128)(2,1)S(1)}, bf16[128,1024]{1,0:T(8,128)(2,1)S(1)}) custom-call(s32[12]{0:T(128)S(1)} %copy-done.3, s32[12]{0:T(128)S(1)} %copy-done.4, bf16[1024,128]{1,0:T(8,128)(2,1)S(1)} %get-tuple-element.46.refs_2_, ...), custom_call_target="tpu_custom_call" | custom-call | flops 2000000000 | bytes 4000000 | tf_op jit(solution)/shard_map/pallas_call | solution.py:512
  13.6 1.0 %collective-permute-done.4.refs_4_ = bf16[80,128]{1,0:T(8,128)(2,1)S(1)} collective-permute-done((bf16[80,128]{1,0:T(8,128)(2,1)S(1)}, bf16[80,128]{1,0:T(8,128)(2,1)S(1)}, u32[]{:S(2)}, u32[]{:S(2)}) %collective-permute-start.4) | collective-permute-done | bytes 20512 | tf_op jit(solution)/shard_map/ppermute | solution.py:537
  14.6 1.8 %shard_map.131 = (bf16[80,128]{1,0:T(8,128)(2,1)S(1)}, bf16[80,128]{1,0:T(8,128)(2,1)S(1)}, bf16[80,128]{1,0:T(8,128)(2,1)S(1)}, bf16[80,128]{1,0:T(8,128)(2,1)S...) custom-call(s32[12]{0:T(128)S(1)} %copy-done.3, ...), custom_call_target="tpu_custom_call" | custom-call | flops 2000000000 | bytes 4000000 | tf_op jit(solution)/shard_map/pallas_call | solution.py:512
  16.5 3.5 %shard_map.132 = (bf16[336,128]{1,0:T(8,128)(2,1)S(1)}, bf16[336,128]{1,0:T(8,128)(2,1)S(1)}, bf16[672,128]{1,0:T(8,128)(2,1)S(1)}, bf16[256,128]{1,0:T(8,128)(2...) custom-call(s32[12]{0:T(128)S(1)} %copy-done.3, s32[12]{0:T(128)S(1)} %copy-done.4, ...), custom_call_target="tpu_custom_call" | custom-call | flops 4000000000 | bytes 8000000 | tf_op jit(solution)/shard_map/pallas_call | solution.py:512
  20.0 0.1 collective-permute-start.6
  20.0 1.6 %collective-permute-start.16 = (bf16[512,128]{1,0:T(8,128)(2,1)S(1)}, bf16[512,128]{1,0:T(8,128)(2,1)S(1)}, u32[]{:S(2)}, u32[]{:S(2)}) collective-permute-start(bf16[512,128]{1,0:T(8,128)(2,1)S(1)} %get-tuple-element.79), channel_id=1, source_target_pairs={{0,2},{1,3},{2,0},{3,1},{4,6},{5,7},{6,4},{7,5},{8,10},{9,11},{10,... | collective-permute-start | bytes 393224 | tf_op jit(solution)/shard_map/ppermute | solution.py:534
  21.7 1.4 %collective-permute-start.7 = (bf16[336,128]{1,0:T(8,128)(2,1)S(1)}, bf16[336,128]{1,0:T(8,128)(2,1)S(1)}, u32[]{:S(2)}, u32[]{:S(2)}) collective-permute-start(bf16[336,128]{1,0:T(8,128)(2,1)S(1)} %get-tuple-element.66), channel_id=1, source_target_pairs={{0,2},{1,3},{2,0},{3,1},{4,6},{5,7},{6,4},{7,5},{8,10},{9,11},{10,... | collective-permute-start | bytes 258056 | tf_op jit(solution)/shard_map/ppermute | solution.py:534
  23.0 2.0 %collective-permute-start.10 = (bf16[80,128]{1,0:T(8,128)(2,1)S(1)}, bf16[80,128]{1,0:T(8,128)(2,1)S(1)}, u32[]{:S(2)}, u32[]{:S(2)}) collective-permute-start(bf16[80,128]{1,0:T(8,128)(2,1)S(1)} %get-tuple-element.71), channel_id=1, source_target_pairs={{0,8},{1,9},{2,10},{3,11},{4,12},{5,13},{6,14},{7,15},{8,0},{9,1},... | collective-permute-start | bytes 61448 | tf_op jit(solution)/shard_map/ppermute | solution.py:537
  25.1 1.0 %collective-permute-start.11 = (bf16[80,128]{1,0:T(8,128)(2,1)S(1)}, bf16[80,128]{1,0:T(8,128)(2,1)S(1)}, u32[]{:S(2)}, u32[]{:S(2)}) collective-permute-start(bf16[80,128]{1,0:T(8,128)(2,1)S(1)} %get-tuple-element.72), channel_id=1, source_target_pairs={{0,12},{1,13},{2,14},{3,15},{4,8},{5,9},{6,10},{7,11},{8,4},{9,5},... | collective-permute-start | bytes 61448 | tf_op jit(solution)/shard_map/ppermute | solution.py:537
  26.1 0.5 collective-permute-start.9
  26.6 1.2 %collective-permute-done.7.theirs_ref.refs_5_ = bf16[336,128]{1,0:T(8,128)(2,1)S(1)} collective-permute-done((bf16[336,128]{1,0:T(8,128)(2,1)S(1)}, bf16[336,128]{1,0:T(8,128)(2,1)S(1)}, u32[]{:S(2)}, u32[]{:S(2)}) %collective-permute-start.7) | collective-permute-done | bytes 86048 | tf_op jit(solution)/shard_map/ppermute | solution.py:534
  27.8 0.1 collective-permute-done.10.refs_8_
  27.9 0.8 %collective-permute-start.8 = (bf16[256,128]{1,0:T(8,128)(2,1)S(1)}, bf16[256,128]{1,0:T(8,128)(2,1)S(1)}, u32[]{:S(2)}, u32[]{:S(2)}) collective-permute-start(bf16[256,128]{1,0:T(8,128)(2,1)S(1)} %shard_map.134.w0), channel_id=1, source_target_pairs={{0,4},{1,5},{2,6},{3,7},{4,0},{5,1},{6,2},{7,3},{8,12},{9,13},{10,... | collective-permute-start | bytes 196616 | tf_op jit(solution)/shard_map/ppermute | solution.py:537
  28.7 1.9 %collective-permute-done.11.refs_9_ = bf16[80,128]{1,0:T(8,128)(2,1)S(1)} collective-permute-done((bf16[80,128]{1,0:T(8,128)(2,1)S(1)}, bf16[80,128]{1,0:T(8,128)(2,1)S(1)}, u32[]{:S(2)}, u32[]{:S(2)}) %collective-permute-start.11) | collective-permute-done | bytes 20512 | tf_op jit(solution)/shard_map/ppermute | solution.py:537
  30.7 1.3 %shard_map.135 = (bf16[640,64]{1,0:T(8,128)(2,1)S(1)}, bf16[128,128]{1,0:T(8,128)(2,1)S(1)}) custom-call(s32[12]{0:T(128)S(1)} %copy-done.3, s32[12]{0:T(128)S(1)} %copy-done.4, bf16[512,512]{1,0:T(8,128)(2,1)S(1)} %get-tuple-element.67.refs_2_, bf16[640,256]{1,0:T(8,128)(2,1)S(1)} %get-tuple-element.68.refs_3_, ...), custom_call_target="tpu_custom_call" | custom-call | flops 1000000000 | bytes 2000000 | tf_op jit(solution)/shard_map/pallas_call | solution.py:512
  32.0 2.6 %collective-permute-start.14 = (bf16[128,128]{1,0:T(8,128)(2,1)S(1)}, bf16[128,128]{1,0:T(8,128)(2,1)S(1)}, u32[]{:S(2)}, u32[]{:S(2)}) collective-permute-start(bf16[128,128]{1,0:T(8,128)(2,1)S(1)} %get-tuple-element.73.fm_ref), channel_id=1, source_target_pairs={{0,12},{1,13},{2,14},{3,15},{4,8},{5,9},{6,10},{7,11},{8,4},{9,5},... | collective-permute-start | bytes 98312 | tf_op jit(solution)/shard_map/ppermute | solution.py:537
  34.6 1.0 %collective-permute-start.13 = (bf16[384,128]{1,0:T(8,128)(2,1)S(1)}, bf16[384,128]{1,0:T(8,128)(2,1)S(1)}, u32[]{:S(2)}, u32[]{:S(2)}) collective-permute-start(bf16[384,128]{1,0:T(8,128)(2,1)S(1)} %shard_map.136.refs_0_), channel_id=1, source_target_pairs={{0,8},{1,9},{2,10},{3,11},{4,12},{5,13},{6,14},{7,15},{8,0},{9,1},... | collective-permute-start | bytes 294920 | tf_op jit(solution)/shard_map/ppermute | solution.py:537
  35.6 1.1 %shard_map.137 = bf16[80,8,256]{2,1,0:T(8,128)(2,1)} custom-call(bf16[640,64]{1,0:T(8,128)(2,1)S(1)} %get-tuple-element.74.pg_ref, bf16[64,256]{1,0:T(8,128)(2,1)S(1)} %bitcast.7, f32[1,256]{1,0:T(1,128)S(1)} %bitcast.9, f32[640,256]{1,0:T(8,128)S(1)} %get-tuple-element.75.hat_ref, f32[640,128]{1,0:T(8,128)S(1)} %get-tuple-element.76.rstd_ref), custom_call_target="tpu_custom_call" | custom-call | flops 1000000000 | bytes 2000000 | tf_op jit(solution)/shard_map/pallas_call | solution.py:512
  36.8 1.0 %shard_map.138 = bf16[8,128,128]{2,1,0:T(8,128)(2,1)} custom-call(bf16[256,128]{1,0:T(8,128)(2,1)S(1)} %get-tuple-element.77.refs_0_, bf16[256,128]{1,0:T(8,128)(2,1)S(1)} %collective-permute-done.15.refs_1_, bf16[512,128]{1,0:T(8,128)(2,1)S(1)} %collective-permute-done.16.refs_2_, bf16[512,128]{1,0:T(8,128)(2,1)S(1)} %collective-permute-done.17.refs_3_), custom_call_target="tpu_custom_call" | custom-call | flops 1000000000 | bytes 2000000 | tf_op jit(solution)/shard_map/pallas_call | solution.py:512
  37.8 0.3 collective-permute-done.14.refs_3_
  38.1 3.4 %collective-permute-done.13.refs_2_ = bf16[384,128]{1,0:T(8,128)(2,1)S(1)} collective-permute-done((bf16[384,128]{1,0:T(8,128)(2,1)S(1)}, bf16[384,128]{1,0:T(8,128)(2,1)S(1)}, u32[]{:S(2)}, u32[]{:S(2)}) %collective-permute-start.13) | collective-permute-done | bytes 98336 | tf_op jit(solution)/shard_map/ppermute | solution.py:537
  41.5 1.2 %collective-permute-start.18 = (bf16[384,128]{1,0:T(8,128)(2,1)S(1)}, bf16[384,128]{1,0:T(8,128)(2,1)S(1)}, u32[]{:S(2)}, u32[]{:S(2)}) collective-permute-start(bf16[384,128]{1,0:T(8,128)(2,1)S(1)} %shard_map.139.own_ref), channel_id=1, source_target_pairs={{0,2},{1,3},{2,0},{3,1},{4,6},{5,7},{6,4},{7,5},{8,10},{9,11},{10,... | collective-permute-start | bytes 294920 | tf_op jit(solution)/shard_map/ppermute | solution.py:534
  42.8 3.4 %collective-permute-done.18.cross_ref = bf16[384,128]{1,0:T(8,128)(2,1)S(1)} collective-permute-done((bf16[384,128]{1,0:T(8,128)(2,1)S(1)}, bf16[384,128]{1,0:T(8,128)(2,1)S(1)}, u32[]{:S(2)}, u32[]{:S(2)}) %collective-permute-start.18) | collective-permute-done | bytes 98336 | tf_op jit(solution)/shard_map/ppermute | solution.py:534
  46.2 0.1 collective-permute-start.19
  46.3 1.4 %collective-permute-done.19.core_ref = bf16[640,128]{1,0:T(8,128)(2,1)S(1)} collective-permute-done((bf16[640,128]{1,0:T(8,128)(2,1)S(1)}, bf16[640,128]{1,0:T(8,128)(2,1)S(1)}, u32[]{:S(2)}, u32[]{:S(2)}) %collective-permute-start.19) | collective-permute-done | bytes 163872 | tf_op jit(solution)/shard_map/ppermute | solution.py:534
  47.7 0.8 %shard_map.141 = (f32[1024,128]{1,0:T(8,128)}, f32[64,256]{1,0:T(8,128)}) custom-call(bf16[640,128]{1,0:T(8,128)(2,1)S(1)} %shard_map.140.mine_ref, bf16[640,128]{1,0:T(8,128)(2,1)S(1)} %collective-permute-done.19.core_ref), custom_call_target="tpu_custom_call" | custom-call | flops 100000000 | bytes 200000 | tf_op jit(solution)/shard_map/pallas_call | solution.py:512
  (31 shorter events, 0.3 us)
Async XLA Ops:
  0.6 10.2 %copy-start.3 = (s32[12]{0:T(128)S(1)}, s32[12]{0:T(128)}, u32[]{:S(2)}) copy-start(s32[12]{0:T(128)} %refs_0_.7) | copy-start | bytes 148
  0.6 10.2 %copy-start.4 = (s32[12]{0:T(128)S(1)}, s32[12]{0:T(128)}, u32[]{:S(2)}) copy-start(s32[12]{0:T(128)} %refs_1_.5) | copy-start | bytes 148
  3.0 7.0 %collective-permute-start = (bf16[336,128]{1,0:T(8,128)(2,1)S(1)}, bf16[336,128]{1,0:T(8,128)(2,1)S(1)}, u32[]{:S(2)}, u32[]{:S(2)}) collective-permute-start(bf16[336,128]{1,0:T(8,128)(2,1)S(1)} %get-tuple-element.49), channel_id=1, source_target_pairs={{0,1},{1,0},{2,3},{3,2},{4,5},{5,4},{6,7},{7,6},{8,9},{9,8},{10,11... | collective-permute-start | bytes 258056 | tf_op jit(solution)/shard_map/ppermute | solution.py:534
  3.5 7.0 %collective-permute-start.1 = (bf16[336,128]{1,0:T(8,128)(2,1)S(1)}, bf16[336,128]{1,0:T(8,128)(2,1)S(1)}, u32[]{:S(2)}, u32[]{:S(2)}) collective-permute-start(bf16[336,128]{1,0:T(8,128)(2,1)S(1)} %get-tuple-element.50), channel_id=1, source_target_pairs={{0,2},{1,3},{2,0},{3,1},{4,6},{5,7},{6,4},{7,5},{8,10},{9,11},{10,... | collective-permute-start | bytes 258056 | tf_op jit(solution)/shard_map/ppermute | solution.py:534
  6.0 4.8 %collective-permute-start.2 = (bf16[336,128]{1,0:T(8,128)(2,1)S(1)}, bf16[336,128]{1,0:T(8,128)(2,1)S(1)}, u32[]{:S(2)}, u32[]{:S(2)}) collective-permute-start(bf16[336,128]{1,0:T(8,128)(2,1)S(1)} %get-tuple-element.51), channel_id=1, source_target_pairs={{0,3},{1,2},{2,1},{3,0},{4,7},{5,6},{6,5},{7,4},{8,11},{9,10},{10,... | collective-permute-start | bytes 258056 | tf_op jit(solution)/shard_map/ppermute | solution.py:534
  6.1 7.5 %collective-permute-start.3 = (bf16[80,128]{1,0:T(8,128)(2,1)S(1)}, bf16[80,128]{1,0:T(8,128)(2,1)S(1)}, u32[]{:S(2)}, u32[]{:S(2)}) collective-permute-start(bf16[80,128]{1,0:T(8,128)(2,1)S(1)} %get-tuple-element.56.refs_6_), channel_id=1, source_target_pairs={{0,12},{1,13},{2,14},{3,15},{4,8},{5,9},{6,10},{7,11},{8,4},{9,5},... | collective-permute-start | bytes 61448 | tf_op jit(solution)/shard_map/ppermute | solution.py:537
  9.9 4.7 %collective-permute-start.4 = (bf16[80,128]{1,0:T(8,128)(2,1)S(1)}, bf16[80,128]{1,0:T(8,128)(2,1)S(1)}, u32[]{:S(2)}, u32[]{:S(2)}) collective-permute-start(bf16[80,128]{1,0:T(8,128)(2,1)S(1)} %get-tuple-element.56.refs_6_), channel_id=1, source_target_pairs={{0,8},{1,9},{2,10},{3,11},{4,12},{5,13},{6,14},{7,15},{8,0},{9,1},... | collective-permute-start | bytes 61448 | tf_op jit(solution)/shard_map/ppermute | solution.py:537
  10.0 4.7 %collective-permute-start.5 = (bf16[80,128]{1,0:T(8,128)(2,1)S(1)}, bf16[80,128]{1,0:T(8,128)(2,1)S(1)}, u32[]{:S(2)}, u32[]{:S(2)}) collective-permute-start(bf16[80,128]{1,0:T(8,128)(2,1)S(1)} %get-tuple-element.56.refs_6_), channel_id=1, source_target_pairs={{0,4},{1,5},{2,6},{3,7},{4,0},{5,1},{6,2},{7,3},{8,12},{9,13},{10,... | collective-permute-start | bytes 61448 | tf_op jit(solution)/shard_map/ppermute | solution.py:537
  14.6 1.8 %copy-start.2 = (f32[128]{0:T(128)S(1)}, f32[128]{0:T(128)}, u32[]{:S(2)}) copy-start(f32[128]{0:T(128)} %param.16) | copy-start | bytes 1540
  20.0 1.6 %collective-permute-start.6 = (bf16[672,128]{1,0:T(8,128)(2,1)S(1)}, bf16[672,128]{1,0:T(8,128)(2,1)S(1)}, u32[]{:S(2)}, u32[]{:S(2)}) collective-permute-start(bf16[672,128]{1,0:T(8,128)(2,1)S(1)} %get-tuple-element.64), channel_id=1, source_target_pairs={{0,1},{1,0},{2,3},{3,2},{4,5},{5,4},{6,7},{7,6},{8,9},{9,8},{10,11... | collective-permute-start | bytes 516104 | tf_op jit(solution)/shard_map/ppermute | solution.py:534
  20.0 6.5 %collective-permute-start.16 = (bf16[512,128]{1,0:T(8,128)(2,1)S(1)}, bf16[512,128]{1,0:T(8,128)(2,1)S(1)}, u32[]{:S(2)}, u32[]{:S(2)}) collective-permute-start(bf16[512,128]{1,0:T(8,128)(2,1)S(1)} %get-tuple-element.79), channel_id=1, source_target_pairs={{0,2},{1,3},{2,0},{3,1},{4,6},{5,7},{6,4},{7,5},{8,10},{9,11},{10,... | collective-permute-start | bytes 393224 | tf_op jit(solution)/shard_map/ppermute | solution.py:534
  21.7 6.2 %collective-permute-start.7 = (bf16[336,128]{1,0:T(8,128)(2,1)S(1)}, bf16[336,128]{1,0:T(8,128)(2,1)S(1)}, u32[]{:S(2)}, u32[]{:S(2)}) collective-permute-start(bf16[336,128]{1,0:T(8,128)(2,1)S(1)} %get-tuple-element.66), channel_id=1, source_target_pairs={{0,2},{1,3},{2,0},{3,1},{4,6},{5,7},{6,4},{7,5},{8,10},{9,11},{10,... | collective-permute-start | bytes 258056 | tf_op jit(solution)/shard_map/ppermute | solution.py:534
  23.0 4.9 %collective-permute-start.10 = (bf16[80,128]{1,0:T(8,128)(2,1)S(1)}, bf16[80,128]{1,0:T(8,128)(2,1)S(1)}, u32[]{:S(2)}, u32[]{:S(2)}) collective-permute-start(bf16[80,128]{1,0:T(8,128)(2,1)S(1)} %get-tuple-element.71), channel_id=1, source_target_pairs={{0,8},{1,9},{2,10},{3,11},{4,12},{5,13},{6,14},{7,15},{8,0},{9,1},... | collective-permute-start | bytes 61448 | tf_op jit(solution)/shard_map/ppermute | solution.py:537
  25.1 5.6 %collective-permute-start.11 = (bf16[80,128]{1,0:T(8,128)(2,1)S(1)}, bf16[80,128]{1,0:T(8,128)(2,1)S(1)}, u32[]{:S(2)}, u32[]{:S(2)}) collective-permute-start(bf16[80,128]{1,0:T(8,128)(2,1)S(1)} %get-tuple-element.72), channel_id=1, source_target_pairs={{0,12},{1,13},{2,14},{3,15},{4,8},{5,9},{6,10},{7,11},{8,4},{9,5},... | collective-permute-start | bytes 61448 | tf_op jit(solution)/shard_map/ppermute | solution.py:537
  26.1 4.6 %collective-permute-start.9 = (bf16[80,128]{1,0:T(8,128)(2,1)S(1)}, bf16[80,128]{1,0:T(8,128)(2,1)S(1)}, u32[]{:S(2)}, u32[]{:S(2)}) collective-permute-start(bf16[80,128]{1,0:T(8,128)(2,1)S(1)} %get-tuple-element.70), channel_id=1, source_target_pairs={{0,4},{1,5},{2,6},{3,7},{4,0},{5,1},{6,2},{7,3},{8,12},{9,13},{10,... | collective-permute-start | bytes 61448 | tf_op jit(solution)/shard_map/ppermute | solution.py:537
  26.6 10.2 %collective-permute-start.15 = (bf16[256,128]{1,0:T(8,128)(2,1)S(1)}, bf16[256,128]{1,0:T(8,128)(2,1)S(1)}, u32[]{:S(2)}, u32[]{:S(2)}) collective-permute-start(bf16[256,128]{1,0:T(8,128)(2,1)S(1)} %get-tuple-element.78), channel_id=1, source_target_pairs={{0,1},{1,0},{2,3},{3,2},{4,5},{5,4},{6,7},{7,6},{8,9},{9,8},{10,11... | collective-permute-start | bytes 196616 | tf_op jit(solution)/shard_map/ppermute | solution.py:534
  27.8 8.9 %collective-permute-start.17 = (bf16[512,128]{1,0:T(8,128)(2,1)S(1)}, bf16[512,128]{1,0:T(8,128)(2,1)S(1)}, u32[]{:S(2)}, u32[]{:S(2)}) collective-permute-start(bf16[512,128]{1,0:T(8,128)(2,1)S(1)} %collective-permute-done.16.refs_2_), channel_id=1, source_target_pairs={{0,1},{1,0},{2,3},{3,2},{4,5},{5,4},{6,7},{7,6},{8,9},{9,8},{10,11... | collective-permute-start | bytes 393224 | tf_op jit(solution)/shard_map/ppermute | solution.py:534
  27.8 7.8 %copy-start = (bf16[256,64]{0,1:T(8,128)(2,1)S(1)}, bf16[256,64]{0,1:T(8,128)(2,1)}, u32[]{:S(2)}) copy-start(bf16[256,64]{0,1:T(8,128)(2,1)} %param.13) | copy-start | bytes 98308
  27.8 7.8 %copy-start.1 = (f32[256]{0:T(256)S(1)}, f32[256]{0:T(256)}, u32[]{:S(2)}) copy-start(f32[256]{0:T(256)} %param.11) | copy-start | bytes 3076
  27.9 6.7 %collective-permute-start.8 = (bf16[256,128]{1,0:T(8,128)(2,1)S(1)}, bf16[256,128]{1,0:T(8,128)(2,1)S(1)}, u32[]{:S(2)}, u32[]{:S(2)}) collective-permute-start(bf16[256,128]{1,0:T(8,128)(2,1)S(1)} %shard_map.134.w0), channel_id=1, source_target_pairs={{0,4},{1,5},{2,6},{3,7},{4,0},{5,1},{6,2},{7,3},{8,12},{9,13},{10,... | collective-permute-start | bytes 196616 | tf_op jit(solution)/shard_map/ppermute | solution.py:537
  32.0 5.8 %collective-permute-start.12 = (bf16[128,128]{1,0:T(8,128)(2,1)S(1)}, bf16[128,128]{1,0:T(8,128)(2,1)S(1)}, u32[]{:S(2)}, u32[]{:S(2)}) collective-permute-start(bf16[128,128]{1,0:T(8,128)(2,1)S(1)} %get-tuple-element.73.fm_ref), channel_id=1, source_target_pairs={{0,4},{1,5},{2,6},{3,7},{4,0},{5,1},{6,2},{7,3},{8,12},{9,13},{10,... | collective-permute-start | bytes 98312 | tf_op jit(solution)/shard_map/ppermute | solution.py:537
  32.0 6.1 %collective-permute-start.14 = (bf16[128,128]{1,0:T(8,128)(2,1)S(1)}, bf16[128,128]{1,0:T(8,128)(2,1)S(1)}, u32[]{:S(2)}, u32[]{:S(2)}) collective-permute-start(bf16[128,128]{1,0:T(8,128)(2,1)S(1)} %get-tuple-element.73.fm_ref), channel_id=1, source_target_pairs={{0,12},{1,13},{2,14},{3,15},{4,8},{5,9},{6,10},{7,11},{8,4},{9,5},... | collective-permute-start | bytes 98312 | tf_op jit(solution)/shard_map/ppermute | solution.py:537
  34.6 6.9 %collective-permute-start.13 = (bf16[384,128]{1,0:T(8,128)(2,1)S(1)}, bf16[384,128]{1,0:T(8,128)(2,1)S(1)}, u32[]{:S(2)}, u32[]{:S(2)}) collective-permute-start(bf16[384,128]{1,0:T(8,128)(2,1)S(1)} %shard_map.136.refs_0_), channel_id=1, source_target_pairs={{0,8},{1,9},{2,10},{3,11},{4,12},{5,13},{6,14},{7,15},{8,0},{9,1},... | collective-permute-start | bytes 294920 | tf_op jit(solution)/shard_map/ppermute | solution.py:537
  41.5 4.7 %collective-permute-start.18 = (bf16[384,128]{1,0:T(8,128)(2,1)S(1)}, bf16[384,128]{1,0:T(8,128)(2,1)S(1)}, u32[]{:S(2)}, u32[]{:S(2)}) collective-permute-start(bf16[384,128]{1,0:T(8,128)(2,1)S(1)} %shard_map.139.own_ref), channel_id=1, source_target_pairs={{0,2},{1,3},{2,0},{3,1},{4,6},{5,7},{6,4},{7,5},{8,10},{9,11},{10,... | collective-permute-start | bytes 294920 | tf_op jit(solution)/shard_map/ppermute | solution.py:534
  46.2 1.5 %collective-permute-start.19 = (bf16[640,128]{1,0:T(8,128)(2,1)S(1)}, bf16[640,128]{1,0:T(8,128)(2,1)S(1)}, u32[]{:S(2)}, u32[]{:S(2)}) collective-permute-start(bf16[640,128]{1,0:T(8,128)(2,1)S(1)} %shard_map.140.mine_ref), channel_id=1, source_target_pairs={{0,1},{1,0},{2,3},{3,2},{4,5},{5,4},{6,7},{7,6},{8,9},{9,8},{10,11... | collective-permute-start | bytes 491528 | tf_op jit(solution)/shard_map/ppermute | solution.py:534

commit v4 on v3

--- a/solution.py
+++ b/solution.py
@@ -171,7 +171,6 @@
     depth = x_ref.shape[0]
     residues = adj_ref.shape[1]
     groups = residues // 32
-    chains = len_ref.shape[0]
     a, b = place()
     spread = spread_matrix()
     spread_ref[...] = spread
@@ -206,16 +205,7 @@
     full[0 : depth * BLOCK, :] = proj
     full[depth * BLOCK :, :] = jnp.zeros((EXTRA * BLOCK, 64), F32)
     comp[0 : PAIRED * BLOCK, :] = proj[0 : PAIRED * BLOCK]
-    residue = lax.broadcasted_iota(jnp.int32, (EXTRA * BLOCK, 64), 0)
-    entry = residue >> 3
-    chain = chain_of(32 * a + 8 * b + (residue & 7), bounds_of(len_ref))
-    extra = jnp.zeros((EXTRA * BLOCK, 64), F32)
-    start = jnp.int32(PAIRED)
-    for c in range(chains):
-        rows = full[pl.ds(pl.multiple_of(start * BLOCK, BLOCK), EXTRA * BLOCK), :]
-        extra = jnp.where((chain == c) & (entry < hom_ref[c]), rows, extra)
-        start = start + hom_ref[c]
-    comp[PAIRED * BLOCK :, :] = extra
+    comp[PAIRED * BLOCK :, :] = chain_rows(full, a, b, len_ref, hom_ref)
     rows = PAIRED + EXTRA
     wide = jnp.concatenate([comp[pl.ds(r, rows, stride=BLOCK), :] for r in range(BLOCK)], axis=1)
     out = jnp.dot(wide.astype(BF16), spread, preferred_element_type=F32)
@@ -226,20 +216,42 @@
     copies[8].wait()
 
 
+def chain_rows(full, a, b, len_ref, hom_ref):
+    lanes = full.shape[1]
+    residue = lax.broadcasted_iota(jnp.int32, (EXTRA * BLOCK, lanes), 0)
+    entry = residue >> 3
+    chain = chain_of(32 * a + 8 * b + (residue & 7), bounds_of(len_ref))
+    extra = jnp.zeros((EXTRA * BLOCK, lanes), F32)
+    start = jnp.int32(PAIRED)
+    for c in range(len_ref.shape[0]):
+        rows = full[pl.ds(pl.multiple_of(start * BLOCK, BLOCK), EXTRA * BLOCK), :]
+        extra = jnp.where((chain == c) & (entry < hom_ref[c]), rows, extra)
+        start = start + hom_ref[c]
+    return extra
+
+
 def adjoint_kernel(
-    chunks, len_ref, hom_ref, final_ref, swap_ref, m0, m1, m2, m3,
-    s_ref, og_ref, ft_ref, lx_ref,
+    chunks, len_ref, hom_ref, final_ref, swap_ref, spread_ref, norm_ref, m0, m1, m2, m3,
+    s_ref, og_ref, ft_ref, lx_ref, lt_ref, gather_ref, few_ref, nfull,
 ):
     messages = (m0, m1, m2, m3)
     a, b = place()
     ends = bounds_of(len_ref)
     swap = swap_ref[...]
     bottom = chunks * 256
-    lx_ref[...] = spread_rows(
+    lx = spread_rows(
         left_lanes([m[bottom : bottom + PACKED, :] for m in messages]),
         left_chain(a, b, ends),
         len_ref.shape[0],
-    ).astype(BF16)
+    )
+    lx_ref[...] = lx.astype(BF16)
+    lt_ref[...] = lx.T.astype(BF16)
+    gather_ref[...] = spread_ref[...].astype(F32).T.astype(BF16)
+    depth8 = norm_ref.shape[0]
+    nfull[0:depth8, :] = norm_ref[...].astype(F32)
+    nfull[depth8:, :] = jnp.zeros((EXTRA * BLOCK, 256), F32)
+    few_ref[0 : PAIRED * BLOCK, :] = norm_ref[0 : PAIRED * BLOCK, :]
+    few_ref[PAIRED * BLOCK :, :] = chain_rows(nfull, a, b, len_ref, hom_ref).astype(BF16)
     low = lax.broadcasted_iota(jnp.int32, (32, 128), 0)
     chain_i, inv_same = [], []
     for t in range(QUAD):
@@ -295,7 +307,7 @@
 
 
 def grad_kernel(
-    chunks, len_ref, og_ref, lx_ref, r3, r2, r1, r0,
+    chunks, len_ref, og_ref, lt_ref, r3, r2, r1, r0,
     l0, l1, l2, l3, g0, g1, g2, g3, rt_ref, lg_acc,
 ):
     rights = (r0, r1, r2, r3)
@@ -304,7 +316,7 @@
     a, b = place()
     ends = bounds_of(len_ref)
     chain_l = left_chain(a, b, ends)
-    lx = lx_ref[...]
+    lt = lt_ref[...]
     lg_acc[...] = jnp.zeros(lg_acc.shape, F32)
 
     def step(g, _):
@@ -314,7 +326,7 @@
         rx = spread_rows(right_lanes([r[at80, :] for r in rights]), chain_r, chains)
         rt_ref[at1024, :] = rx.T.astype(BF16)
         og = og_ref[at1024, :]
-        rg = lax.dot_general(lx, og, (((1,), (1,)), ((), ())), preferred_element_type=F32)
+        rg = jnp.dot(og, lt, preferred_element_type=F32).T
         rg = gather_rows(rg, chain_r, chains)
         for tt in range(4):
             grads[tt][at80, :] = pack(
@@ -406,49 +418,48 @@
     theirs_ref[...] = total([cross_ref[...], core_ref[rows:, :]]).astype(BF16)
 
 
-def back_kernel(groups, len_ref, hom_ref, spread_ref, norm_ref, *refs):
+def back_kernel(groups, gather_ref, few_ref, *refs):
     quads, rgs = refs[:2], refs[2 : 2 + groups]
-    pg_ref, out_ref, comp, full = refs[2 + groups :]
-    chains = len_ref.shape[0]
-    depth8 = pg_ref.shape[0]
-    a, b = place()
+    pg_ref, out_ref, comp = refs[2 + groups :]
     lg = total([q[256:, :] for q in quads])
     rg = total([r[...] for r in rgs])
     wide = jnp.concatenate([blk for g in (lg, rg) for blk in unpack(g)], axis=1)
     rows = PAIRED + EXTRA
-    per = lax.dot_general(
-        wide.astype(BF16), spread_ref[...], (((1,), (1,)), ((), ())), preferred_element_type=F32
-    )
+    per = jnp.dot(wide.astype(BF16), gather_ref[...], preferred_element_type=F32)
     for r in range(BLOCK):
         comp[pl.ds(r, rows, stride=BLOCK), :] = per[:, r * 64 : r * 64 + 64]
-    full[0 : PAIRED * BLOCK, :] = comp[0 : PAIRED * BLOCK, :]
+    pg = comp[...]
+    pg_ref[...] = pg.astype(BF16)
+    fm = jnp.dot(pg.T.astype(BF16), few_ref[...], preferred_element_type=F32)
+    out_ref[...] = jnp.concatenate([fm[:, 0:128], fm[:, 128:256]], axis=0).astype(BF16)
+
+
+def fold_kernel(mine_ref, theirs_ref, out_ref):
+    out_ref[...] = total([mine_ref[0:256, :], theirs_ref[0:256, :]]).astype(BF16)
+
+
+def join_kernel(w0, w1, fm_ref, out_ref):
+    out_ref[0:256, :] = total([w0[...], w1[...]]).astype(BF16)
+    out_ref[256:384, :] = fm_ref[...]
+
+
+def align_kernel(
+    len_ref, hom_ref, pg_ref, mat_ref, scale_ref, hat_ref, rstd_ref, out_ref, full
+):
+    a, b = place()
+    depth8 = hat_ref.shape[0]
+    full[0 : PAIRED * BLOCK, :] = pg_ref[0 : PAIRED * BLOCK, :].astype(F32)
     full[PAIRED * BLOCK :, :] = jnp.zeros((full.shape[0] - PAIRED * BLOCK, 64), F32)
-    extra = comp[PAIRED * BLOCK :, :]
+    extra = pg_ref[PAIRED * BLOCK :, :].astype(F32)
     residue = lax.broadcasted_iota(jnp.int32, (EXTRA * BLOCK, 64), 0)
     entry = residue >> 3
     chain = chain_of(32 * a + 8 * b + (residue & 7), bounds_of(len_ref))
     start = jnp.int32(PAIRED)
-    for c in range(chains):
+    for c in range(len_ref.shape[0]):
         at = pl.ds(pl.multiple_of(start * BLOCK, BLOCK), EXTRA * BLOCK)
         full[at, :] += jnp.where((chain == c) & (entry < hom_ref[c]), extra, 0.0)
         start = start + hom_ref[c]
-    pg = full[0:depth8, :]
-    pg_ref[...] = pg.astype(BF16)
-    fm = jnp.dot(pg.T.astype(BF16), norm_ref[...], preferred_element_type=F32)
-    out_ref[...] = jnp.concatenate([fm[:, 0:128], fm[:, 128:256]], axis=0).astype(BF16)
-
-
-def fold_kernel(mine_ref, theirs_ref, out_ref):
-    out_ref[...] = total([mine_ref[0:256, :], theirs_ref[0:256, :]]).astype(BF16)
-
-
-def join_kernel(w0, w1, fm_ref, out_ref):
-    out_ref[0:256, :] = total([w0[...], w1[...]]).astype(BF16)
-    out_ref[256:384, :] = fm_ref[...]
-
-
-def align_kernel(pg_ref, mat_ref, scale_ref, hat_ref, rstd_ref, out_ref):
-    g = jnp.dot(pg_ref[...], mat_ref[...], preferred_element_type=F32)
+    g = jnp.dot(full[0:depth8, :].astype(BF16), mat_ref[...], preferred_element_type=F32)
     g = g * scale_ref[...]
     hat = hat_ref[...]
     m1 = jnp.mean(g, axis=-1, keepdims=True)
@@ -477,9 +488,9 @@
     out_ref[...] = work[...].reshape(out_ref.shape).astype(BF16)
 
 
-def merge_kernel(far_half, *refs):
+def merge_kernel(*refs):
     out_ref, fms = refs[-1], refs[:-1]
-    out_ref[0:256, :] = total([fms[0][0:256, :], fms[far_half][0:256, :]]).astype(BF16)
+    out_ref[0:256, :] = total([fms[0][0:256, :], fms[1][0:256, :]]).astype(BF16)
     out_ref[256:384, :] = total([f[f.shape[0] - 128 :, :] for f in fms]).astype(BF16)
 
 
@@ -582,16 +593,20 @@
     messages = quad(messages)
     rights = by_slot([right] + [far(right, u) for u in range(1, groups)])
 
-    s, og, final_t, lx = call(
+    s, og, final_t, lx, lt, gather, few = call(
         lambda *refs: adjoint_kernel(chunks, *refs),
         [
             sds((chunks * 1024, 128), BF16),
             sds((chunks * 1024, 1024), BF16),
             sds((128, 1024), BF16),
             sds((128, 1024), BF16),
+            sds((1024, 128), BF16),
+            sds((512, 512), BF16),
+            sds(((PAIRED + EXTRA) * BLOCK, 256), BF16),
         ],
-        [lengths, homologs, final, swap, *messages],
-        in_specs=[SMEM] * 2 + [vmem()] * (2 + QUAD),
+        [lengths, homologs, final, swap, spread, normed, *messages],
+        in_specs=[SMEM] * 2 + [vmem()] * (4 + QUAD),
+        scratch=[pltpu.VMEM(((depth + EXTRA) * BLOCK, 256), F32)],
         work=2 * 10**9,
     )
 
@@ -600,7 +615,7 @@
         [sds((PACKED, 128), BF16)] * QUAD
         + [sds((chunks * PACKED, 128), BF16)] * 4
         + [sds((chunks * 1024, 128), BF16)],
-        [lengths, og, lx, *rights[::-1]],
+        [lengths, og, lt, *rights[::-1]],
         in_specs=[SMEM] + [vmem()] * (2 + QUAD),
         scratch=[pltpu.VMEM((128, 1024), F32)],
         work=2 * 10**9,
@@ -630,28 +645,26 @@
 
     pg, fm = call(
         lambda *refs: back_kernel(groups, *refs),
-        [sds((depth * BLOCK, 64), BF16), sds((128, 128), BF16)],
-        [lengths, homologs, spread, normed, *quads, *rgs],
-        in_specs=[SMEM] * 2 + [vmem()] * (4 + groups),
-        scratch=[
-            pltpu.VMEM(((PAIRED + EXTRA) * BLOCK, 64), F32),
-            pltpu.VMEM(((depth + EXTRA) * BLOCK, 64), F32),
-        ],
+        [sds(((PAIRED + EXTRA) * BLOCK, 64), BF16), sds((128, 128), BF16)],
+        [gather, few, *quads, *rgs],
+        scratch=[pltpu.VMEM(((PAIRED + EXTRA) * BLOCK, 64), F32)],
         work=10**9,
     )
     half = groups // 2
     w = call(fold_kernel, sds((256, 128), BF16), quads, work=10**7)
-    steps = [1 << k for k in range(half.bit_length() - 1)]
+    steps = [half >> k for k in range(half.bit_length() - 1)]
     for u in steps[:-1]:
         w = call(fold_kernel, sds((256, 128), BF16), [w, far(w, u)], work=10**7)
     part = call(join_kernel, sds((384, 128), BF16), [w, far(w, steps[-1]), fm], work=10**7)
-    parts = [part] + [far(part if u == half else fm, u) for u in range(1, groups)]
+    parts = [part] + [far(part if u == 1 else fm, u) for u in range(1, groups)]
     pair_cross = near(pair_cross, 2)
     pairs = [pair_own, near(pair_core, 1), pair_cross, near(pair_cross, 1)]
     alignment_gradient = call(
         align_kernel,
         sds(x.shape, BF16),
-        [pg, mat, scale, hat, rstd],
+        [lengths, homologs, pg, mat, scale, hat, rstd],
+        in_specs=[SMEM] * 2 + [vmem()] * 5,
+        scratch=[pltpu.VMEM(((depth + EXTRA) * BLOCK, 64), F32)],
         work=10**9,
     )
     pair_delta = call(
@@ -665,7 +678,7 @@
         (parts, alignment_gradient, pair_delta)
     )
     merged = call(
-        lambda *refs: merge_kernel(half, *refs), sds((384, 128), BF16), parts, work=10**7
+        merge_kernel, sds((384, 128), BF16), parts, work=10**7
     )
     relay = call(relay_kernel, sds((640, 128), BF16), [merged, near(merged, 2)], work=10**7)
     w, fm = call(

time: 48.7 us -> 46.9 us (0.963)
  waiting for transfers between devices: 13.1 us -> 9.2 us
  starting transfers between devices: 19.8 us -> 21.9 us
    ppermute x10, waiting for transfers between devices: 6.75 us -> 3.29 us  [far(): return lax.ppermute(value, 'row', [(k, k ^ 4 * u) for k in range(devices)])]
    ppermute x10, starting transfers between devices: 12.3 us -> 14 us  [far(): return lax.ppermute(value, 'row', [(k, k ^ 4 * u) for k in range(devices)])]
  transfers between devices with their start and end apart: 20 -> 20, of which waited for: 9 -> 9; matrix products, arithmetic and copies ran while one was open for 0% -> 0% of each run, Pallas kernels for 13% -> 14%
where the time goes in v4:
time: 46.9 us; the launch traced here: 46.8 us
  starting transfers between devices  21.9 us (47%)
  Pallas kernels  15 us (32%)
  waiting for transfers between devices  9.2 us (20%)
  between operations  0.75 us (2%)
    pallas_call x13, Pallas kernels, call(): pl.pallas_call(kernel, out_shape=outs, in_specs=in_specs if in_specs is n...  15 us
    ppermute x10, starting transfers between devices, far(): return lax.ppermute(value, 'row', [(k, k ^ 4 * u) for k in range(devices)])  14 us
    ppermute x10, starting transfers between devices, near(): return lax.ppermute(value, 'row', [(k, k ^ t) for k in range(devices)])  7.82 us
    ppermute x10, waiting for transfers between devices, near(): return lax.ppermute(value, 'row', [(k, k ^ t) for k in range(devices)])  5.9 us
    ppermute x10, waiting for transfers between devices, far(): return lax.ppermute(value, 'row', [(k, k ^ 4 * u) for k in range(devices)])  3.29 us
  transfers between devices with their start and end apart: 20, of which 9 were waited for; matrix products, arithmetic and copies ran while one was open for 0% of the time, Pallas kernels for 14%

profile of v4, /device:TPU:0, one launch (start us, length us, event | category | flops | bytes accessed | tf_op | source)
XLA Modules:
  0.0 46.8 jit_solution(8764443367577523185)
XLA Ops:
  0.7 2.3 %shard_map.129 = (bf16[336,128]{1,0:T(8,128)(2,1)S(1)}, bf16[336,128]{1,0:T(8,128)(2,1)S(1)}, bf16[336,128]{1,0:T(8,128)(2,1)S(1)}, bf16[336,128]{1,0:T(8,128)(2...) custom-call(bf16[80,8,256]{2,1,0:T(8,128)(2,1)} %x_hbm.1, ...), custom_call_target="tpu_custom_call" | custom-call | flops 1000000000 | bytes 2000000 | tf_op jit(solution)/shard_map/pallas_call | solution.py:523
  3.0 0.5 %collective-permute-start = (bf16[336,128]{1,0:T(8,128)(2,1)S(1)}, bf16[336,128]{1,0:T(8,128)(2,1)S(1)}, u32[]{:S(2)}, u32[]{:S(2)}) collective-permute-start(bf16[336,128]{1,0:T(8,128)(2,1)S(1)} %get-tuple-element.54), channel_id=1, source_target_pairs={{0,1},{1,0},{2,3},{3,2},{4,5},{5,4},{6,7},{7,6},{8,9},{9,8},{10,11... | collective-permute-start | bytes 258056 | tf_op jit(solution)/shard_map/ppermute | solution.py:545
  3.5 2.6 %collective-permute-start.1 = (bf16[336,128]{1,0:T(8,128)(2,1)S(1)}, bf16[336,128]{1,0:T(8,128)(2,1)S(1)}, u32[]{:S(2)}, u32[]{:S(2)}) collective-permute-start(bf16[336,128]{1,0:T(8,128)(2,1)S(1)} %get-tuple-element.55), channel_id=1, source_target_pairs={{0,2},{1,3},{2,0},{3,1},{4,6},{5,7},{6,4},{7,5},{8,10},{9,11},{10,... | collective-permute-start | bytes 258056 | tf_op jit(solution)/shard_map/ppermute | solution.py:545
  6.1 3.8 %collective-permute-start.3 = (bf16[80,128]{1,0:T(8,128)(2,1)S(1)}, bf16[80,128]{1,0:T(8,128)(2,1)S(1)}, u32[]{:S(2)}, u32[]{:S(2)}) collective-permute-start(bf16[80,128]{1,0:T(8,128)(2,1)S(1)} %get-tuple-element.62.refs_6_), channel_id=1, source_target_pairs={{0,12},{1,13},{2,14},{3,15},{4,8},{5,9},{6,10},{7,11},{8,4},{9,5},... | collective-permute-start | bytes 61448 | tf_op jit(solution)/shard_map/ppermute | solution.py:548
  10.0 0.6 %collective-permute-start.5 = (bf16[80,128]{1,0:T(8,128)(2,1)S(1)}, bf16[80,128]{1,0:T(8,128)(2,1)S(1)}, u32[]{:S(2)}, u32[]{:S(2)}) collective-permute-start(bf16[80,128]{1,0:T(8,128)(2,1)S(1)} %get-tuple-element.62.refs_6_), channel_id=1, source_target_pairs={{0,4},{1,5},{2,6},{3,7},{4,0},{5,1},{6,2},{7,3},{8,12},{9,13},{10,... | collective-permute-start | bytes 61448 | tf_op jit(solution)/shard_map/ppermute | solution.py:548
  10.5 0.3 collective-permute-done.2.refs_9_
  10.8 3.0 %shard_map.130 = (bf16[1024,128]{1,0:T(8,128)(2,1)S(1)}, bf16[1024,1024]{1,0:T(8,128)(2,1)S(1)}, bf16[128,1024]{1,0:T(8,128)(2,1)S(1)}, bf16[128,1024]{1,0:T(8,1...) custom-call(s32[12]{0:T(128)S(1)} %copy-done.3, ...), custom_call_target="tpu_custom_call" | custom-call | flops 2000000000 | bytes 4000000 | tf_op jit(solution)/shard_map/pallas_call | solution.py:523
  13.8 0.8 %collective-permute-done.4.refs_4_ = bf16[80,128]{1,0:T(8,128)(2,1)S(1)} collective-permute-done((bf16[80,128]{1,0:T(8,128)(2,1)S(1)}, bf16[80,128]{1,0:T(8,128)(2,1)S(1)}, u32[]{:S(2)}, u32[]{:S(2)}) %collective-permute-start.4) | collective-permute-done | bytes 20512 | tf_op jit(solution)/shard_map/ppermute | solution.py:548
  14.6 1.8 %shard_map.131 = (bf16[80,128]{1,0:T(8,128)(2,1)S(1)}, bf16[80,128]{1,0:T(8,128)(2,1)S(1)}, bf16[80,128]{1,0:T(8,128)(2,1)S(1)}, bf16[80,128]{1,0:T(8,128)(2,1)S...) custom-call(s32[12]{0:T(128)S(1)} %copy-done.3, ...), custom_call_target="tpu_custom_call" | custom-call | flops 2000000000 | bytes 4000000 | tf_op jit(solution)/shard_map/pallas_call | solution.py:523
  16.4 3.5 %shard_map.132 = (bf16[336,128]{1,0:T(8,128)(2,1)S(1)}, bf16[336,128]{1,0:T(8,128)(2,1)S(1)}, bf16[672,128]{1,0:T(8,128)(2,1)S(1)}, bf16[256,128]{1,0:T(8,128)(2...) custom-call(s32[12]{0:T(128)S(1)} %copy-done.3, s32[12]{0:T(128)S(1)} %copy-done.4, ...), custom_call_target="tpu_custom_call" | custom-call | flops 4000000000 | bytes 8000000 | tf_op jit(solution)/shard_map/pallas_call | solution.py:523
  20.0 1.6 %collective-permute-start.16 = (bf16[512,128]{1,0:T(8,128)(2,1)S(1)}, bf16[512,128]{1,0:T(8,128)(2,1)S(1)}, u32[]{:S(2)}, u32[]{:S(2)}) collective-permute-start(bf16[512,128]{1,0:T(8,128)(2,1)S(1)} %get-tuple-element.85), channel_id=1, source_target_pairs={{0,2},{1,3},{2,0},{3,1},{4,6},{5,7},{6,4},{7,5},{8,10},{9,11},{10,... | collective-permute-start | bytes 393224 | tf_op jit(solution)/shard_map/ppermute | solution.py:545
  21.6 1.4 %collective-permute-start.7 = (bf16[336,128]{1,0:T(8,128)(2,1)S(1)}, bf16[336,128]{1,0:T(8,128)(2,1)S(1)}, u32[]{:S(2)}, u32[]{:S(2)}) collective-permute-start(bf16[336,128]{1,0:T(8,128)(2,1)S(1)} %get-tuple-element.72), channel_id=1, source_target_pairs={{0,2},{1,3},{2,0},{3,1},{4,6},{5,7},{6,4},{7,5},{8,10},{9,11},{10,... | collective-permute-start | bytes 258056 | tf_op jit(solution)/shard_map/ppermute | solution.py:545
  23.0 2.0 %collective-permute-start.10 = (bf16[80,128]{1,0:T(8,128)(2,1)S(1)}, bf16[80,128]{1,0:T(8,128)(2,1)S(1)}, u32[]{:S(2)}, u32[]{:S(2)}) collective-permute-start(bf16[80,128]{1,0:T(8,128)(2,1)S(1)} %get-tuple-element.77), channel_id=1, source_target_pairs={{0,8},{1,9},{2,10},{3,11},{4,12},{5,13},{6,14},{7,15},{8,0},{9,1},... | collective-permute-start | bytes 61448 | tf_op jit(solution)/shard_map/ppermute | solution.py:548
  25.0 1.1 %collective-permute-start.11 = (bf16[80,128]{1,0:T(8,128)(2,1)S(1)}, bf16[80,128]{1,0:T(8,128)(2,1)S(1)}, u32[]{:S(2)}, u32[]{:S(2)}) collective-permute-start(bf16[80,128]{1,0:T(8,128)(2,1)S(1)} %get-tuple-element.78), channel_id=1, source_target_pairs={{0,12},{1,13},{2,14},{3,15},{4,8},{5,9},{6,10},{7,11},{8,4},{9,5},... | collective-permute-start | bytes 61448 | tf_op jit(solution)/shard_map/ppermute | solution.py:548
  26.2 0.5 %collective-permute-start.9 = (bf16[80,128]{1,0:T(8,128)(2,1)S(1)}, bf16[80,128]{1,0:T(8,128)(2,1)S(1)}, u32[]{:S(2)}, u32[]{:S(2)}) collective-permute-start(bf16[80,128]{1,0:T(8,128)(2,1)S(1)} %get-tuple-element.76), channel_id=1, source_target_pairs={{0,4},{1,5},{2,6},{3,7},{4,0},{5,1},{6,2},{7,3},{8,12},{9,13},{10,... | collective-permute-start | bytes 61448 | tf_op jit(solution)/shard_map/ppermute | solution.py:548
  26.7 1.1 %collective-permute-done.7.theirs_ref.refs_3_ = bf16[336,128]{1,0:T(8,128)(2,1)S(1)} collective-permute-done((bf16[336,128]{1,0:T(8,128)(2,1)S(1)}, bf16[336,128]{1,0:T(8,128)(2,1)S(1)}, u32[]{:S(2)}, u32[]{:S(2)}) %collective-permute-start.7) | collective-permute-done | bytes 86048 | tf_op jit(solution)/shard_map/ppermute | solution.py:545
  27.8 2.2 %collective-permute-start.8 = (bf16[256,128]{1,0:T(8,128)(2,1)S(1)}, bf16[256,128]{1,0:T(8,128)(2,1)S(1)}, u32[]{:S(2)}, u32[]{:S(2)}) collective-permute-start(bf16[256,128]{1,0:T(8,128)(2,1)S(1)} %shard_map.134.w0), channel_id=1, source_target_pairs={{0,8},{1,9},{2,10},{3,11},{4,12},{5,13},{6,14},{7,15},{8,0},{9,1},... | collective-permute-start | bytes 196616 | tf_op jit(solution)/shard_map/ppermute | solution.py:548
  30.1 0.6 %collective-permute-done.11.refs_7_ = bf16[80,128]{1,0:T(8,128)(2,1)S(1)} collective-permute-done((bf16[80,128]{1,0:T(8,128)(2,1)S(1)}, bf16[80,128]{1,0:T(8,128)(2,1)S(1)}, u32[]{:S(2)}, u32[]{:S(2)}) %collective-permute-start.11) | collective-permute-done | bytes 20512 | tf_op jit(solution)/shard_map/ppermute | solution.py:548
  30.6 0.5 %shard_map.135 = (bf16[320,64]{1,0:T(8,128)(2,1)S(1)}, bf16[128,128]{1,0:T(8,128)(2,1)S(1)}) custom-call(bf16[512,512]{1,0:T(8,128)(2,1)S(1)} %get-tuple-element.73.refs_0_, bf16[320,256]{1,0:T(8,128)(2,1)S(1)} %get-tuple-element.74.refs_1_, f32[336,128]{1,0:T(8,128)S(1)} %get-tuple-element.71.mine_ref.refs_2_, ...), custom_call_target="tpu_custom_call" | custom-call | flops 1000000000 | bytes 2000000 | tf_op jit(solution)/shard_map/pallas_call | solution.py:523
  31.2 1.3 %collective-permute-start.13 = (bf16[128,128]{1,0:T(8,128)(2,1)S(1)}, bf16[128,128]{1,0:T(8,128)(2,1)S(1)}, u32[]{:S(2)}, u32[]{:S(2)}) collective-permute-start(bf16[128,128]{1,0:T(8,128)(2,1)S(1)} %get-tuple-element.79.fm_ref), channel_id=1, source_target_pairs={{0,8},{1,9},{2,10},{3,11},{4,12},{5,13},{6,14},{7,15},{8,0},{9,1},... | collective-permute-start | bytes 98312 | tf_op jit(solution)/shard_map/ppermute | solution.py:548
  32.5 2.1 %collective-permute-start.14 = (bf16[128,128]{1,0:T(8,128)(2,1)S(1)}, bf16[128,128]{1,0:T(8,128)(2,1)S(1)}, u32[]{:S(2)}, u32[]{:S(2)}) collective-permute-start(bf16[128,128]{1,0:T(8,128)(2,1)S(1)} %get-tuple-element.79.fm_ref), channel_id=1, source_target_pairs={{0,12},{1,13},{2,14},{3,15},{4,8},{5,9},{6,10},{7,11},{8,4},{9,5},... | collective-permute-start | bytes 98312 | tf_op jit(solution)/shard_map/ppermute | solution.py:548
  34.6 0.4 collective-permute-done.8.w1
  35.0 0.3 collective-permute-start.12
  35.3 1.9 %shard_map.137 = bf16[80,8,256]{2,1,0:T(8,128)(2,1)} custom-call(s32[12]{0:T(128)S(1)} %copy-done.3, s32[12]{0:T(128)S(1)} %copy-done.4, bf16[320,64]{1,0:T(8,128)(2,1)S(1)} %get-tuple-element.80.pg_ref, bf16[64,256]{1,0:T(8,128)(2,1)S(1)} %bitcast.7, f32[1,256]{1,0:T(1,128)S(1)} %bitcast.9, f32[640,256]{1,0:T(8,128)S(1)} %get-tuple-element.81.hat_ref, ...), custom_call_target="tpu_custom_call" | custom-call | flops 1000000000 | bytes 2000000 | tf_op jit(solution)/shard_map/pallas_call | solution.py:523
  37.2 1.0 %shard_map.138 = bf16[8,128,128]{2,1,0:T(8,128)(2,1)} custom-call(bf16[256,128]{1,0:T(8,128)(2,1)S(1)} %get-tuple-element.83.refs_0_, bf16[256,128]{1,0:T(8,128)(2,1)S(1)} %collective-permute-done.15.refs_1_, bf16[512,128]{1,0:T(8,128)(2,1)S(1)} %collective-permute-done.16.refs_2_, bf16[512,128]{1,0:T(8,128)(2,1)S(1)} %collective-permute-done.17.refs_3_), custom_call_target="tpu_custom_call" | custom-call | flops 1000000000 | bytes 2000000 | tf_op jit(solution)/shard_map/pallas_call | solution.py:523
  38.2 0.1 collective-permute-done.14.refs_3_
  38.3 1.4 %collective-permute-done.12.refs_1_ = bf16[384,128]{1,0:T(8,128)(2,1)S(1)} collective-permute-done((bf16[384,128]{1,0:T(8,128)(2,1)S(1)}, bf16[384,128]{1,0:T(8,128)(2,1)S(1)}, u32[]{:S(2)}, u32[]{:S(2)}) %collective-permute-start.12) | collective-permute-done | bytes 98336 | tf_op jit(solution)/shard_map/ppermute | solution.py:548
  39.8 1.6 %collective-permute-start.18 = (bf16[384,128]{1,0:T(8,128)(2,1)S(1)}, bf16[384,128]{1,0:T(8,128)(2,1)S(1)}, u32[]{:S(2)}, u32[]{:S(2)}) collective-permute-start(bf16[384,128]{1,0:T(8,128)(2,1)S(1)} %shard_map.139.own_ref), channel_id=1, source_target_pairs={{0,2},{1,3},{2,0},{3,1},{4,6},{5,7},{6,4},{7,5},{8,10},{9,11},{10,... | collective-permute-start | bytes 294920 | tf_op jit(solution)/shard_map/ppermute | solution.py:545
  41.3 3.1 %collective-permute-done.18.cross_ref = bf16[384,128]{1,0:T(8,128)(2,1)S(1)} collective-permute-done((bf16[384,128]{1,0:T(8,128)(2,1)S(1)}, bf16[384,128]{1,0:T(8,128)(2,1)S(1)}, u32[]{:S(2)}, u32[]{:S(2)}) %collective-permute-start.18) | collective-permute-done | bytes 98336 | tf_op jit(solution)/shard_map/ppermute | solution.py:545
  44.5 0.1 collective-permute-start.19
  44.5 1.4 %collective-permute-done.19.core_ref = bf16[640,128]{1,0:T(8,128)(2,1)S(1)} collective-permute-done((bf16[640,128]{1,0:T(8,128)(2,1)S(1)}, bf16[640,128]{1,0:T(8,128)(2,1)S(1)}, u32[]{:S(2)}, u32[]{:S(2)}) %collective-permute-start.19) | collective-permute-done | bytes 163872 | tf_op jit(solution)/shard_map/ppermute | solution.py:545
  45.9 0.8 %shard_map.141 = (f32[1024,128]{1,0:T(8,128)}, f32[64,256]{1,0:T(8,128)}) custom-call(bf16[640,128]{1,0:T(8,128)(2,1)S(1)} %shard_map.140.mine_ref, bf16[640,128]{1,0:T(8,128)(2,1)S(1)} %collective-permute-done.19.core_ref), custom_call_target="tpu_custom_call" | custom-call | flops 100000000 | bytes 200000 | tf_op jit(solution)/shard_map/pallas_call | solution.py:523
  (31 shorter events, 0.3 us)
Async XLA Ops:
  0.6 10.2 %copy-start.3 = (s32[12]{0:T(128)S(1)}, s32[12]{0:T(128)}, u32[]{:S(2)}) copy-start(s32[12]{0:T(128)} %len_ref.1) | copy-start | bytes 148
  0.6 10.2 %copy-start.4 = (s32[12]{0:T(128)S(1)}, s32[12]{0:T(128)}, u32[]{:S(2)}) copy-start(s32[12]{0:T(128)} %hom_ref.1) | copy-start | bytes 148
  3.0 7.0 %collective-permute-start = (bf16[336,128]{1,0:T(8,128)(2,1)S(1)}, bf16[336,128]{1,0:T(8,128)(2,1)S(1)}, u32[]{:S(2)}, u32[]{:S(2)}) collective-permute-start(bf16[336,128]{1,0:T(8,128)(2,1)S(1)} %get-tuple-element.54), channel_id=1, source_target_pairs={{0,1},{1,0},{2,3},{3,2},{4,5},{5,4},{6,7},{7,6},{8,9},{9,8},{10,11... | collective-permute-start | bytes 258056 | tf_op jit(solution)/shard_map/ppermute | solution.py:545
  3.5 7.0 %collective-permute-start.1 = (bf16[336,128]{1,0:T(8,128)(2,1)S(1)}, bf16[336,128]{1,0:T(8,128)(2,1)S(1)}, u32[]{:S(2)}, u32[]{:S(2)}) collective-permute-start(bf16[336,128]{1,0:T(8,128)(2,1)S(1)} %get-tuple-element.55), channel_id=1, source_target_pairs={{0,2},{1,3},{2,0},{3,1},{4,6},{5,7},{6,4},{7,5},{8,10},{9,11},{10,... | collective-permute-start | bytes 258056 | tf_op jit(solution)/shard_map/ppermute | solution.py:545
  6.0 4.8 %collective-permute-start.2 = (bf16[336,128]{1,0:T(8,128)(2,1)S(1)}, bf16[336,128]{1,0:T(8,128)(2,1)S(1)}, u32[]{:S(2)}, u32[]{:S(2)}) collective-permute-start(bf16[336,128]{1,0:T(8,128)(2,1)S(1)} %get-tuple-element.56), channel_id=1, source_target_pairs={{0,3},{1,2},{2,1},{3,0},{4,7},{5,6},{6,5},{7,4},{8,11},{9,10},{10,... | collective-permute-start | bytes 258056 | tf_op jit(solution)/shard_map/ppermute | solution.py:545
  6.1 7.7 %collective-permute-start.3 = (bf16[80,128]{1,0:T(8,128)(2,1)S(1)}, bf16[80,128]{1,0:T(8,128)(2,1)S(1)}, u32[]{:S(2)}, u32[]{:S(2)}) collective-permute-start(bf16[80,128]{1,0:T(8,128)(2,1)S(1)} %get-tuple-element.62.refs_6_), channel_id=1, source_target_pairs={{0,12},{1,13},{2,14},{3,15},{4,8},{5,9},{6,10},{7,11},{8,4},{9,5},... | collective-permute-start | bytes 61448 | tf_op jit(solution)/shard_map/ppermute | solution.py:548
  9.9 4.7 %collective-permute-start.4 = (bf16[80,128]{1,0:T(8,128)(2,1)S(1)}, bf16[80,128]{1,0:T(8,128)(2,1)S(1)}, u32[]{:S(2)}, u32[]{:S(2)}) collective-permute-start(bf16[80,128]{1,0:T(8,128)(2,1)S(1)} %get-tuple-element.62.refs_6_), channel_id=1, source_target_pairs={{0,8},{1,9},{2,10},{3,11},{4,12},{5,13},{6,14},{7,15},{8,0},{9,1},... | collective-permute-start | bytes 61448 | tf_op jit(solution)/shard_map/ppermute | solution.py:548
  10.0 4.7 %collective-permute-start.5 = (bf16[80,128]{1,0:T(8,128)(2,1)S(1)}, bf16[80,128]{1,0:T(8,128)(2,1)S(1)}, u32[]{:S(2)}, u32[]{:S(2)}) collective-permute-start(bf16[80,128]{1,0:T(8,128)(2,1)S(1)} %get-tuple-element.62.refs_6_), channel_id=1, source_target_pairs={{0,4},{1,5},{2,6},{3,7},{4,0},{5,1},{6,2},{7,3},{8,12},{9,13},{10,... | collective-permute-start | bytes 61448 | tf_op jit(solution)/shard_map/ppermute | solution.py:548
  14.6 1.8 %copy-start.2 = (f32[128]{0:T(128)S(1)}, f32[128]{0:T(128)}, u32[]{:S(2)}) copy-start(f32[128]{0:T(128)} %param.16) | copy-start | bytes 1540
  19.9 1.6 %collective-permute-start.6 = (bf16[672,128]{1,0:T(8,128)(2,1)S(1)}, bf16[672,128]{1,0:T(8,128)(2,1)S(1)}, u32[]{:S(2)}, u32[]{:S(2)}) collective-permute-start(bf16[672,128]{1,0:T(8,128)(2,1)S(1)} %get-tuple-element.70), channel_id=1, source_target_pairs={{0,1},{1,0},{2,3},{3,2},{4,5},{5,4},{6,7},{7,6},{8,9},{9,8},{10,11... | collective-permute-start | bytes 516104 | tf_op jit(solution)/shard_map/ppermute | solution.py:545
  20.0 6.6 %collective-permute-start.16 = (bf16[512,128]{1,0:T(8,128)(2,1)S(1)}, bf16[512,128]{1,0:T(8,128)(2,1)S(1)}, u32[]{:S(2)}, u32[]{:S(2)}) collective-permute-start(bf16[512,128]{1,0:T(8,128)(2,1)S(1)} %get-tuple-element.85), channel_id=1, source_target_pairs={{0,2},{1,3},{2,0},{3,1},{4,6},{5,7},{6,4},{7,5},{8,10},{9,11},{10,... | collective-permute-start | bytes 393224 | tf_op jit(solution)/shard_map/ppermute | solution.py:545
  21.6 6.2 %collective-permute-start.7 = (bf16[336,128]{1,0:T(8,128)(2,1)S(1)}, bf16[336,128]{1,0:T(8,128)(2,1)S(1)}, u32[]{:S(2)}, u32[]{:S(2)}) collective-permute-start(bf16[336,128]{1,0:T(8,128)(2,1)S(1)} %get-tuple-element.72), channel_id=1, source_target_pairs={{0,2},{1,3},{2,0},{3,1},{4,6},{5,7},{6,4},{7,5},{8,10},{9,11},{10,... | collective-permute-start | bytes 258056 | tf_op jit(solution)/shard_map/ppermute | solution.py:545
  23.0 4.8 %collective-permute-start.10 = (bf16[80,128]{1,0:T(8,128)(2,1)S(1)}, bf16[80,128]{1,0:T(8,128)(2,1)S(1)}, u32[]{:S(2)}, u32[]{:S(2)}) collective-permute-start(bf16[80,128]{1,0:T(8,128)(2,1)S(1)} %get-tuple-element.77), channel_id=1, source_target_pairs={{0,8},{1,9},{2,10},{3,11},{4,12},{5,13},{6,14},{7,15},{8,0},{9,1},... | collective-permute-start | bytes 61448 | tf_op jit(solution)/shard_map/ppermute | solution.py:548
  25.0 5.6 %collective-permute-start.11 = (bf16[80,128]{1,0:T(8,128)(2,1)S(1)}, bf16[80,128]{1,0:T(8,128)(2,1)S(1)}, u32[]{:S(2)}, u32[]{:S(2)}) collective-permute-start(bf16[80,128]{1,0:T(8,128)(2,1)S(1)} %get-tuple-element.78), channel_id=1, source_target_pairs={{0,12},{1,13},{2,14},{3,15},{4,8},{5,9},{6,10},{7,11},{8,4},{9,5},... | collective-permute-start | bytes 61448 | tf_op jit(solution)/shard_map/ppermute | solution.py:548
  26.2 4.5 %collective-permute-start.9 = (bf16[80,128]{1,0:T(8,128)(2,1)S(1)}, bf16[80,128]{1,0:T(8,128)(2,1)S(1)}, u32[]{:S(2)}, u32[]{:S(2)}) collective-permute-start(bf16[80,128]{1,0:T(8,128)(2,1)S(1)} %get-tuple-element.76), channel_id=1, source_target_pairs={{0,4},{1,5},{2,6},{3,7},{4,0},{5,1},{6,2},{7,3},{8,12},{9,13},{10,... | collective-permute-start | bytes 61448 | tf_op jit(solution)/shard_map/ppermute | solution.py:548
  26.6 10.6 %collective-permute-start.15 = (bf16[256,128]{1,0:T(8,128)(2,1)S(1)}, bf16[256,128]{1,0:T(8,128)(2,1)S(1)}, u32[]{:S(2)}, u32[]{:S(2)}) collective-permute-start(bf16[256,128]{1,0:T(8,128)(2,1)S(1)} %get-tuple-element.84), channel_id=1, source_target_pairs={{0,1},{1,0},{2,3},{3,2},{4,5},{5,4},{6,7},{7,6},{8,9},{9,8},{10,11... | collective-permute-start | bytes 196616 | tf_op jit(solution)/shard_map/ppermute | solution.py:545
  27.8 9.4 %collective-permute-start.17 = (bf16[512,128]{1,0:T(8,128)(2,1)S(1)}, bf16[512,128]{1,0:T(8,128)(2,1)S(1)}, u32[]{:S(2)}, u32[]{:S(2)}) collective-permute-start(bf16[512,128]{1,0:T(8,128)(2,1)S(1)} %collective-permute-done.16.refs_2_), channel_id=1, source_target_pairs={{0,1},{1,0},{2,3},{3,2},{4,5},{5,4},{6,7},{7,6},{8,9},{9,8},{10,11... | collective-permute-start | bytes 393224 | tf_op jit(solution)/shard_map/ppermute | solution.py:545
  27.8 7.6 %copy-start = (bf16[256,64]{0,1:T(8,128)(2,1)S(1)}, bf16[256,64]{0,1:T(8,128)(2,1)}, u32[]{:S(2)}) copy-start(bf16[256,64]{0,1:T(8,128)(2,1)} %param.13) | copy-start | bytes 98308
  27.8 7.6 %copy-start.1 = (f32[256]{0:T(256)S(1)}, f32[256]{0:T(256)}, u32[]{:S(2)}) copy-start(f32[256]{0:T(256)} %param.11) | copy-start | bytes 3076
  27.8 7.2 %collective-permute-start.8 = (bf16[256,128]{1,0:T(8,128)(2,1)S(1)}, bf16[256,128]{1,0:T(8,128)(2,1)S(1)}, u32[]{:S(2)}, u32[]{:S(2)}) collective-permute-start(bf16[256,128]{1,0:T(8,128)(2,1)S(1)} %shard_map.134.w0), channel_id=1, source_target_pairs={{0,8},{1,9},{2,10},{3,11},{4,12},{5,13},{6,14},{7,15},{8,0},{9,1},... | collective-permute-start | bytes 196616 | tf_op jit(solution)/shard_map/ppermute | solution.py:548
  31.2 7.1 %collective-permute-start.13 = (bf16[128,128]{1,0:T(8,128)(2,1)S(1)}, bf16[128,128]{1,0:T(8,128)(2,1)S(1)}, u32[]{:S(2)}, u32[]{:S(2)}) collective-permute-start(bf16[128,128]{1,0:T(8,128)(2,1)S(1)} %get-tuple-element.79.fm_ref), channel_id=1, source_target_pairs={{0,8},{1,9},{2,10},{3,11},{4,12},{5,13},{6,14},{7,15},{8,0},{9,1},... | collective-permute-start | bytes 98312 | tf_op jit(solution)/shard_map/ppermute | solution.py:548
  32.5 5.8 %collective-permute-start.14 = (bf16[128,128]{1,0:T(8,128)(2,1)S(1)}, bf16[128,128]{1,0:T(8,128)(2,1)S(1)}, u32[]{:S(2)}, u32[]{:S(2)}) collective-permute-start(bf16[128,128]{1,0:T(8,128)(2,1)S(1)} %get-tuple-element.79.fm_ref), channel_id=1, source_target_pairs={{0,12},{1,13},{2,14},{3,15},{4,8},{5,9},{6,10},{7,11},{8,4},{9,5},... | collective-permute-start | bytes 98312 | tf_op jit(solution)/shard_map/ppermute | solution.py:548
  35.0 4.7 %collective-permute-start.12 = (bf16[384,128]{1,0:T(8,128)(2,1)S(1)}, bf16[384,128]{1,0:T(8,128)(2,1)S(1)}, u32[]{:S(2)}, u32[]{:S(2)}) collective-permute-start(bf16[384,128]{1,0:T(8,128)(2,1)S(1)} %shard_map.136.refs_0_), channel_id=1, source_target_pairs={{0,4},{1,5},{2,6},{3,7},{4,0},{5,1},{6,2},{7,3},{8,12},{9,13},{10,... | collective-permute-start | bytes 294920 | tf_op jit(solution)/shard_map/ppermute | solution.py:548
  39.8 4.7 %collective-permute-start.18 = (bf16[384,128]{1,0:T(8,128)(2,1)S(1)}, bf16[384,128]{1,0:T(8,128)(2,1)S(1)}, u32[]{:S(2)}, u32[]{:S(2)}) collective-permute-start(bf16[384,128]{1,0:T(8,128)(2,1)S(1)} %shard_map.139.own_ref), channel_id=1, source_target_pairs={{0,2},{1,3},{2,0},{3,1},{4,6},{5,7},{6,4},{7,5},{8,10},{9,11},{10,... | collective-permute-start | bytes 294920 | tf_op jit(solution)/shard_map/ppermute | solution.py:545
  44.5 1.5 %collective-permute-start.19 = (bf16[640,128]{1,0:T(8,128)(2,1)S(1)}, bf16[640,128]{1,0:T(8,128)(2,1)S(1)}, u32[]{:S(2)}, u32[]{:S(2)}) collective-permute-start(bf16[640,128]{1,0:T(8,128)(2,1)S(1)} %shard_map.140.mine_ref), channel_id=1, source_target_pairs={{0,1},{1,0},{2,3},{3,2},{4,5},{5,4},{6,7},{7,6},{8,9},{9,8},{10,11... | collective-permute-start | bytes 491528 | tf_op jit(solution)/shard_map/ppermute | solution.py:545

commit v5 on v4

--- a/solution.py
+++ b/solution.py
@@ -494,19 +494,12 @@
     out_ref[256:384, :] = total([f[f.shape[0] - 128 :, :] for f in fms]).astype(BF16)
 
 
-def relay_kernel(own_ref, cross_ref, out_ref):
-    out_ref[0:256, :] = own_ref[0:256, :]
-    out_ref[256:512, :] = cross_ref[0:256, :]
-    out_ref[512:640, :] = total([own_ref[256:384, :], cross_ref[256:384, :]]).astype(BF16)
-
-
-def final_kernel(mine_ref, core_ref, w_ref, fm_ref):
+def final_kernel(m0, m1, m2, m3, w_ref, fm_ref):
     _, b = place()
-    for t in range(QUAD):
+    for t, m in enumerate((m0, m1, m2, m3)):
         rows = pl.ds(pl.multiple_of((b ^ t) * 256, 256), 256)
-        ref, top = (mine_ref, core_ref)[t & 1], (t >> 1) * 256
-        w_ref[rows, :] = ref[top : top + 256, :].astype(F32)
-    fm = total([mine_ref[512:640, :], core_ref[512:640, :]])
+        w_ref[rows, :] = m[0:256, :].astype(F32)
+    fm = total([m[256:384, :] for m in (m0, m1, m2, m3)])
     fm_ref[...] = jnp.concatenate([fm[0:64], fm[64:128]], axis=1)
 
 
@@ -680,11 +673,11 @@
     merged = call(
         merge_kernel, sds((384, 128), BF16), parts, work=10**7
     )
-    relay = call(relay_kernel, sds((640, 128), BF16), [merged, near(merged, 2)], work=10**7)
+    cross = near(merged, 2)
     w, fm = call(
         final_kernel,
         [sds((1024, 128), F32), sds((64, 256), F32)],
-        [relay, near(relay, 1)],
+        [merged, near(merged, 1), cross, near(cross, 1)],
         work=10**8,
     )
     return pair_delta, alignment_gradient, w, fm.T

time: 46.9 us -> 46.7 us (level)
    ppermute x10 -> x11, waiting for transfers between devices: 5.9 us -> 5.82 us  [near(): return lax.ppermute(value, 'row', [(k, k ^ t) for k in range(devices)])]
    ppermute x10 -> x11, starting transfers between devices: 7.82 us -> 7.75 us  [near(): return lax.ppermute(value, 'row', [(k, k ^ t) for k in range(devices)])]
    pallas_call x13 -> x12, Pallas kernels: 15 us -> 14.9 us  [call(): pl.pallas_call(kernel, out_shape=outs, in_specs=in_specs if in_specs is n...]
  transfers between devices with their start and end apart: 20 -> 21, of which waited for: 9 -> 9; matrix products, arithmetic and copies ran while one was open for 0% -> 0% of each run, Pallas kernels for 14% -> 14%
where the time goes in v5:
time: 46.7 us; the launch traced here: 46.6 us
  starting transfers between devices  21.8 us (47%)
  Pallas kernels  14.9 us (32%)
  waiting for transfers between devices  9.12 us (20%)
  between operations  0.74 us (2%)
    pallas_call x12, Pallas kernels, call(): pl.pallas_call(kernel, out_shape=outs, in_specs=in_specs if in_specs is n...  14.9 us
    ppermute x10, starting transfers between devices, far(): return lax.ppermute(value, 'row', [(k, k ^ 4 * u) for k in range(devices)])  14 us
    ppermute x11, starting transfers between devices, near(): return lax.ppermute(value, 'row', [(k, k ^ t) for k in range(devices)])  7.75 us
    ppermute x11, waiting for transfers between devices, near(): return lax.ppermute(value, 'row', [(k, k ^ t) for k in range(devices)])  5.82 us
    ppermute x10, waiting for transfers between devices, far(): return lax.ppermute(value, 'row', [(k, k ^ 4 * u) for k in range(devices)])  3.3 us
  transfers between devices with their start and end apart: 21, of which 9 were waited for; matrix products, arithmetic and copies ran while one was open for 0% of the time, Pallas kernels for 14%

profile of v5, /device:TPU:0, one launch (start us, length us, event | category | flops | bytes accessed | tf_op | source)
XLA Modules:
  0.0 46.6 jit_solution(3355975993996472918)
XLA Ops:
  0.7 2.3 %shard_map.129 = (bf16[336,128]{1,0:T(8,128)(2,1)S(1)}, bf16[336,128]{1,0:T(8,128)(2,1)S(1)}, bf16[336,128]{1,0:T(8,128)(2,1)S(1)}, bf16[336,128]{1,0:T(8,128)(2...) custom-call(bf16[80,8,256]{2,1,0:T(8,128)(2,1)} %x_hbm.1, ...), custom_call_target="tpu_custom_call" | custom-call | flops 1000000000 | bytes 2000000 | tf_op jit(solution)/shard_map/pallas_call | solution.py:516
  3.0 0.5 %collective-permute-start = (bf16[336,128]{1,0:T(8,128)(2,1)S(1)}, bf16[336,128]{1,0:T(8,128)(2,1)S(1)}, u32[]{:S(2)}, u32[]{:S(2)}) collective-permute-start(bf16[336,128]{1,0:T(8,128)(2,1)S(1)} %get-tuple-element.54), channel_id=1, source_target_pairs={{0,1},{1,0},{2,3},{3,2},{4,5},{5,4},{6,7},{7,6},{8,9},{9,8},{10,11... | collective-permute-start | bytes 258056 | tf_op jit(solution)/shard_map/ppermute | solution.py:538
  3.5 2.6 %collective-permute-start.1 = (bf16[336,128]{1,0:T(8,128)(2,1)S(1)}, bf16[336,128]{1,0:T(8,128)(2,1)S(1)}, u32[]{:S(2)}, u32[]{:S(2)}) collective-permute-start(bf16[336,128]{1,0:T(8,128)(2,1)S(1)} %get-tuple-element.55), channel_id=1, source_target_pairs={{0,2},{1,3},{2,0},{3,1},{4,6},{5,7},{6,4},{7,5},{8,10},{9,11},{10,... | collective-permute-start | bytes 258056 | tf_op jit(solution)/shard_map/ppermute | solution.py:538
  6.1 3.8 %collective-permute-start.3 = (bf16[80,128]{1,0:T(8,128)(2,1)S(1)}, bf16[80,128]{1,0:T(8,128)(2,1)S(1)}, u32[]{:S(2)}, u32[]{:S(2)}) collective-permute-start(bf16[80,128]{1,0:T(8,128)(2,1)S(1)} %get-tuple-element.62.refs_6_), channel_id=1, source_target_pairs={{0,12},{1,13},{2,14},{3,15},{4,8},{5,9},{6,10},{7,11},{8,4},{9,5},... | collective-permute-start | bytes 61448 | tf_op jit(solution)/shard_map/ppermute | solution.py:541
  10.0 0.6 %collective-permute-start.5 = (bf16[80,128]{1,0:T(8,128)(2,1)S(1)}, bf16[80,128]{1,0:T(8,128)(2,1)S(1)}, u32[]{:S(2)}, u32[]{:S(2)}) collective-permute-start(bf16[80,128]{1,0:T(8,128)(2,1)S(1)} %get-tuple-element.62.refs_6_), channel_id=1, source_target_pairs={{0,4},{1,5},{2,6},{3,7},{4,0},{5,1},{6,2},{7,3},{8,12},{9,13},{10,... | collective-permute-start | bytes 61448 | tf_op jit(solution)/shard_map/ppermute | solution.py:541
  10.5 0.3 collective-permute-done.2.refs_9_
  10.8 3.0 %shard_map.130 = (bf16[1024,128]{1,0:T(8,128)(2,1)S(1)}, bf16[1024,1024]{1,0:T(8,128)(2,1)S(1)}, bf16[128,1024]{1,0:T(8,128)(2,1)S(1)}, bf16[128,1024]{1,0:T(8,1...) custom-call(s32[12]{0:T(128)S(1)} %copy-done.3, ...), custom_call_target="tpu_custom_call" | custom-call | flops 2000000000 | bytes 4000000 | tf_op jit(solution)/shard_map/pallas_call | solution.py:516
  13.8 0.8 %collective-permute-done.4.refs_4_ = bf16[80,128]{1,0:T(8,128)(2,1)S(1)} collective-permute-done((bf16[80,128]{1,0:T(8,128)(2,1)S(1)}, bf16[80,128]{1,0:T(8,128)(2,1)S(1)}, u32[]{:S(2)}, u32[]{:S(2)}) %collective-permute-start.4) | collective-permute-done | bytes 20512 | tf_op jit(solution)/shard_map/ppermute | solution.py:541
  14.6 1.8 %shard_map.131 = (bf16[80,128]{1,0:T(8,128)(2,1)S(1)}, bf16[80,128]{1,0:T(8,128)(2,1)S(1)}, bf16[80,128]{1,0:T(8,128)(2,1)S(1)}, bf16[80,128]{1,0:T(8,128)(2,1)S...) custom-call(s32[12]{0:T(128)S(1)} %copy-done.3, ...), custom_call_target="tpu_custom_call" | custom-call | flops 2000000000 | bytes 4000000 | tf_op jit(solution)/shard_map/pallas_call | solution.py:516
  16.4 3.5 %shard_map.132 = (bf16[336,128]{1,0:T(8,128)(2,1)S(1)}, bf16[336,128]{1,0:T(8,128)(2,1)S(1)}, bf16[672,128]{1,0:T(8,128)(2,1)S(1)}, bf16[256,128]{1,0:T(8,128)(2...) custom-call(s32[12]{0:T(128)S(1)} %copy-done.3, s32[12]{0:T(128)S(1)} %copy-done.4, ...), custom_call_target="tpu_custom_call" | custom-call | flops 4000000000 | bytes 8000000 | tf_op jit(solution)/shard_map/pallas_call | solution.py:516
  19.9 0.1 collective-permute-start.6
  20.0 1.6 %collective-permute-start.16 = (bf16[512,128]{1,0:T(8,128)(2,1)S(1)}, bf16[512,128]{1,0:T(8,128)(2,1)S(1)}, u32[]{:S(2)}, u32[]{:S(2)}) collective-permute-start(bf16[512,128]{1,0:T(8,128)(2,1)S(1)} %get-tuple-element.85), channel_id=1, source_target_pairs={{0,2},{1,3},{2,0},{3,1},{4,6},{5,7},{6,4},{7,5},{8,10},{9,11},{10,... | collective-permute-start | bytes 393224 | tf_op jit(solution)/shard_map/ppermute | solution.py:538
  21.6 1.4 %collective-permute-start.7 = (bf16[336,128]{1,0:T(8,128)(2,1)S(1)}, bf16[336,128]{1,0:T(8,128)(2,1)S(1)}, u32[]{:S(2)}, u32[]{:S(2)}) collective-permute-start(bf16[336,128]{1,0:T(8,128)(2,1)S(1)} %get-tuple-element.72), channel_id=1, source_target_pairs={{0,2},{1,3},{2,0},{3,1},{4,6},{5,7},{6,4},{7,5},{8,10},{9,11},{10,... | collective-permute-start | bytes 258056 | tf_op jit(solution)/shard_map/ppermute | solution.py:538
  23.0 2.0 %collective-permute-start.10 = (bf16[80,128]{1,0:T(8,128)(2,1)S(1)}, bf16[80,128]{1,0:T(8,128)(2,1)S(1)}, u32[]{:S(2)}, u32[]{:S(2)}) collective-permute-start(bf16[80,128]{1,0:T(8,128)(2,1)S(1)} %get-tuple-element.77), channel_id=1, source_target_pairs={{0,8},{1,9},{2,10},{3,11},{4,12},{5,13},{6,14},{7,15},{8,0},{9,1},... | collective-permute-start | bytes 61448 | tf_op jit(solution)/shard_map/ppermute | solution.py:541
  25.0 1.1 %collective-permute-start.11 = (bf16[80,128]{1,0:T(8,128)(2,1)S(1)}, bf16[80,128]{1,0:T(8,128)(2,1)S(1)}, u32[]{:S(2)}, u32[]{:S(2)}) collective-permute-start(bf16[80,128]{1,0:T(8,128)(2,1)S(1)} %get-tuple-element.78), channel_id=1, source_target_pairs={{0,12},{1,13},{2,14},{3,15},{4,8},{5,9},{6,10},{7,11},{8,4},{9,5},... | collective-permute-start | bytes 61448 | tf_op jit(solution)/shard_map/ppermute | solution.py:541
  26.2 0.5 %collective-permute-start.9 = (bf16[80,128]{1,0:T(8,128)(2,1)S(1)}, bf16[80,128]{1,0:T(8,128)(2,1)S(1)}, u32[]{:S(2)}, u32[]{:S(2)}) collective-permute-start(bf16[80,128]{1,0:T(8,128)(2,1)S(1)} %get-tuple-element.76), channel_id=1, source_target_pairs={{0,4},{1,5},{2,6},{3,7},{4,0},{5,1},{6,2},{7,3},{8,12},{9,13},{10,... | collective-permute-start | bytes 61448 | tf_op jit(solution)/shard_map/ppermute | solution.py:541
  26.7 1.1 %collective-permute-done.7.theirs_ref.refs_3_ = bf16[336,128]{1,0:T(8,128)(2,1)S(1)} collective-permute-done((bf16[336,128]{1,0:T(8,128)(2,1)S(1)}, bf16[336,128]{1,0:T(8,128)(2,1)S(1)}, u32[]{:S(2)}, u32[]{:S(2)}) %collective-permute-start.7) | collective-permute-done | bytes 86048 | tf_op jit(solution)/shard_map/ppermute | solution.py:538
  27.8 2.2 %collective-permute-start.8 = (bf16[256,128]{1,0:T(8,128)(2,1)S(1)}, bf16[256,128]{1,0:T(8,128)(2,1)S(1)}, u32[]{:S(2)}, u32[]{:S(2)}) collective-permute-start(bf16[256,128]{1,0:T(8,128)(2,1)S(1)} %shard_map.134.w0), channel_id=1, source_target_pairs={{0,8},{1,9},{2,10},{3,11},{4,12},{5,13},{6,14},{7,15},{8,0},{9,1},... | collective-permute-start | bytes 196616 | tf_op jit(solution)/shard_map/ppermute | solution.py:541
  30.1 0.6 %collective-permute-done.11.refs_7_ = bf16[80,128]{1,0:T(8,128)(2,1)S(1)} collective-permute-done((bf16[80,128]{1,0:T(8,128)(2,1)S(1)}, bf16[80,128]{1,0:T(8,128)(2,1)S(1)}, u32[]{:S(2)}, u32[]{:S(2)}) %collective-permute-start.11) | collective-permute-done | bytes 20512 | tf_op jit(solution)/shard_map/ppermute | solution.py:541
  30.6 0.5 %shard_map.135 = (bf16[320,64]{1,0:T(8,128)(2,1)S(1)}, bf16[128,128]{1,0:T(8,128)(2,1)S(1)}) custom-call(bf16[512,512]{1,0:T(8,128)(2,1)S(1)} %get-tuple-element.73.refs_0_, bf16[320,256]{1,0:T(8,128)(2,1)S(1)} %get-tuple-element.74.refs_1_, f32[336,128]{1,0:T(8,128)S(1)} %get-tuple-element.71.mine_ref.refs_2_, ...), custom_call_target="tpu_custom_call" | custom-call | flops 1000000000 | bytes 2000000 | tf_op jit(solution)/shard_map/pallas_call | solution.py:516
  31.2 1.3 %collective-permute-start.13 = (bf16[128,128]{1,0:T(8,128)(2,1)S(1)}, bf16[128,128]{1,0:T(8,128)(2,1)S(1)}, u32[]{:S(2)}, u32[]{:S(2)}) collective-permute-start(bf16[128,128]{1,0:T(8,128)(2,1)S(1)} %get-tuple-element.79.fm_ref), channel_id=1, source_target_pairs={{0,8},{1,9},{2,10},{3,11},{4,12},{5,13},{6,14},{7,15},{8,0},{9,1},... | collective-permute-start | bytes 98312 | tf_op jit(solution)/shard_map/ppermute | solution.py:541
  32.5 2.1 %collective-permute-start.14 = (bf16[128,128]{1,0:T(8,128)(2,1)S(1)}, bf16[128,128]{1,0:T(8,128)(2,1)S(1)}, u32[]{:S(2)}, u32[]{:S(2)}) collective-permute-start(bf16[128,128]{1,0:T(8,128)(2,1)S(1)} %get-tuple-element.79.fm_ref), channel_id=1, source_target_pairs={{0,12},{1,13},{2,14},{3,15},{4,8},{5,9},{6,10},{7,11},{8,4},{9,5},... | collective-permute-start | bytes 98312 | tf_op jit(solution)/shard_map/ppermute | solution.py:541
  34.6 0.4 collective-permute-done.8.w1
  35.0 0.3 collective-permute-start.12
  35.3 1.8 %shard_map.137 = bf16[80,8,256]{2,1,0:T(8,128)(2,1)} custom-call(s32[12]{0:T(128)S(1)} %copy-done.3, s32[12]{0:T(128)S(1)} %copy-done.4, bf16[320,64]{1,0:T(8,128)(2,1)S(1)} %get-tuple-element.80.pg_ref, bf16[64,256]{1,0:T(8,128)(2,1)S(1)} %bitcast.7, f32[1,256]{1,0:T(1,128)S(1)} %bitcast.9, f32[640,256]{1,0:T(8,128)S(1)} %get-tuple-element.81.hat_ref, ...), custom_call_target="tpu_custom_call" | custom-call | flops 1000000000 | bytes 2000000 | tf_op jit(solution)/shard_map/pallas_call | solution.py:516
  37.2 1.0 %shard_map.138 = bf16[8,128,128]{2,1,0:T(8,128)(2,1)} custom-call(bf16[256,128]{1,0:T(8,128)(2,1)S(1)} %get-tuple-element.83.refs_0_, bf16[256,128]{1,0:T(8,128)(2,1)S(1)} %collective-permute-done.15.refs_1_, bf16[512,128]{1,0:T(8,128)(2,1)S(1)} %collective-permute-done.16.refs_2_, bf16[512,128]{1,0:T(8,128)(2,1)S(1)} %collective-permute-done.17.refs_3_), custom_call_target="tpu_custom_call" | custom-call | flops 1000000000 | bytes 2000000 | tf_op jit(solution)/shard_map/pallas_call | solution.py:516
  38.2 0.1 collective-permute-done.14.refs_3_
  38.3 1.4 %collective-permute-done.12.refs_1_ = bf16[384,128]{1,0:T(8,128)(2,1)S(1)} collective-permute-done((bf16[384,128]{1,0:T(8,128)(2,1)S(1)}, bf16[384,128]{1,0:T(8,128)(2,1)S(1)}, u32[]{:S(2)}, u32[]{:S(2)}) %collective-permute-start.12) | collective-permute-done | bytes 98336 | tf_op jit(solution)/shard_map/ppermute | solution.py:541
  39.8 1.6 %collective-permute-start.19 = (bf16[384,128]{1,0:T(8,128)(2,1)S(1)}, bf16[384,128]{1,0:T(8,128)(2,1)S(1)}, u32[]{:S(2)}, u32[]{:S(2)}) collective-permute-start(bf16[384,128]{1,0:T(8,128)(2,1)S(1)} %shard_map.139.m0), channel_id=1, source_target_pairs={{0,2},{1,3},{2,0},{3,1},{4,6},{5,7},{6,4},{7,5},{8,10},{9,11},{10,... | collective-permute-start | bytes 294920 | tf_op jit(solution)/shard_map/ppermute | solution.py:538
  41.3 3.1 %collective-permute-done.19.m2 = bf16[384,128]{1,0:T(8,128)(2,1)S(1)} collective-permute-done((bf16[384,128]{1,0:T(8,128)(2,1)S(1)}, bf16[384,128]{1,0:T(8,128)(2,1)S(1)}, u32[]{:S(2)}, u32[]{:S(2)}) %collective-permute-start.19) | collective-permute-done | bytes 98336 | tf_op jit(solution)/shard_map/ppermute | solution.py:538
  44.5 1.3 %collective-permute-done.20.m3 = bf16[384,128]{1,0:T(8,128)(2,1)S(1)} collective-permute-done((bf16[384,128]{1,0:T(8,128)(2,1)S(1)}, bf16[384,128]{1,0:T(8,128)(2,1)S(1)}, u32[]{:S(2)}, u32[]{:S(2)}) %collective-permute-start.20) | collective-permute-done | bytes 98336 | tf_op jit(solution)/shard_map/ppermute | solution.py:538
  45.7 0.8 %shard_map.140 = (f32[1024,128]{1,0:T(8,128)}, f32[64,256]{1,0:T(8,128)}) custom-call(bf16[384,128]{1,0:T(8,128)(2,1)S(1)} %shard_map.139.m0, bf16[384,128]{1,0:T(8,128)(2,1)S(1)} %collective-permute-done.18.m1, bf16[384,128]{1,0:T(8,128)(2,1)S(1)} %collective-permute-done.19.m2, bf16[384,128]{1,0:T(8,128)(2,1)S(1)} %collective-permute-done.20.m3), custom_call_target="tpu_custom_call" | custom-call | flops 100000000 | bytes 200000 | tf_op jit(solution)/shard_map/pallas_call | solution.py:516
  (32 shorter events, 0.3 us)
Async XLA Ops:
  0.6 10.2 %copy-start.3 = (s32[12]{0:T(128)S(1)}, s32[12]{0:T(128)}, u32[]{:S(2)}) copy-start(s32[12]{0:T(128)} %len_ref.1) | copy-start | bytes 148
  0.6 10.2 %copy-start.4 = (s32[12]{0:T(128)S(1)}, s32[12]{0:T(128)}, u32[]{:S(2)}) copy-start(s32[12]{0:T(128)} %hom_ref.1) | copy-start | bytes 148
  3.0 7.0 %collective-permute-start = (bf16[336,128]{1,0:T(8,128)(2,1)S(1)}, bf16[336,128]{1,0:T(8,128)(2,1)S(1)}, u32[]{:S(2)}, u32[]{:S(2)}) collective-permute-start(bf16[336,128]{1,0:T(8,128)(2,1)S(1)} %get-tuple-element.54), channel_id=1, source_target_pairs={{0,1},{1,0},{2,3},{3,2},{4,5},{5,4},{6,7},{7,6},{8,9},{9,8},{10,11... | collective-permute-start | bytes 258056 | tf_op jit(solution)/shard_map/ppermute | solution.py:538
  3.5 7.0 %collective-permute-start.1 = (bf16[336,128]{1,0:T(8,128)(2,1)S(1)}, bf16[336,128]{1,0:T(8,128)(2,1)S(1)}, u32[]{:S(2)}, u32[]{:S(2)}) collective-permute-start(bf16[336,128]{1,0:T(8,128)(2,1)S(1)} %get-tuple-element.55), channel_id=1, source_target_pairs={{0,2},{1,3},{2,0},{3,1},{4,6},{5,7},{6,4},{7,5},{8,10},{9,11},{10,... | collective-permute-start | bytes 258056 | tf_op jit(solution)/shard_map/ppermute | solution.py:538
  6.0 4.8 %collective-permute-start.2 = (bf16[336,128]{1,0:T(8,128)(2,1)S(1)}, bf16[336,128]{1,0:T(8,128)(2,1)S(1)}, u32[]{:S(2)}, u32[]{:S(2)}) collective-permute-start(bf16[336,128]{1,0:T(8,128)(2,1)S(1)} %get-tuple-element.56), channel_id=1, source_target_pairs={{0,3},{1,2},{2,1},{3,0},{4,7},{5,6},{6,5},{7,4},{8,11},{9,10},{10,... | collective-permute-start | bytes 258056 | tf_op jit(solution)/shard_map/ppermute | solution.py:538
  6.1 7.7 %collective-permute-start.3 = (bf16[80,128]{1,0:T(8,128)(2,1)S(1)}, bf16[80,128]{1,0:T(8,128)(2,1)S(1)}, u32[]{:S(2)}, u32[]{:S(2)}) collective-permute-start(bf16[80,128]{1,0:T(8,128)(2,1)S(1)} %get-tuple-element.62.refs_6_), channel_id=1, source_target_pairs={{0,12},{1,13},{2,14},{3,15},{4,8},{5,9},{6,10},{7,11},{8,4},{9,5},... | collective-permute-start | bytes 61448 | tf_op jit(solution)/shard_map/ppermute | solution.py:541
  9.9 4.7 %collective-permute-start.4 = (bf16[80,128]{1,0:T(8,128)(2,1)S(1)}, bf16[80,128]{1,0:T(8,128)(2,1)S(1)}, u32[]{:S(2)}, u32[]{:S(2)}) collective-permute-start(bf16[80,128]{1,0:T(8,128)(2,1)S(1)} %get-tuple-element.62.refs_6_), channel_id=1, source_target_pairs={{0,8},{1,9},{2,10},{3,11},{4,12},{5,13},{6,14},{7,15},{8,0},{9,1},... | collective-permute-start | bytes 61448 | tf_op jit(solution)/shard_map/ppermute | solution.py:541
  10.0 4.7 %collective-permute-start.5 = (bf16[80,128]{1,0:T(8,128)(2,1)S(1)}, bf16[80,128]{1,0:T(8,128)(2,1)S(1)}, u32[]{:S(2)}, u32[]{:S(2)}) collective-permute-start(bf16[80,128]{1,0:T(8,128)(2,1)S(1)} %get-tuple-element.62.refs_6_), channel_id=1, source_target_pairs={{0,4},{1,5},{2,6},{3,7},{4,0},{5,1},{6,2},{7,3},{8,12},{9,13},{10,... | collective-permute-start | bytes 61448 | tf_op jit(solution)/shard_map/ppermute | solution.py:541
  14.6 1.8 %copy-start.2 = (f32[128]{0:T(128)S(1)}, f32[128]{0:T(128)}, u32[]{:S(2)}) copy-start(f32[128]{0:T(128)} %param.16) | copy-start | bytes 1540
  19.9 1.6 %collective-permute-start.6 = (bf16[672,128]{1,0:T(8,128)(2,1)S(1)}, bf16[672,128]{1,0:T(8,128)(2,1)S(1)}, u32[]{:S(2)}, u32[]{:S(2)}) collective-permute-start(bf16[672,128]{1,0:T(8,128)(2,1)S(1)} %get-tuple-element.70), channel_id=1, source_target_pairs={{0,1},{1,0},{2,3},{3,2},{4,5},{5,4},{6,7},{7,6},{8,9},{9,8},{10,11... | collective-permute-start | bytes 516104 | tf_op jit(solution)/shard_map/ppermute | solution.py:538
  20.0 6.6 %collective-permute-start.16 = (bf16[512,128]{1,0:T(8,128)(2,1)S(1)}, bf16[512,128]{1,0:T(8,128)(2,1)S(1)}, u32[]{:S(2)}, u32[]{:S(2)}) collective-permute-start(bf16[512,128]{1,0:T(8,128)(2,1)S(1)} %get-tuple-element.85), channel_id=1, source_target_pairs={{0,2},{1,3},{2,0},{3,1},{4,6},{5,7},{6,4},{7,5},{8,10},{9,11},{10,... | collective-permute-start | bytes 393224 | tf_op jit(solution)/shard_map/ppermute | solution.py:538
  21.6 6.2 %collective-permute-start.7 = (bf16[336,128]{1,0:T(8,128)(2,1)S(1)}, bf16[336,128]{1,0:T(8,128)(2,1)S(1)}, u32[]{:S(2)}, u32[]{:S(2)}) collective-permute-start(bf16[336,128]{1,0:T(8,128)(2,1)S(1)} %get-tuple-element.72), channel_id=1, source_target_pairs={{0,2},{1,3},{2,0},{3,1},{4,6},{5,7},{6,4},{7,5},{8,10},{9,11},{10,... | collective-permute-start | bytes 258056 | tf_op jit(solution)/shard_map/ppermute | solution.py:538
  23.0 4.8 %collective-permute-start.10 = (bf16[80,128]{1,0:T(8,128)(2,1)S(1)}, bf16[80,128]{1,0:T(8,128)(2,1)S(1)}, u32[]{:S(2)}, u32[]{:S(2)}) collective-permute-start(bf16[80,128]{1,0:T(8,128)(2,1)S(1)} %get-tuple-element.77), channel_id=1, source_target_pairs={{0,8},{1,9},{2,10},{3,11},{4,12},{5,13},{6,14},{7,15},{8,0},{9,1},... | collective-permute-start | bytes 61448 | tf_op jit(solution)/shard_map/ppermute | solution.py:541
  25.0 5.6 %collective-permute-start.11 = (bf16[80,128]{1,0:T(8,128)(2,1)S(1)}, bf16[80,128]{1,0:T(8,128)(2,1)S(1)}, u32[]{:S(2)}, u32[]{:S(2)}) collective-permute-start(bf16[80,128]{1,0:T(8,128)(2,1)S(1)} %get-tuple-element.78), channel_id=1, source_target_pairs={{0,12},{1,13},{2,14},{3,15},{4,8},{5,9},{6,10},{7,11},{8,4},{9,5},... | collective-permute-start | bytes 61448 | tf_op jit(solution)/shard_map/ppermute | solution.py:541
  26.2 4.5 %collective-permute-start.9 = (bf16[80,128]{1,0:T(8,128)(2,1)S(1)}, bf16[80,128]{1,0:T(8,128)(2,1)S(1)}, u32[]{:S(2)}, u32[]{:S(2)}) collective-permute-start(bf16[80,128]{1,0:T(8,128)(2,1)S(1)} %get-tuple-element.76), channel_id=1, source_target_pairs={{0,4},{1,5},{2,6},{3,7},{4,0},{5,1},{6,2},{7,3},{8,12},{9,13},{10,... | collective-permute-start | bytes 61448 | tf_op jit(solution)/shard_map/ppermute | solution.py:541
  26.6 10.5 %collective-permute-start.15 = (bf16[256,128]{1,0:T(8,128)(2,1)S(1)}, bf16[256,128]{1,0:T(8,128)(2,1)S(1)}, u32[]{:S(2)}, u32[]{:S(2)}) collective-permute-start(bf16[256,128]{1,0:T(8,128)(2,1)S(1)} %get-tuple-element.84), channel_id=1, source_target_pairs={{0,1},{1,0},{2,3},{3,2},{4,5},{5,4},{6,7},{7,6},{8,9},{9,8},{10,11... | collective-permute-start | bytes 196616 | tf_op jit(solution)/shard_map/ppermute | solution.py:538
  27.8 9.4 %collective-permute-start.17 = (bf16[512,128]{1,0:T(8,128)(2,1)S(1)}, bf16[512,128]{1,0:T(8,128)(2,1)S(1)}, u32[]{:S(2)}, u32[]{:S(2)}) collective-permute-start(bf16[512,128]{1,0:T(8,128)(2,1)S(1)} %collective-permute-done.16.refs_2_), channel_id=1, source_target_pairs={{0,1},{1,0},{2,3},{3,2},{4,5},{5,4},{6,7},{7,6},{8,9},{9,8},{10,11... | collective-permute-start | bytes 393224 | tf_op jit(solution)/shard_map/ppermute | solution.py:538
  27.8 7.6 %copy-start = (bf16[256,64]{0,1:T(8,128)(2,1)S(1)}, bf16[256,64]{0,1:T(8,128)(2,1)}, u32[]{:S(2)}) copy-start(bf16[256,64]{0,1:T(8,128)(2,1)} %param.13) | copy-start | bytes 98308
  27.8 7.6 %copy-start.1 = (f32[256]{0:T(256)S(1)}, f32[256]{0:T(256)}, u32[]{:S(2)}) copy-start(f32[256]{0:T(256)} %param.11) | copy-start | bytes 3076
  27.8 7.2 %collective-permute-start.8 = (bf16[256,128]{1,0:T(8,128)(2,1)S(1)}, bf16[256,128]{1,0:T(8,128)(2,1)S(1)}, u32[]{:S(2)}, u32[]{:S(2)}) collective-permute-start(bf16[256,128]{1,0:T(8,128)(2,1)S(1)} %shard_map.134.w0), channel_id=1, source_target_pairs={{0,8},{1,9},{2,10},{3,11},{4,12},{5,13},{6,14},{7,15},{8,0},{9,1},... | collective-permute-start | bytes 196616 | tf_op jit(solution)/shard_map/ppermute | solution.py:541
  31.2 7.0 %collective-permute-start.13 = (bf16[128,128]{1,0:T(8,128)(2,1)S(1)}, bf16[128,128]{1,0:T(8,128)(2,1)S(1)}, u32[]{:S(2)}, u32[]{:S(2)}) collective-permute-start(bf16[128,128]{1,0:T(8,128)(2,1)S(1)} %get-tuple-element.79.fm_ref), channel_id=1, source_target_pairs={{0,8},{1,9},{2,10},{3,11},{4,12},{5,13},{6,14},{7,15},{8,0},{9,1},... | collective-permute-start | bytes 98312 | tf_op jit(solution)/shard_map/ppermute | solution.py:541
  32.5 5.8 %collective-permute-start.14 = (bf16[128,128]{1,0:T(8,128)(2,1)S(1)}, bf16[128,128]{1,0:T(8,128)(2,1)S(1)}, u32[]{:S(2)}, u32[]{:S(2)}) collective-permute-start(bf16[128,128]{1,0:T(8,128)(2,1)S(1)} %get-tuple-element.79.fm_ref), channel_id=1, source_target_pairs={{0,12},{1,13},{2,14},{3,15},{4,8},{5,9},{6,10},{7,11},{8,4},{9,5},... | collective-permute-start | bytes 98312 | tf_op jit(solution)/shard_map/ppermute | solution.py:541
  35.0 4.7 %collective-permute-start.12 = (bf16[384,128]{1,0:T(8,128)(2,1)S(1)}, bf16[384,128]{1,0:T(8,128)(2,1)S(1)}, u32[]{:S(2)}, u32[]{:S(2)}) collective-permute-start(bf16[384,128]{1,0:T(8,128)(2,1)S(1)} %shard_map.136.refs_0_), channel_id=1, source_target_pairs={{0,4},{1,5},{2,6},{3,7},{4,0},{5,1},{6,2},{7,3},{8,12},{9,13},{10,... | collective-permute-start | bytes 294920 | tf_op jit(solution)/shard_map/ppermute | solution.py:541
  39.8 4.7 %collective-permute-start.19 = (bf16[384,128]{1,0:T(8,128)(2,1)S(1)}, bf16[384,128]{1,0:T(8,128)(2,1)S(1)}, u32[]{:S(2)}, u32[]{:S(2)}) collective-permute-start(bf16[384,128]{1,0:T(8,128)(2,1)S(1)} %shard_map.139.m0), channel_id=1, source_target_pairs={{0,2},{1,3},{2,0},{3,1},{4,6},{5,7},{6,4},{7,5},{8,10},{9,11},{10,... | collective-permute-start | bytes 294920 | tf_op jit(solution)/shard_map/ppermute | solution.py:538
  41.3 3.1 %collective-permute-start.18 = (bf16[384,128]{1,0:T(8,128)(2,1)S(1)}, bf16[384,128]{1,0:T(8,128)(2,1)S(1)}, u32[]{:S(2)}, u32[]{:S(2)}) collective-permute-start(bf16[384,128]{1,0:T(8,128)(2,1)S(1)} %shard_map.139.m0), channel_id=1, source_target_pairs={{0,1},{1,0},{2,3},{3,2},{4,5},{5,4},{6,7},{7,6},{8,9},{9,8},{10,11... | collective-permute-start | bytes 294920 | tf_op jit(solution)/shard_map/ppermute | solution.py:538
  44.4 1.3 %collective-permute-start.20 = (bf16[384,128]{1,0:T(8,128)(2,1)S(1)}, bf16[384,128]{1,0:T(8,128)(2,1)S(1)}, u32[]{:S(2)}, u32[]{:S(2)}) collective-permute-start(bf16[384,128]{1,0:T(8,128)(2,1)S(1)} %collective-permute-done.19.m2), channel_id=1, source_target_pairs={{0,1},{1,0},{2,3},{3,2},{4,5},{5,4},{6,7},{7,6},{8,9},{9,8},{10,11... | collective-permute-start | bytes 294920 | tf_op jit(solution)/shard_map/ppermute | solution.py:538

commit v6 on v5

--- a/solution.py
+++ b/solution.py
@@ -155,8 +155,8 @@
 
 def start_kernel(
     x_hbm, adj_hbm, scale_hbm, shift_hbm, mat_hbm, off_hbm, len_hbm, hom_hbm, final_hbm,
-    m0, m1, m2, m3, right_ref, norm_ref, hat_ref, rstd_ref, spread_ref, swap_ref, final_ref,
-    x_ref, adj_ref, scale_ref, shift_ref, mat_ref, off_ref, len_ref, hom_ref,
+    m0, m1, m2, m3, right_ref, norm_ref, x_ref, spread_ref, swap_ref, final_ref,
+    adj_ref, scale_ref, shift_ref, mat_ref, off_ref, len_ref, hom_ref,
     work, full, comp, sems,
 ):
     messages = (m0, m1, m2, m3)
@@ -196,9 +196,7 @@
     rstd = lax.rsqrt(jnp.mean(centred * centred, axis=-1, keepdims=True) + 1e-05)
     hat = (centred * rstd).reshape(depth * BLOCK, 256)
     normed = (hat * scale_ref[...] + shift_ref[...]).astype(BF16)
-    hat_ref[...] = hat
     norm_ref[...] = normed
-    rstd_ref[...] = jnp.broadcast_to(rstd, (depth, BLOCK, 128)).reshape(depth * BLOCK, 128)
     proj = lax.dot_general(
         normed, mat_ref[...], (((1,), (1,)), ((), ())), preferred_element_type=F32
     ) + off_ref[...]
@@ -444,10 +442,10 @@
 
 
 def align_kernel(
-    len_ref, hom_ref, pg_ref, mat_ref, scale_ref, hat_ref, rstd_ref, out_ref, full
+    len_ref, hom_ref, pg_ref, mat_ref, scale_ref, x_ref, out_ref, full
 ):
     a, b = place()
-    depth8 = hat_ref.shape[0]
+    depth8 = x_ref.shape[0] * BLOCK
     full[0 : PAIRED * BLOCK, :] = pg_ref[0 : PAIRED * BLOCK, :].astype(F32)
     full[PAIRED * BLOCK :, :] = jnp.zeros((full.shape[0] - PAIRED * BLOCK, 64), F32)
     extra = pg_ref[PAIRED * BLOCK :, :].astype(F32)
@@ -461,11 +459,13 @@
         start = start + hom_ref[c]
     g = jnp.dot(full[0:depth8, :].astype(BF16), mat_ref[...], preferred_element_type=F32)
     g = g * scale_ref[...]
-    hat = hat_ref[...]
+    x = x_ref[...].astype(F32).reshape(depth8, 256)
+    centred = x - jnp.mean(x, axis=-1, keepdims=True)
+    rstd = lax.rsqrt(jnp.mean(centred * centred, axis=-1, keepdims=True) + 1e-05)
+    hat = centred * rstd
     m1 = jnp.mean(g, axis=-1, keepdims=True)
     m2 = jnp.mean(g * hat, axis=-1, keepdims=True)
-    rstd = rstd_ref[...]
-    dx = (g - m1 - hat * m2) * jnp.concatenate([rstd, rstd], axis=1)
+    dx = (g - m1 - hat * m2) * rstd
     out_ref[...] = dx.reshape(out_ref.shape).astype(BF16)
 
 
@@ -553,14 +553,13 @@
             return parts
         return [parts[u % 4][(u // 4) * rows : (u // 4 + 1) * rows] for u in range(groups)]
 
-    *messages, right, normed, hat, rstd, spread, swap, final = call(
+    *messages, right, normed, x, spread, swap, final = call(
         start_kernel,
         [sds((groups * 64 + PACKED, 128), BF16)] * QUAD
         + [
             sds((PACKED, 128), BF16),
             sds((depth * BLOCK, 256), BF16),
-            sds((depth * BLOCK, 256), F32),
-            sds((depth * BLOCK, 128), F32),
+            sds(x.shape, BF16),
             sds((512, 512), BF16),
             sds((512, 512), BF16),
             sds(final.shape, BF16),
@@ -568,7 +567,6 @@
         [x, adjoint, scale, shift, mat, off, lengths, homologs, final],
         in_specs=[HBM] * 9,
         scratch=[
-            pltpu.VMEM(x.shape, BF16),
             pltpu.VMEM(adjoint.shape, BF16),
             pltpu.VMEM((1, 256), F32),
             pltpu.VMEM((1, 256), F32),
@@ -655,8 +653,8 @@
     alignment_gradient = call(
         align_kernel,
         sds(x.shape, BF16),
-        [lengths, homologs, pg, mat, scale, hat, rstd],
-        in_specs=[SMEM] * 2 + [vmem()] * 5,
+        [lengths, homologs, pg, mat, scale, x],
+        in_specs=[SMEM] * 2 + [vmem()] * 4,
         scratch=[pltpu.VMEM(((depth + EXTRA) * BLOCK, 64), F32)],
         work=10**9,
     )

time: 46.7 us -> 46.8 us (level)
  transfers between devices with their start and end apart: 21 -> 21, of which waited for: 9 -> 8; matrix products, arithmetic and copies ran while one was open for 0% -> 0% of each run, Pallas kernels for 14% -> 14%
where the time goes in v6:
time: 46.8 us; the launch traced here: 46.6 us
  starting transfers between devices  21.8 us (47%)
  Pallas kernels  15 us (32%)
  waiting for transfers between devices  9.11 us (19%)
  between operations  0.74 us (2%)
    pallas_call x12, Pallas kernels, call(): pl.pallas_call(kernel, out_shape=outs, in_specs=in_specs if in_specs is n...  15 us
    ppermute x10, starting transfers between devices, far(): return lax.ppermute(value, 'row', [(k, k ^ 4 * u) for k in range(devices)])  14 us
    ppermute x11, starting transfers between devices, near(): return lax.ppermute(value, 'row', [(k, k ^ t) for k in range(devices)])  7.74 us
    ppermute x11, waiting for transfers between devices, near(): return lax.ppermute(value, 'row', [(k, k ^ t) for k in range(devices)])  5.83 us
    ppermute x10, waiting for transfers between devices, far(): return lax.ppermute(value, 'row', [(k, k ^ 4 * u) for k in range(devices)])  3.27 us
  transfers between devices with their start and end apart: 21, of which 8 were waited for; matrix products, arithmetic and copies ran while one was open for 0% of the time, Pallas kernels for 14%

profile of v6, /device:TPU:0, one launch (start us, length us, event | category | flops | bytes accessed | tf_op | source)
XLA Modules:
  0.0 46.6 jit_solution(11764113204461631438)
XLA Ops:
  0.7 2.3 %shard_map.129 = (bf16[336,128]{1,0:T(8,128)(2,1)S(1)}, bf16[336,128]{1,0:T(8,128)(2,1)S(1)}, bf16[336,128]{1,0:T(8,128)(2,1)S(1)}, bf16[336,128]{1,0:T(8,128)(2...) custom-call(bf16[80,8,256]{2,1,0:T(8,128)(2,1)} %x_hbm.1, ...), custom_call_target="tpu_custom_call" | custom-call | flops 1000000000 | bytes 2000000 | tf_op jit(solution)/shard_map/pallas_call | solution.py:516
  3.0 0.5 %collective-permute-start = (bf16[336,128]{1,0:T(8,128)(2,1)S(1)}, bf16[336,128]{1,0:T(8,128)(2,1)S(1)}, u32[]{:S(2)}, u32[]{:S(2)}) collective-permute-start(bf16[336,128]{1,0:T(8,128)(2,1)S(1)} %get-tuple-element.53), channel_id=1, source_target_pairs={{0,1},{1,0},{2,3},{3,2},{4,5},{5,4},{6,7},{7,6},{8,9},{9,8},{10,11... | collective-permute-start | bytes 258056 | tf_op jit(solution)/shard_map/ppermute | solution.py:538
  3.5 2.6 %collective-permute-start.1 = (bf16[336,128]{1,0:T(8,128)(2,1)S(1)}, bf16[336,128]{1,0:T(8,128)(2,1)S(1)}, u32[]{:S(2)}, u32[]{:S(2)}) collective-permute-start(bf16[336,128]{1,0:T(8,128)(2,1)S(1)} %get-tuple-element.54), channel_id=1, source_target_pairs={{0,2},{1,3},{2,0},{3,1},{4,6},{5,7},{6,4},{7,5},{8,10},{9,11},{10,... | collective-permute-start | bytes 258056 | tf_op jit(solution)/shard_map/ppermute | solution.py:538
  6.0 0.1 collective-permute-start.2
  6.1 3.8 %collective-permute-start.3 = (bf16[80,128]{1,0:T(8,128)(2,1)S(1)}, bf16[80,128]{1,0:T(8,128)(2,1)S(1)}, u32[]{:S(2)}, u32[]{:S(2)}) collective-permute-start(bf16[80,128]{1,0:T(8,128)(2,1)S(1)} %get-tuple-element.61.refs_6_), channel_id=1, source_target_pairs={{0,12},{1,13},{2,14},{3,15},{4,8},{5,9},{6,10},{7,11},{8,4},{9,5},... | collective-permute-start | bytes 61448 | tf_op jit(solution)/shard_map/ppermute | solution.py:541
  10.0 0.6 %collective-permute-start.5 = (bf16[80,128]{1,0:T(8,128)(2,1)S(1)}, bf16[80,128]{1,0:T(8,128)(2,1)S(1)}, u32[]{:S(2)}, u32[]{:S(2)}) collective-permute-start(bf16[80,128]{1,0:T(8,128)(2,1)S(1)} %get-tuple-element.61.refs_6_), channel_id=1, source_target_pairs={{0,4},{1,5},{2,6},{3,7},{4,0},{5,1},{6,2},{7,3},{8,12},{9,13},{10,... | collective-permute-start | bytes 61448 | tf_op jit(solution)/shard_map/ppermute | solution.py:541
  10.5 0.3 collective-permute-done.2.refs_9_
  10.8 3.0 %shard_map.130 = (bf16[1024,128]{1,0:T(8,128)(2,1)S(1)}, bf16[1024,1024]{1,0:T(8,128)(2,1)S(1)}, bf16[128,1024]{1,0:T(8,128)(2,1)S(1)}, bf16[128,1024]{1,0:T(8,1...) custom-call(s32[12]{0:T(128)S(1)} %copy-done.3, ...), custom_call_target="tpu_custom_call" | custom-call | flops 2000000000 | bytes 4000000 | tf_op jit(solution)/shard_map/pallas_call | solution.py:516
  13.8 0.8 %collective-permute-done.4.refs_4_ = bf16[80,128]{1,0:T(8,128)(2,1)S(1)} collective-permute-done((bf16[80,128]{1,0:T(8,128)(2,1)S(1)}, bf16[80,128]{1,0:T(8,128)(2,1)S(1)}, u32[]{:S(2)}, u32[]{:S(2)}) %collective-permute-start.4) | collective-permute-done | bytes 20512 | tf_op jit(solution)/shard_map/ppermute | solution.py:541
  14.6 1.8 %shard_map.131 = (bf16[80,128]{1,0:T(8,128)(2,1)S(1)}, bf16[80,128]{1,0:T(8,128)(2,1)S(1)}, bf16[80,128]{1,0:T(8,128)(2,1)S(1)}, bf16[80,128]{1,0:T(8,128)(2,1)S...) custom-call(s32[12]{0:T(128)S(1)} %copy-done.3, ...), custom_call_target="tpu_custom_call" | custom-call | flops 2000000000 | bytes 4000000 | tf_op jit(solution)/shard_map/pallas_call | solution.py:516
  16.4 3.5 %shard_map.132 = (bf16[336,128]{1,0:T(8,128)(2,1)S(1)}, bf16[336,128]{1,0:T(8,128)(2,1)S(1)}, bf16[672,128]{1,0:T(8,128)(2,1)S(1)}, bf16[256,128]{1,0:T(8,128)(2...) custom-call(s32[12]{0:T(128)S(1)} %copy-done.3, s32[12]{0:T(128)S(1)} %copy-done.4, ...), custom_call_target="tpu_custom_call" | custom-call | flops 4000000000 | bytes 8000000 | tf_op jit(solution)/shard_map/pallas_call | solution.py:516
  20.0 0.1 collective-permute-start.6
  20.0 1.5 %collective-permute-start.16 = (bf16[512,128]{1,0:T(8,128)(2,1)S(1)}, bf16[512,128]{1,0:T(8,128)(2,1)S(1)}, u32[]{:S(2)}, u32[]{:S(2)}) collective-permute-start(bf16[512,128]{1,0:T(8,128)(2,1)S(1)} %get-tuple-element.83), channel_id=1, source_target_pairs={{0,2},{1,3},{2,0},{3,1},{4,6},{5,7},{6,4},{7,5},{8,10},{9,11},{10,... | collective-permute-start | bytes 393224 | tf_op jit(solution)/shard_map/ppermute | solution.py:538
  21.6 1.4 %collective-permute-start.7 = (bf16[336,128]{1,0:T(8,128)(2,1)S(1)}, bf16[336,128]{1,0:T(8,128)(2,1)S(1)}, u32[]{:S(2)}, u32[]{:S(2)}) collective-permute-start(bf16[336,128]{1,0:T(8,128)(2,1)S(1)} %get-tuple-element.71), channel_id=1, source_target_pairs={{0,2},{1,3},{2,0},{3,1},{4,6},{5,7},{6,4},{7,5},{8,10},{9,11},{10,... | collective-permute-start | bytes 258056 | tf_op jit(solution)/shard_map/ppermute | solution.py:538
  23.0 2.0 %collective-permute-start.10 = (bf16[80,128]{1,0:T(8,128)(2,1)S(1)}, bf16[80,128]{1,0:T(8,128)(2,1)S(1)}, u32[]{:S(2)}, u32[]{:S(2)}) collective-permute-start(bf16[80,128]{1,0:T(8,128)(2,1)S(1)} %get-tuple-element.76), channel_id=1, source_target_pairs={{0,8},{1,9},{2,10},{3,11},{4,12},{5,13},{6,14},{7,15},{8,0},{9,1},... | collective-permute-start | bytes 61448 | tf_op jit(solution)/shard_map/ppermute | solution.py:541
  25.0 1.1 %collective-permute-start.11 = (bf16[80,128]{1,0:T(8,128)(2,1)S(1)}, bf16[80,128]{1,0:T(8,128)(2,1)S(1)}, u32[]{:S(2)}, u32[]{:S(2)}) collective-permute-start(bf16[80,128]{1,0:T(8,128)(2,1)S(1)} %get-tuple-element.77), channel_id=1, source_target_pairs={{0,12},{1,13},{2,14},{3,15},{4,8},{5,9},{6,10},{7,11},{8,4},{9,5},... | collective-permute-start | bytes 61448 | tf_op jit(solution)/shard_map/ppermute | solution.py:541
  26.2 0.5 collective-permute-start.9
  26.7 1.1 %collective-permute-done.7.theirs_ref.refs_3_ = bf16[336,128]{1,0:T(8,128)(2,1)S(1)} collective-permute-done((bf16[336,128]{1,0:T(8,128)(2,1)S(1)}, bf16[336,128]{1,0:T(8,128)(2,1)S(1)}, u32[]{:S(2)}, u32[]{:S(2)}) %collective-permute-start.7) | collective-permute-done | bytes 86048 | tf_op jit(solution)/shard_map/ppermute | solution.py:538
  27.8 2.2 %collective-permute-start.8 = (bf16[256,128]{1,0:T(8,128)(2,1)S(1)}, bf16[256,128]{1,0:T(8,128)(2,1)S(1)}, u32[]{:S(2)}, u32[]{:S(2)}) collective-permute-start(bf16[256,128]{1,0:T(8,128)(2,1)S(1)} %shard_map.134.w0), channel_id=1, source_target_pairs={{0,8},{1,9},{2,10},{3,11},{4,12},{5,13},{6,14},{7,15},{8,0},{9,1},... | collective-permute-start | bytes 196616 | tf_op jit(solution)/shard_map/ppermute | solution.py:541
  30.1 0.6 %collective-permute-done.11.refs_7_ = bf16[80,128]{1,0:T(8,128)(2,1)S(1)} collective-permute-done((bf16[80,128]{1,0:T(8,128)(2,1)S(1)}, bf16[80,128]{1,0:T(8,128)(2,1)S(1)}, u32[]{:S(2)}, u32[]{:S(2)}) %collective-permute-start.11) | collective-permute-done | bytes 20512 | tf_op jit(solution)/shard_map/ppermute | solution.py:541
  30.6 0.5 %shard_map.135 = (bf16[320,64]{1,0:T(8,128)(2,1)S(1)}, bf16[128,128]{1,0:T(8,128)(2,1)S(1)}) custom-call(bf16[512,512]{1,0:T(8,128)(2,1)S(1)} %get-tuple-element.72.refs_0_, bf16[320,256]{1,0:T(8,128)(2,1)S(1)} %get-tuple-element.73.refs_1_, f32[336,128]{1,0:T(8,128)S(1)} %get-tuple-element.70.mine_ref.refs_2_, ...), custom_call_target="tpu_custom_call" | custom-call | flops 1000000000 | bytes 2000000 | tf_op jit(solution)/shard_map/pallas_call | solution.py:516
  31.2 1.3 %collective-permute-start.13 = (bf16[128,128]{1,0:T(8,128)(2,1)S(1)}, bf16[128,128]{1,0:T(8,128)(2,1)S(1)}, u32[]{:S(2)}, u32[]{:S(2)}) collective-permute-start(bf16[128,128]{1,0:T(8,128)(2,1)S(1)} %get-tuple-element.78.fm_ref), channel_id=1, source_target_pairs={{0,8},{1,9},{2,10},{3,11},{4,12},{5,13},{6,14},{7,15},{8,0},{9,1},... | collective-permute-start | bytes 98312 | tf_op jit(solution)/shard_map/ppermute | solution.py:541
  32.5 2.1 %collective-permute-start.14 = (bf16[128,128]{1,0:T(8,128)(2,1)S(1)}, bf16[128,128]{1,0:T(8,128)(2,1)S(1)}, u32[]{:S(2)}, u32[]{:S(2)}) collective-permute-start(bf16[128,128]{1,0:T(8,128)(2,1)S(1)} %get-tuple-element.78.fm_ref), channel_id=1, source_target_pairs={{0,12},{1,13},{2,14},{3,15},{4,8},{5,9},{6,10},{7,11},{8,4},{9,5},... | collective-permute-start | bytes 98312 | tf_op jit(solution)/shard_map/ppermute | solution.py:541
  34.6 0.4 collective-permute-done.8.w1
  35.1 0.3 collective-permute-start.12
  35.3 1.9 %shard_map.137 = bf16[80,8,256]{2,1,0:T(8,128)(2,1)} custom-call(s32[12]{0:T(128)S(1)} %copy-done.3, s32[12]{0:T(128)S(1)} %copy-done.4, bf16[320,64]{1,0:T(8,128)(2,1)S(1)} %get-tuple-element.79.pg_ref, bf16[64,256]{1,0:T(8,128)(2,1)S(1)} %bitcast.7, f32[1,256]{1,0:T(1,128)S(1)} %bitcast.9, bf16[80,8,256]{2,1,0:T(8,128)(2,1)S(1)} %get-tuple-element.80.x_ref), custom_call_target="tpu_custom_call" | custom-call | flops 1000000000 | bytes 2000000 | tf_op jit(solution)/shard_map/pallas_call | solution.py:516
  37.2 1.0 %shard_map.138 = bf16[8,128,128]{2,1,0:T(8,128)(2,1)} custom-call(bf16[256,128]{1,0:T(8,128)(2,1)S(1)} %get-tuple-element.81.refs_0_, bf16[256,128]{1,0:T(8,128)(2,1)S(1)} %collective-permute-done.15.refs_1_, bf16[512,128]{1,0:T(8,128)(2,1)S(1)} %collective-permute-done.16.refs_2_, bf16[512,128]{1,0:T(8,128)(2,1)S(1)} %collective-permute-done.17.refs_3_), custom_call_target="tpu_custom_call" | custom-call | flops 1000000000 | bytes 2000000 | tf_op jit(solution)/shard_map/pallas_call | solution.py:516
  38.3 1.4 %collective-permute-done.12.refs_1_ = bf16[384,128]{1,0:T(8,128)(2,1)S(1)} collective-permute-done((bf16[384,128]{1,0:T(8,128)(2,1)S(1)}, bf16[384,128]{1,0:T(8,128)(2,1)S(1)}, u32[]{:S(2)}, u32[]{:S(2)}) %collective-permute-start.12) | collective-permute-done | bytes 98336 | tf_op jit(solution)/shard_map/ppermute | solution.py:541
  39.8 1.6 %collective-permute-start.19 = (bf16[384,128]{1,0:T(8,128)(2,1)S(1)}, bf16[384,128]{1,0:T(8,128)(2,1)S(1)}, u32[]{:S(2)}, u32[]{:S(2)}) collective-permute-start(bf16[384,128]{1,0:T(8,128)(2,1)S(1)} %shard_map.139.m0), channel_id=1, source_target_pairs={{0,2},{1,3},{2,0},{3,1},{4,6},{5,7},{6,4},{7,5},{8,10},{9,11},{10,... | collective-permute-start | bytes 294920 | tf_op jit(solution)/shard_map/ppermute | solution.py:538
  41.3 3.1 %collective-permute-done.19.m2 = bf16[384,128]{1,0:T(8,128)(2,1)S(1)} collective-permute-done((bf16[384,128]{1,0:T(8,128)(2,1)S(1)}, bf16[384,128]{1,0:T(8,128)(2,1)S(1)}, u32[]{:S(2)}, u32[]{:S(2)}) %collective-permute-start.19) | collective-permute-done | bytes 98336 | tf_op jit(solution)/shard_map/ppermute | solution.py:538
  44.5 1.3 %collective-permute-done.20.m3 = bf16[384,128]{1,0:T(8,128)(2,1)S(1)} collective-permute-done((bf16[384,128]{1,0:T(8,128)(2,1)S(1)}, bf16[384,128]{1,0:T(8,128)(2,1)S(1)}, u32[]{:S(2)}, u32[]{:S(2)}) %collective-permute-start.20) | collective-permute-done | bytes 98336 | tf_op jit(solution)/shard_map/ppermute | solution.py:538
  45.8 0.8 %shard_map.140 = (f32[1024,128]{1,0:T(8,128)}, f32[64,256]{1,0:T(8,128)}) custom-call(bf16[384,128]{1,0:T(8,128)(2,1)S(1)} %shard_map.139.m0, bf16[384,128]{1,0:T(8,128)(2,1)S(1)} %collective-permute-done.18.m1, bf16[384,128]{1,0:T(8,128)(2,1)S(1)} %collective-permute-done.19.m2, bf16[384,128]{1,0:T(8,128)(2,1)S(1)} %collective-permute-done.20.m3), custom_call_target="tpu_custom_call" | custom-call | flops 100000000 | bytes 200000 | tf_op jit(solution)/shard_map/pallas_call | solution.py:516
  (32 shorter events, 0.2 us)
Async XLA Ops:
  0.6 10.2 %copy-start.3 = (s32[12]{0:T(128)S(1)}, s32[12]{0:T(128)}, u32[]{:S(2)}) copy-start(s32[12]{0:T(128)} %len_ref.1) | copy-start | bytes 148
  0.6 10.2 %copy-start.4 = (s32[12]{0:T(128)S(1)}, s32[12]{0:T(128)}, u32[]{:S(2)}) copy-start(s32[12]{0:T(128)} %hom_ref.1) | copy-start | bytes 148
  3.0 7.0 %collective-permute-start = (bf16[336,128]{1,0:T(8,128)(2,1)S(1)}, bf16[336,128]{1,0:T(8,128)(2,1)S(1)}, u32[]{:S(2)}, u32[]{:S(2)}) collective-permute-start(bf16[336,128]{1,0:T(8,128)(2,1)S(1)} %get-tuple-element.53), channel_id=1, source_target_pairs={{0,1},{1,0},{2,3},{3,2},{4,5},{5,4},{6,7},{7,6},{8,9},{9,8},{10,11... | collective-permute-start | bytes 258056 | tf_op jit(solution)/shard_map/ppermute | solution.py:538
  3.5 7.0 %collective-permute-start.1 = (bf16[336,128]{1,0:T(8,128)(2,1)S(1)}, bf16[336,128]{1,0:T(8,128)(2,1)S(1)}, u32[]{:S(2)}, u32[]{:S(2)}) collective-permute-start(bf16[336,128]{1,0:T(8,128)(2,1)S(1)} %get-tuple-element.54), channel_id=1, source_target_pairs={{0,2},{1,3},{2,0},{3,1},{4,6},{5,7},{6,4},{7,5},{8,10},{9,11},{10,... | collective-permute-start | bytes 258056 | tf_op jit(solution)/shard_map/ppermute | solution.py:538
  6.0 4.8 %collective-permute-start.2 = (bf16[336,128]{1,0:T(8,128)(2,1)S(1)}, bf16[336,128]{1,0:T(8,128)(2,1)S(1)}, u32[]{:S(2)}, u32[]{:S(2)}) collective-permute-start(bf16[336,128]{1,0:T(8,128)(2,1)S(1)} %get-tuple-element.55), channel_id=1, source_target_pairs={{0,3},{1,2},{2,1},{3,0},{4,7},{5,6},{6,5},{7,4},{8,11},{9,10},{10,... | collective-permute-start | bytes 258056 | tf_op jit(solution)/shard_map/ppermute | solution.py:538
  6.1 7.7 %collective-permute-start.3 = (bf16[80,128]{1,0:T(8,128)(2,1)S(1)}, bf16[80,128]{1,0:T(8,128)(2,1)S(1)}, u32[]{:S(2)}, u32[]{:S(2)}) collective-permute-start(bf16[80,128]{1,0:T(8,128)(2,1)S(1)} %get-tuple-element.61.refs_6_), channel_id=1, source_target_pairs={{0,12},{1,13},{2,14},{3,15},{4,8},{5,9},{6,10},{7,11},{8,4},{9,5},... | collective-permute-start | bytes 61448 | tf_op jit(solution)/shard_map/ppermute | solution.py:541
  10.0 4.7 %collective-permute-start.4 = (bf16[80,128]{1,0:T(8,128)(2,1)S(1)}, bf16[80,128]{1,0:T(8,128)(2,1)S(1)}, u32[]{:S(2)}, u32[]{:S(2)}) collective-permute-start(bf16[80,128]{1,0:T(8,128)(2,1)S(1)} %get-tuple-element.61.refs_6_), channel_id=1, source_target_pairs={{0,8},{1,9},{2,10},{3,11},{4,12},{5,13},{6,14},{7,15},{8,0},{9,1},... | collective-permute-start | bytes 61448 | tf_op jit(solution)/shard_map/ppermute | solution.py:541
  10.0 4.7 %collective-permute-start.5 = (bf16[80,128]{1,0:T(8,128)(2,1)S(1)}, bf16[80,128]{1,0:T(8,128)(2,1)S(1)}, u32[]{:S(2)}, u32[]{:S(2)}) collective-permute-start(bf16[80,128]{1,0:T(8,128)(2,1)S(1)} %get-tuple-element.61.refs_6_), channel_id=1, source_target_pairs={{0,4},{1,5},{2,6},{3,7},{4,0},{5,1},{6,2},{7,3},{8,12},{9,13},{10,... | collective-permute-start | bytes 61448 | tf_op jit(solution)/shard_map/ppermute | solution.py:541
  14.6 1.8 %copy-start.2 = (f32[128]{0:T(128)S(1)}, f32[128]{0:T(128)}, u32[]{:S(2)}) copy-start(f32[128]{0:T(128)} %param.16) | copy-start | bytes 1540
  20.0 1.6 %collective-permute-start.6 = (bf16[672,128]{1,0:T(8,128)(2,1)S(1)}, bf16[672,128]{1,0:T(8,128)(2,1)S(1)}, u32[]{:S(2)}, u32[]{:S(2)}) collective-permute-start(bf16[672,128]{1,0:T(8,128)(2,1)S(1)} %get-tuple-element.69), channel_id=1, source_target_pairs={{0,1},{1,0},{2,3},{3,2},{4,5},{5,4},{6,7},{7,6},{8,9},{9,8},{10,11... | collective-permute-start | bytes 516104 | tf_op jit(solution)/shard_map/ppermute | solution.py:538
  20.0 6.6 %collective-permute-start.16 = (bf16[512,128]{1,0:T(8,128)(2,1)S(1)}, bf16[512,128]{1,0:T(8,128)(2,1)S(1)}, u32[]{:S(2)}, u32[]{:S(2)}) collective-permute-start(bf16[512,128]{1,0:T(8,128)(2,1)S(1)} %get-tuple-element.83), channel_id=1, source_target_pairs={{0,2},{1,3},{2,0},{3,1},{4,6},{5,7},{6,4},{7,5},{8,10},{9,11},{10,... | collective-permute-start | bytes 393224 | tf_op jit(solution)/shard_map/ppermute | solution.py:538
  21.6 6.2 %collective-permute-start.7 = (bf16[336,128]{1,0:T(8,128)(2,1)S(1)}, bf16[336,128]{1,0:T(8,128)(2,1)S(1)}, u32[]{:S(2)}, u32[]{:S(2)}) collective-permute-start(bf16[336,128]{1,0:T(8,128)(2,1)S(1)} %get-tuple-element.71), channel_id=1, source_target_pairs={{0,2},{1,3},{2,0},{3,1},{4,6},{5,7},{6,4},{7,5},{8,10},{9,11},{10,... | collective-permute-start | bytes 258056 | tf_op jit(solution)/shard_map/ppermute | solution.py:538
  23.0 4.8 %collective-permute-start.10 = (bf16[80,128]{1,0:T(8,128)(2,1)S(1)}, bf16[80,128]{1,0:T(8,128)(2,1)S(1)}, u32[]{:S(2)}, u32[]{:S(2)}) collective-permute-start(bf16[80,128]{1,0:T(8,128)(2,1)S(1)} %get-tuple-element.76), channel_id=1, source_target_pairs={{0,8},{1,9},{2,10},{3,11},{4,12},{5,13},{6,14},{7,15},{8,0},{9,1},... | collective-permute-start | bytes 61448 | tf_op jit(solution)/shard_map/ppermute | solution.py:541
  25.0 5.6 %collective-permute-start.11 = (bf16[80,128]{1,0:T(8,128)(2,1)S(1)}, bf16[80,128]{1,0:T(8,128)(2,1)S(1)}, u32[]{:S(2)}, u32[]{:S(2)}) collective-permute-start(bf16[80,128]{1,0:T(8,128)(2,1)S(1)} %get-tuple-element.77), channel_id=1, source_target_pairs={{0,12},{1,13},{2,14},{3,15},{4,8},{5,9},{6,10},{7,11},{8,4},{9,5},... | collective-permute-start | bytes 61448 | tf_op jit(solution)/shard_map/ppermute | solution.py:541
  26.2 4.4 %collective-permute-start.9 = (bf16[80,128]{1,0:T(8,128)(2,1)S(1)}, bf16[80,128]{1,0:T(8,128)(2,1)S(1)}, u32[]{:S(2)}, u32[]{:S(2)}) collective-permute-start(bf16[80,128]{1,0:T(8,128)(2,1)S(1)} %get-tuple-element.75), channel_id=1, source_target_pairs={{0,4},{1,5},{2,6},{3,7},{4,0},{5,1},{6,2},{7,3},{8,12},{9,13},{10,... | collective-permute-start | bytes 61448 | tf_op jit(solution)/shard_map/ppermute | solution.py:541
  26.6 10.6 %collective-permute-start.15 = (bf16[256,128]{1,0:T(8,128)(2,1)S(1)}, bf16[256,128]{1,0:T(8,128)(2,1)S(1)}, u32[]{:S(2)}, u32[]{:S(2)}) collective-permute-start(bf16[256,128]{1,0:T(8,128)(2,1)S(1)} %get-tuple-element.82), channel_id=1, source_target_pairs={{0,1},{1,0},{2,3},{3,2},{4,5},{5,4},{6,7},{7,6},{8,9},{9,8},{10,11... | collective-permute-start | bytes 196616 | tf_op jit(solution)/shard_map/ppermute | solution.py:538
  27.8 9.4 %collective-permute-start.17 = (bf16[512,128]{1,0:T(8,128)(2,1)S(1)}, bf16[512,128]{1,0:T(8,128)(2,1)S(1)}, u32[]{:S(2)}, u32[]{:S(2)}) collective-permute-start(bf16[512,128]{1,0:T(8,128)(2,1)S(1)} %collective-permute-done.16.refs_2_), channel_id=1, source_target_pairs={{0,1},{1,0},{2,3},{3,2},{4,5},{5,4},{6,7},{7,6},{8,9},{9,8},{10,11... | collective-permute-start | bytes 393224 | tf_op jit(solution)/shard_map/ppermute | solution.py:538
  27.8 7.5 %copy-start = (bf16[256,64]{0,1:T(8,128)(2,1)S(1)}, bf16[256,64]{0,1:T(8,128)(2,1)}, u32[]{:S(2)}) copy-start(bf16[256,64]{0,1:T(8,128)(2,1)} %param.13) | copy-start | bytes 98308
  27.8 7.5 %copy-start.1 = (f32[256]{0:T(256)S(1)}, f32[256]{0:T(256)}, u32[]{:S(2)}) copy-start(f32[256]{0:T(256)} %param.11) | copy-start | bytes 3076
  27.8 7.2 %collective-permute-start.8 = (bf16[256,128]{1,0:T(8,128)(2,1)S(1)}, bf16[256,128]{1,0:T(8,128)(2,1)S(1)}, u32[]{:S(2)}, u32[]{:S(2)}) collective-permute-start(bf16[256,128]{1,0:T(8,128)(2,1)S(1)} %shard_map.134.w0), channel_id=1, source_target_pairs={{0,8},{1,9},{2,10},{3,11},{4,12},{5,13},{6,14},{7,15},{8,0},{9,1},... | collective-permute-start | bytes 196616 | tf_op jit(solution)/shard_map/ppermute | solution.py:541
  31.2 7.1 %collective-permute-start.13 = (bf16[128,128]{1,0:T(8,128)(2,1)S(1)}, bf16[128,128]{1,0:T(8,128)(2,1)S(1)}, u32[]{:S(2)}, u32[]{:S(2)}) collective-permute-start(bf16[128,128]{1,0:T(8,128)(2,1)S(1)} %get-tuple-element.78.fm_ref), channel_id=1, source_target_pairs={{0,8},{1,9},{2,10},{3,11},{4,12},{5,13},{6,14},{7,15},{8,0},{9,1},... | collective-permute-start | bytes 98312 | tf_op jit(solution)/shard_map/ppermute | solution.py:541
  32.5 5.8 %collective-permute-start.14 = (bf16[128,128]{1,0:T(8,128)(2,1)S(1)}, bf16[128,128]{1,0:T(8,128)(2,1)S(1)}, u32[]{:S(2)}, u32[]{:S(2)}) collective-permute-start(bf16[128,128]{1,0:T(8,128)(2,1)S(1)} %get-tuple-element.78.fm_ref), channel_id=1, source_target_pairs={{0,12},{1,13},{2,14},{3,15},{4,8},{5,9},{6,10},{7,11},{8,4},{9,5},... | collective-permute-start | bytes 98312 | tf_op jit(solution)/shard_map/ppermute | solution.py:541
  35.1 4.7 %collective-permute-start.12 = (bf16[384,128]{1,0:T(8,128)(2,1)S(1)}, bf16[384,128]{1,0:T(8,128)(2,1)S(1)}, u32[]{:S(2)}, u32[]{:S(2)}) collective-permute-start(bf16[384,128]{1,0:T(8,128)(2,1)S(1)} %shard_map.136.refs_0_), channel_id=1, source_target_pairs={{0,4},{1,5},{2,6},{3,7},{4,0},{5,1},{6,2},{7,3},{8,12},{9,13},{10,... | collective-permute-start | bytes 294920 | tf_op jit(solution)/shard_map/ppermute | solution.py:541
  39.8 4.7 %collective-permute-start.19 = (bf16[384,128]{1,0:T(8,128)(2,1)S(1)}, bf16[384,128]{1,0:T(8,128)(2,1)S(1)}, u32[]{:S(2)}, u32[]{:S(2)}) collective-permute-start(bf16[384,128]{1,0:T(8,128)(2,1)S(1)} %shard_map.139.m0), channel_id=1, source_target_pairs={{0,2},{1,3},{2,0},{3,1},{4,6},{5,7},{6,4},{7,5},{8,10},{9,11},{10,... | collective-permute-start | bytes 294920 | tf_op jit(solution)/shard_map/ppermute | solution.py:538
  41.3 3.1 %collective-permute-start.18 = (bf16[384,128]{1,0:T(8,128)(2,1)S(1)}, bf16[384,128]{1,0:T(8,128)(2,1)S(1)}, u32[]{:S(2)}, u32[]{:S(2)}) collective-permute-start(bf16[384,128]{1,0:T(8,128)(2,1)S(1)} %shard_map.139.m0), channel_id=1, source_target_pairs={{0,1},{1,0},{2,3},{3,2},{4,5},{5,4},{6,7},{7,6},{8,9},{9,8},{10,11... | collective-permute-start | bytes 294920 | tf_op jit(solution)/shard_map/ppermute | solution.py:538
  44.5 1.3 %collective-permute-start.20 = (bf16[384,128]{1,0:T(8,128)(2,1)S(1)}, bf16[384,128]{1,0:T(8,128)(2,1)S(1)}, u32[]{:S(2)}, u32[]{:S(2)}) collective-permute-start(bf16[384,128]{1,0:T(8,128)(2,1)S(1)} %collective-permute-done.19.m2), channel_id=1, source_target_pairs={{0,1},{1,0},{2,3},{3,2},{4,5},{5,4},{6,7},{7,6},{8,9},{9,8},{10,11... | collective-permute-start | bytes 294920 | tf_op jit(solution)/shard_map/ppermute | solution.py:538
